TPU v7x, 32 devices: a whole 2x2x4 slice. The times are simulated.
32 devices in a mesh: exc: 8 (over z, y), space: 4 (over x, core).
Axes of the slice: x: 2, y: 2, z: 4, core: 2. Of those that a mesh axis runs over, the one named last changes fastest.
Arguments:
- adj_e: float32 [8, 192, 1024], P('exc', None, 'space'), may hold values from -6 to 6
- adj_h: float32 [8, 192, 1024], P('exc', None, 'space'), may hold values from -6 to 6
- adj_j: float32 [8, 192, 1024], P('exc', None, 'space'), may hold values from -6 to 6
- fwd_e: bfloat16 [8, 5, 192, 1024], P('exc', None, None, 'space'), may hold values from -6 to 6
- inv_eps: float32 [64, 1024], P(None, 'space'), may hold values from 0.08 to 1
- drude_weight: float32 [64, 1024], P(None, 'space'), may hold values from 0.5 to 20
- neighbor: int32 [6, 1024], P(None, 'space'), may hold values from -1 to 1023, as said below
- design_map: int32 [1024], P('space'), may hold values from 0 to 511, as said below
- port_elems: int32 [8, 512], P('exc', 'space'), may hold values from 0 to 1023, as said below
- port_profile: float32 [8, 192, 512], P('exc', None, 'space'), may hold values from -48 to 48
Outputs:
- adj_e_out: float32 [8, 192, 1024], P('exc', None, 'space')
- adj_h_out: float32 [8, 192, 1024], P('exc', None, 'space')
- grad_eps: float32 [64, 512], P(None, ('space', 'exc'))
- grad_drude: float32 [64, 512], P(None, ('space', 'exc'))
Inputs may be any that keep to these rules, and one draw needn't show every extreme that they name: neighbor[f, e] is the element across face f (x-, x+, y-, y+, z-, z+) of element e, which touches it with its opposite face; it is -1 across the x- face of the first and the x+ face of the last element layer. Elements are stored layer by layer in layers of 128 elements along x, so each block of 256 elements is 2 whole layers; a y or z neighbour lies in the same layer (periodic in y and z), an x neighbour in the adjacent layer. `design_map`: an element of the b-th block of 256 elements maps to a pixel of the b-th block of 128 pixels, and every pixel holds exactly two elements. `port_elems`: columns b * 128 to (b + 1) * 128 - 1 of each row hold 128 distinct elements of the b-th block of 256 elements.
All inputs are finite; a program needn't handle non-finite values.
Results may differ from a plain program's by a relative error of at most 0.00035.
Values sent between devices are 32-bit elements; how exact they have to be, the bound alone decides.
No kernel may reach another device: no remote copies, remote signals or barrier semaphores. Data moves between devices by JAX's collectives and lax.ppermute only.
A program may use at most 64 MiB of HBM per device.

v0:
```python
import functools

import jax
import jax.numpy as jnp
import ml_dtypes
import numpy as np
from jax import lax
from jax.experimental import pallas as pl
from jax.experimental.pallas import tpu as pltpu
from jax.sharding import PartitionSpec as P

NODES = 64
ROWS = 3 * NODES
LAYER = 128
PIX_DEV = 128

TIME_STEP = 0.025
DAMPING = 0.5
KEEP = 1.0 - TIME_STEP * DAMPING

TANGENT = 32
E_START = 0
H_FIRST = 32
E_FIRST = 64
H_SECOND = 96
SECOND = 128
V_NEAR = 128
N_NEAR = V_NEAR + NODES
FIRST = N_NEAR + 8

A1, L0, L1, B1 = range(4)

BF16 = jnp.bfloat16
F32 = jnp.float32


def tangential(face):
    return [c for c in range(3) if c != face // 2]


def node_tables():
    points = np.array([-1.0, -1.0 / np.sqrt(5.0), 1.0 / np.sqrt(5.0), 1.0])
    barycentric = np.array(
        [1.0 / np.prod([points[j] - points[k] for k in range(4) if k != j]) for j in range(4)]
    )
    deriv = np.zeros((4, 4))
    for row in range(4):
        for column in range(4):
            if row != column:
                deriv[row, column] = (
                    barycentric[column] / barycentric[row] / (points[row] - points[column])
                )
        deriv[row, row] = -np.sum(deriv[row])
    identity = np.eye(4)
    along_x = 2.0 * np.kron(np.kron(deriv, identity), identity)
    along_y = 2.0 * np.kron(np.kron(identity, deriv), identity)
    along_z = 2.0 * np.kron(np.kron(identity, identity), deriv)
    curl = np.zeros((192, 192))
    curl[0:64, 64:128] = -along_z
    curl[0:64, 128:192] = along_y
    curl[64:128, 0:64] = along_z
    curl[64:128, 128:192] = -along_x
    curl[128:192, 0:64] = -along_y
    curl[128:192, 64:128] = along_x
    numbers = np.arange(64).reshape(4, 4, 4)
    faces = np.stack(
        [
            numbers[0].ravel(),
            numbers[3].ravel(),
            numbers[:, 0].ravel(),
            numbers[:, 3].ravel(),
            numbers[:, :, 0].ravel(),
            numbers[:, :, 3].ravel(),
        ]
    )
    inner = np.zeros((192, 192))
    outer = np.zeros((192, 192))
    for face in range(6):
        direction = face // 2
        sign = 1.0 if face % 2 else -1.0
        for component in range(3):
            for place, other in enumerate(tangential(face)):
                parity = (component - direction) * (direction - other) * (other - component) / 2.0
                if parity != 0:
                    for node in range(16):
                        value = 6.0 * sign * parity
                        row = component * 64 + faces[face, node]
                        outer[row, face * 32 + place * 16 + node] += value
                        inner[row, other * 64 + faces[face, node]] += value
    return inner - curl, outer


def step_table():
    own, outer = node_tables()
    high = own.astype(ml_dtypes.bfloat16)
    low = (own - high.astype(np.float64)).astype(ml_dtypes.bfloat16)
    lift = (-outer).astype(ml_dtypes.bfloat16)
    return np.concatenate([high, high, low, lift, lift], axis=1)


def halves(x):
    high = x.astype(BF16)
    return high, (x - high.astype(F32)).astype(BF16)


def dot(a, b):
    return jnp.dot(a, b, preferred_element_type=F32)


def dot_t(a, b):
    return lax.dot_general(a, b, (((1,), (1,)), ((), ())), preferred_element_type=F32)


def thrice(x):
    return jnp.concatenate([x, x, x], axis=0)


def folded(x):
    return x[0:NODES] + x[NODES : 2 * NODES] + x[2 * NODES : ROWS]


def local_index(neighbor):
    return jnp.where(neighbor < 0, -1, jnp.bitwise_and(neighbor, LAYER - 1))


def hot_at(layer, face):
    if layer in (L0, L1):
        return 6 * (layer - L0) + face
    return 12 + (face - 1 if layer == A1 else 5 + (face - 1 if face else 0))


def one_hot(rows, targets):
    return (rows == targets).astype(F32).astype(BF16)


def layer_rows():
    return lax.broadcasted_iota(jnp.int32, (LAYER, LAYER), 0)


def face_rows(field, layer, face):
    offset = face % 2
    pieces = []
    for c in tangential(face):
        base = c * NODES
        if face < 2:
            pieces.append(field[layer, base + 48 * offset : base + 48 * offset + 16, :])
        elif face < 4:
            for i in range(4):
                at = base + 16 * i + 12 * offset
                pieces.append(field[layer, at : at + 4, :])
        else:
            pieces.append(field[layer, pl.ds(base + 3 * offset, 16, stride=4), :])
    return jnp.concatenate(pieces, axis=0)


def gathered(traces, hot):
    high, low = halves(traces)
    return dot(jnp.concatenate([high, low], axis=0), hot)


def rate(table, x, hots, field, layers, outer):
    first, last = layers[0], layers[-1]
    for layer in layers:
        here = slice(layer * LAYER, (layer + 1) * LAYER)
        high, low = halves(field[layer])
        x[0:ROWS, here] = high
        x[ROWS : 2 * ROWS, here] = low
        x[2 * ROWS : 3 * ROWS, here] = high
        for face in range(6):
            at = 3 * ROWS + TANGENT * face
            traces = outer(layer, face)
            if traces is None:
                nothing = jnp.zeros((TANGENT, LAYER), BF16)
                x[at : at + TANGENT, here] = nothing
                x[at + ROWS : at + ROWS + TANGENT, here] = nothing
            else:
                got = gathered(traces, hots(layer, face)).astype(BF16)
                x[at : at + TANGENT, here] = got[0:TANGENT]
                x[at + ROWS : at + ROWS + TANGENT, here] = got[TANGENT : 2 * TANGENT]
    found = dot(table[...], x[:, first * LAYER : (last + 1) * LAYER])
    return [found[:, i * LAYER : (i + 1) * LAYER] for i in range(len(layers))]


def neighbour(layer, face):
    return layer + (-1, 1, 0, 0, 0, 0)[face]


def lonely(table, x, hots, fe, fh, drive, v):
    own = (L0, L1)

    def outer_of(field):
        def outer(layer, face):
            there = neighbour(layer, face)
            return face_rows(field, there, face ^ 1) if there in own else None

        return outer

    def ends(field):
        return face_rows(field, L1, 1), face_rows(field, L0, 0)

    found = [ends(fe)]
    for i, change in enumerate(rate(table, x, hots, fe, own, outer_of(fe))):
        fh[L0 + i] += TIME_STEP * change
    found.append(ends(fh))
    for i, change in enumerate(rate(table, x, hots, fh, own, outer_of(fh))):
        fe[L0 + i] -= TIME_STEP * thrice(v[i]) * (change + drive[i])
    found.append(ends(fe))
    for i, change in enumerate(rate(table, x, hots, fe, own, outer_of(fe))):
        fh[L0 + i] += TIME_STEP * change
    found.append(ends(fh))
    return [jnp.concatenate(traces, axis=0) for traces in zip(*found)]


def response(traces, hot, face):
    parts = gathered(traces, hot)
    both = (6.0 * TIME_STEP) * (parts[0:TANGENT] + parts[TANGENT : 2 * TANGENT])
    sign = 1.0 if face else -1.0
    return sign * both[16:32], -sign * both[0:16]


def two_steps(table, x, hots, fe, fh, e, h, j, source, v, w, v_near, sent_a, sent_b):
    own, wide = (L0, L1), (A1, L0, L1, B1)
    for i in range(2):
        fe[L0 + i] = e[i]
        fh[L0 + i] = h[i]
    blank = jnp.zeros((ROWS, LAYER), F32)
    fh[A1] = blank
    fh[B1] = blank

    def outer_of(field, start, answered=True):
        def outer(layer, face):
            if (layer, face) in ((A1, 0), (B1, 1)):
                return None
            there = neighbour(layer, face)
            if layer in own and there not in own:
                sent = sent_a if there == A1 else sent_b
                traces = sent[start : start + TANGENT, :]
                return traces + face_rows(field, there, face ^ 1) if answered else traces
            return face_rows(field, there, face ^ 1)

        return outer

    weight = [TIME_STEP * thrice(w[i]) for i in range(2)]
    changes = rate(table, x, hots, fe, own, outer_of(fe, E_START, False))
    for i in range(2):
        fh[L0 + i] += TIME_STEP * changes[i]
    at_y, at_z = response(face_rows(fe, L0, 0), hots(A1, 1), 1)
    fh[A1, 112:128, :] = at_y
    fh[A1, 176:192, :] = at_z
    at_y, at_z = response(face_rows(fe, L1, 1), hots(B1, 0), 0)
    fh[B1, 64:80, :] = at_y
    fh[B1, 128:144, :] = at_z

    first_j = [KEEP * j[i] + weight[i] * e[i] for i in range(2)]
    changes = rate(table, x, hots, fh, wide, outer_of(fh, H_FIRST))
    for i in range(2):
        fe[L0 + i] -= TIME_STEP * thrice(v[i]) * (changes[1 + i] + first_j[i] + source[i])
    fe[A1] = -TIME_STEP * thrice(v_near[0]) * changes[0]
    fe[B1] = -TIME_STEP * thrice(v_near[1]) * changes[3]
    first_e = [fe[L0], fe[L1]]

    for layer, change in zip(wide, rate(table, x, hots, fe, wide, outer_of(fe, E_FIRST))):
        fh[layer] += TIME_STEP * change
    second_j = [KEEP * first_j[i] + weight[i] * first_e[i] for i in range(2)]
    changes = rate(table, x, hots, fh, own, outer_of(fh, H_SECOND))
    for i in range(2):
        fe[L0 + i] -= TIME_STEP * thrice(v[i]) * (changes[i] + second_j[i] + source[i])
    return first_e, first_j, [fe[L0], fe[L1]], second_j, [fh[L0], fh[L1]]


def odd_rank():
    return lax.rem(lax.axis_index("space"), 2) == 1


def send(across, inside, at, up, down):
    odd = odd_rank()
    rows = slice(at, at + up.shape[0])
    across[rows, :] = jnp.where(odd, up, down)
    inside[rows, :] = jnp.where(odd, down, up)


def sides(across, inside, a, b, rows):
    odd = odd_rank()
    from_across, from_inside = across[0:rows, :], inside[0:rows, :]
    a[...] = jnp.where(odd, from_inside, from_across)
    b[...] = jnp.where(odd, from_across, from_inside)


def first_kernel(
    table_in, e_in, h_in, j_in, v_in, w_in, near_in, ports_in, profile_in, *rest
):
    table, e, h, j, v, w, near, source, hot, across, inside = rest[:11]
    fe, fh, x, ports, profile, sems = rest[11:]
    copies = []

    def fetch(origin, target):
        copies.append(pltpu.make_async_copy(origin, target, sems.at[len(copies)]))
        copies[-1].start()
        return copies[-1]

    early = [fetch(near_in, near), fetch(ports_in, ports), fetch(profile_in, profile)]
    fields = []
    for origin, target in ((e_in, e), (h_in, h), (j_in, j), (w_in, w), (v_in, v)):
        for i in range(2):
            fields.append(fetch(origin.at[:, pl.ds(i * LAYER, LAYER)], target.at[i]))
    last = fetch(table_in, table)

    for copy in early:
        copy.wait()
    rows = layer_rows()
    index = local_index(near[...])
    for i in range(2):
        for face in range(6):
            hot[6 * i + face] = one_hot(rows, index[face : face + 1, i * LAYER : (i + 1) * LAYER])
    count = 2 * LAYER
    place = jnp.bitwise_and(ports[...], count - 1)
    targets = lax.broadcasted_iota(jnp.int32, (count, place.shape[1]), 0)
    spread_hot = one_hot(targets, place)
    high, low = halves(profile[...])
    spread = dot_t(high, spread_hot) + dot_t(low, spread_hot)
    for i in range(2):
        source[i] = spread[:, i * LAYER : (i + 1) * LAYER]
    for copy in fields:
        copy.wait()
    drive = []
    for i in range(2):
        fe[L0 + i] = e[i]
        fh[L0 + i] = h[i]
        drive.append(KEEP * j[i] + TIME_STEP * thrice(w[i]) * e[i] + source[i])
    last.wait()
    up, down = lonely(table, x, lambda l, f: hot[hot_at(l, f)], fe, fh, drive, v)
    send(across, inside, 0, up, down)
    send(across, inside, V_NEAR, v[1], v[0])
    blank = jnp.zeros((2, LAYER), F32)
    index = index.astype(F32)
    send(
        across,
        inside,
        N_NEAR,
        jnp.concatenate([index[:, LAYER : 2 * LAYER], blank], axis=0),
        jnp.concatenate([index[:, 0:LAYER], blank], axis=0),
    )


def middle_kernel(table, e, h, j, v, w, source, hot, across_in, inside_in, *rest):
    out_e, out_h, out_j, mid_e, mid_j, v_near, hot_near, across, inside = rest[:9]
    fe, fh, x, sent_a, sent_b = rest[9:]
    sides(across_in, inside_in, sent_a, sent_b, FIRST)
    v_near[0] = sent_a[V_NEAR : V_NEAR + NODES, :]
    v_near[1] = sent_b[V_NEAR : V_NEAR + NODES, :]
    rows = layer_rows()
    for layer, sent in ((A1, sent_a), (B1, sent_b)):
        index = sent[N_NEAR : N_NEAR + 8, :].astype(jnp.int32)
        for face in range(6):
            if (layer, face) not in ((A1, 0), (B1, 1)):
                hot_near[hot_at(layer, face) - 12] = one_hot(rows, index[face : face + 1, :])

    def hots(layer, face):
        at = hot_at(layer, face)
        return hot[at] if at < 12 else hot_near[at - 12]

    first_e, first_j, second_e, second_j, magnetic = two_steps(
        table, x, hots, fe, fh, e, h, j, source, v, w, v_near, sent_a, sent_b
    )
    drive = []
    for i in range(2):
        mid_e[i] = first_e[i]
        mid_j[i] = first_j[i]
        out_e[i] = second_e[i]
        out_j[i] = second_j[i]
        out_h[i] = magnetic[i]
        drive.append(
            KEEP * second_j[i] + TIME_STEP * thrice(w[i]) * second_e[i] + source[i]
        )
    up, down = lonely(table, x, hots, fe, fh, drive, v)
    send(across, inside, 0, up, down)


def early_kernel(mid_e, mid_j, end_e, end_j, levels, out):
    for i in range(2):
        columns = slice(i * LAYER, (i + 1) * LAYER)
        start, middle, end = (levels[k, :, columns].astype(F32) for k in range(3))
        out[0:NODES, columns] = folded(
            mid_e[i] * (middle - start) + end_e[i] * (end - middle)
        )
        out[NODES : 2 * NODES, columns] = folded(mid_j[i] * start + end_j[i] * middle)


def split(total, keep, give, bit):
    half = total.shape[0] // 2
    side = lax.rem(lax.axis_index("exc") // bit, 2)
    keep[...] = total[pl.ds(pl.multiple_of(side * half, half), half), :]
    give[...] = total[pl.ds(pl.multiple_of((1 - side) * half, half), half), :]


def last_kernel(
    bit, table, e, h, j, v, w, source, hot, v_near, hot_near, across_in, inside_in, *rest
):
    levels, early, design, out_e, out_h, keep, give = rest[:7]
    fe, fh, x, sent_a, sent_b, sums = rest[7:]
    sides(across_in, inside_in, sent_a, sent_b, SECOND)

    def hots(layer, face):
        at = hot_at(layer, face)
        return hot[at] if at < 12 else hot_near[at - 12]

    first_e, first_j, second_e, second_j, magnetic = two_steps(
        table, x, hots, fe, fh, e, h, j, source, v, w, v_near, sent_a, sent_b
    )
    parts = []
    for i in range(2):
        out_e[i] = second_e[i]
        out_h[i] = magnetic[i]
        columns = slice(i * LAYER, (i + 1) * LAYER)
        start, middle, end = (levels[k, :, columns].astype(F32) for k in range(2, 5))
        eps = folded(first_e[i] * (middle - start) + second_e[i] * (end - middle))
        drude = folded(first_j[i] * start + second_j[i] * middle)
        parts.append(jnp.concatenate([eps, drude], axis=0) + early[:, columns])
    both = jnp.concatenate(parts, axis=1)
    pixel = jnp.bitwise_and(design[...], PIX_DEV - 1)
    pixels = one_hot(lax.broadcasted_iota(jnp.int32, (PIX_DEV, both.shape[1]), 0), pixel)
    high, low = halves(both)
    sums[...] = dot_t(pixels, high) + dot_t(pixels, low)
    split(sums, keep, give, bit)


def write_kernel(e, h, out_e, out_h):
    for i in range(2):
        columns = slice(i * LAYER, (i + 1) * LAYER)
        out_e[:, columns] = e[i]
        out_h[:, columns] = h[i]


def halve_kernel(bit, kept, came, keep, give, sums):
    sums[...] = kept[...] + came[...]
    split(sums, keep, give, bit)


def total_kernel(owners, kept, came, eps, drude):
    total = (kept[...] + came[...]) * (1.0 / owners)
    eps[...] = total[:, 0:NODES]
    drude[...] = total[:, NODES : 2 * NODES]


def call(kernel, outs, args, scratch=(), flops=0, space=pltpu.VMEM):
    moved = sum(4 * int(np.prod(o.shape)) for o in outs) + sum(
        a.dtype.itemsize * int(np.prod(a.shape)) for a in args
    )
    return pl.pallas_call(
        kernel,
        out_shape=outs,
        in_specs=[pl.BlockSpec(memory_space=space)] * len(args),
        out_specs=[pl.BlockSpec(memory_space=pltpu.VMEM)] * len(outs),
        scratch_shapes=list(scratch),
        compiler_params=pltpu.CompilerParams(vmem_limit_bytes=24 * 1024 * 1024),
        cost_estimate=pl.CostEstimate(flops=flops, bytes_accessed=moved, transcendentals=0),
    )(*args)


def f32(*shape):
    return jax.ShapeDtypeStruct(shape, F32)


def bf16(*shape):
    return jax.ShapeDtypeStruct(shape, BF16)


def exchange(across, inside):
    size = lax.axis_size("space")

    def pairs(start):
        found = [(i, i + 1) for i in range(start, size - 1, 2)]
        return found + [(j, i) for i, j in found]

    return lax.ppermute(across, "space", pairs(1)), lax.ppermute(inside, "space", pairs(0))


def local(
    adj_e,
    adj_h,
    adj_j,
    fwd_e,
    inv_eps,
    drude_weight,
    neighbor,
    design_map,
    port_elems,
    port_profile,
):
    count = adj_e.shape[2]
    owners = lax.axis_size("exc")
    table = jnp.asarray(step_table())
    levels = fwd_e[0]
    field, nodal = f32(2, ROWS, LAYER), f32(2, NODES, LAYER)
    work = [
        pltpu.VMEM((4, ROWS, LAYER), F32),
        pltpu.VMEM((4, ROWS, LAYER), F32),
        pltpu.VMEM((5 * ROWS, 4 * LAYER), BF16),
    ]
    once = 2 * ROWS * 5 * ROWS * LAYER

    table, e, h, j, v, w, _, source, hot, across, inside = call(
        first_kernel,
        [bf16(*table.shape), field, field, field, nodal, nodal]
        + [jax.ShapeDtypeStruct(neighbor.shape, jnp.int32), field, bf16(12, LAYER, LAYER)]
        + [f32(FIRST, LAYER)] * 2,
        [table, adj_e[0], adj_h[0], adj_j[0], inv_eps, drude_weight]
        + [neighbor, port_elems, port_profile[0]],
        work
        + [
            pltpu.VMEM(port_elems.shape, jnp.int32),
            pltpu.VMEM(port_profile.shape[1:], F32),
            pltpu.SemaphoreType.DMA((14,)),
        ],
        6 * once,
        pltpu.HBM,
    )
    across, inside = exchange(across, inside)
    e2, h2, j2, e1, j1, v_near, hot_near, across, inside = call(
        middle_kernel,
        [field] * 5 + [nodal, bf16(10, LAYER, LAYER)] + [f32(SECOND, LAYER)] * 2,
        [table, e, h, j, v, w, source, hot, across, inside],
        work + [pltpu.VMEM((FIRST, LAYER), F32)] * 2,
        18 * once,
    )
    across, inside = exchange(across, inside)
    (early,) = call(early_kernel, [f32(2 * NODES, count)], [e1, j1, e2, j2, levels])
    bit = owners // 2
    size = PIX_DEV // 2
    e4, h4, keep, give = call(
        functools.partial(last_kernel, bit),
        [field, field] + [f32(size, 2 * NODES)] * 2,
        [table, e2, h2, j2, v, w, source, hot, v_near, hot_near, across, inside]
        + [levels, early, design_map.reshape(1, count)],
        work
        + [pltpu.VMEM((SECOND, LAYER), F32)] * 2
        + [pltpu.VMEM((PIX_DEV, 2 * NODES), F32)],
        12 * once,
    )

    def swap(give, bit):
        return lax.ppermute(give, "exc", [(i, i ^ bit) for i in range(owners)])

    came = swap(give, bit)
    out_e, out_h = call(write_kernel, [f32(ROWS, count)] * 2, [e4, h4])
    while bit > 1:
        bit, size = bit // 2, size // 2
        keep, give = call(
            functools.partial(halve_kernel, bit),
            [f32(size, 2 * NODES)] * 2,
            [keep, came],
            [pltpu.VMEM((2 * size, 2 * NODES), F32)],
        )
        came = swap(give, bit)
    eps, drude = call(
        functools.partial(total_kernel, owners),
        [f32(size, NODES)] * 2,
        [keep, came],
    )
    return out_e[None], out_h[None], eps.T, drude.T


def solution(mesh):
    return jax.shard_map(
        local,
        mesh=mesh,
        in_specs=(
            P("exc", None, "space"),
            P("exc", None, "space"),
            P("exc", None, "space"),
            P("exc", None, None, "space"),
            P(None, "space"),
            P(None, "space"),
            P(None, "space"),
            P("space"),
            P("exc", "space"),
            P("exc", None, "space"),
        ),
        out_specs=(
            P("exc", None, "space"),
            P("exc", None, "space"),
            P(None, ("space", "exc")),
            P(None, ("space", "exc")),
        ),
        check_vma=False,
    )
```

profile of v0, /device:TPU:0, one launch (start us, length us, event | category | flops | bytes accessed | tf_op | source)
XLA Modules:
  0.0 43.0 jit_solution(6477854636980426883)
XLA Ops:
  0.6 0.0 copy-start.10
  0.6 0.6 %copy-done.10 = s32[1,128]{1,0:T(1,128)S(1)} copy-done((s32[1,128]{1,0:T(1,128)S(1)}, s32[1,128]{1,0:T(1,128)}, u32[]{:S(2)}) %copy-start.10) | copy-done | bytes 536
  1.3 1.0 %copy-done.1 = bf16[192,960]{1,0:T(8,128)(2,1)S(1)} copy-done((bf16[192,960]{1,0:T(8,128)(2,1)S(1)}, bf16[192,960]{1,0:T(8,128)(2,1)}, u32[]{:S(2)}) %copy-start.1) | copy-done | bytes 368664
  2.3 0.9 %copy-done.2 = f32[1,192,256]{2,1,0:T(8,128)S(1)} copy-done((f32[1,192,256]{2,1,0:T(8,128)S(1)}, f32[1,192,256]{2,1,0:T(8,128)}, u32[]{:S(2)}) %copy-start.2) | copy-done | bytes 196632
  3.2 0.9 %copy-done.3 = f32[1,192,256]{2,1,0:T(8,128)S(1)} copy-done((f32[1,192,256]{2,1,0:T(8,128)S(1)}, f32[1,192,256]{2,1,0:T(8,128)}, u32[]{:S(2)}) %copy-start.3) | copy-done | bytes 196632
  4.1 0.9 %copy-done.4 = f32[1,192,256]{2,1,0:T(8,128)S(1)} copy-done((f32[1,192,256]{2,1,0:T(8,128)S(1)}, f32[1,192,256]{2,1,0:T(8,128)}, u32[]{:S(2)}) %copy-start.4) | copy-done | bytes 196632
  5.1 0.9 %copy-done.5 = f32[1,192,128]{2,1,0:T(8,128)S(1)} copy-done((f32[1,192,128]{2,1,0:T(8,128)S(1)}, f32[1,192,128]{2,1,0:T(8,128)}, u32[]{:S(2)}) %copy-start.5) | copy-done | bytes 98328
  6.0 0.8 %copy-done.6 = f32[64,256]{1,0:T(8,128)S(1)} copy-done((f32[64,256]{1,0:T(8,128)S(1)}, f32[64,256]{1,0:T(8,128)}, u32[]{:S(2)}) %copy-start.6) | copy-done | bytes 65560
  6.8 0.8 %copy-done.7 = f32[64,256]{1,0:T(8,128)S(1)} copy-done((f32[64,256]{1,0:T(8,128)S(1)}, f32[64,256]{1,0:T(8,128)}, u32[]{:S(2)}) %copy-start.7) | copy-done | bytes 65560
  7.6 0.7 %copy-done.8 = s32[6,256]{1,0:T(8,128)S(1)} copy-done((s32[6,256]{1,0:T(8,128)S(1)}, s32[6,256]{1,0:T(8,128)}, u32[]{:S(2)}) %copy-start.8) | copy-done | bytes 6168
  8.3 2.5 %shard_map.138 = (bf16[192,960]{1,0:T(8,128)(2,1)S(1)}, f32[2,192,128]{2,1,0:T(8,128)S(1)}, f32[2,192,128]{2,1,0:T(8,128)S(1)}, f32[2,192,128]{2,1,0:T(8,128)S(1...) custom-call(bf16[192,960]{1,0:T(8,128)(2,1)S(1)} %copy-done.1, ...), custom_call_target="tpu_custom_call" | custom-call | flops 283115520 | bytes 3846656 | tf_op jit(solution)/shard_map/pallas_call | solution.py:449
  10.8 0.7 %collective-permute-start = (f32[200,128]{1,0:T(8,128)S(1)}, f32[200,128]{1,0:T(8,128)S(1)}, u32[]{:S(2)}, u32[]{:S(2)}) collective-permute-start(f32[200,128]{1,0:T(8,128)S(1)} %get-tuple-element.43), channel_id=1, source_target_pairs={{1,2},{2,1},{5,6},{6,5},{9,10},{10,9},{13,14},{14,13},{17,18},{18,... | collective-permute-start | bytes 307208 | tf_op jit(solution)/shard_map/ppermute | solution.py:475
  11.5 4.4 %collective-permute-start.1 = (f32[200,128]{1,0:T(8,128)S(1)}, f32[200,128]{1,0:T(8,128)S(1)}, u32[]{:S(2)}, u32[]{:S(2)}) collective-permute-start(f32[200,128]{1,0:T(8,128)S(1)} %get-tuple-element.44), channel_id=1, source_target_pairs={{0,1},{2,3},{1,0},{3,2},{4,5},{6,7},{5,4},{7,6},{8,9},{10,11},{9,8... | collective-permute-start | bytes 307208 | tf_op jit(solution)/shard_map/ppermute | solution.py:475
  15.8 0.0 collective-permute-done.across_in
  15.8 0.9 %collective-permute-done.1.inside_in = f32[200,128]{1,0:T(8,128)S(1)} collective-permute-done((f32[200,128]{1,0:T(8,128)S(1)}, f32[200,128]{1,0:T(8,128)S(1)}, u32[]{:S(2)}, u32[]{:S(2)}) %collective-permute-start.1) | collective-permute-done | bytes 102432 | tf_op jit(solution)/shard_map/ppermute | solution.py:475
  16.8 3.8 %shard_map.139 = (f32[2,192,128]{2,1,0:T(8,128)S(1)}, f32[2,192,128]{2,1,0:T(8,128)S(1)}, f32[2,192,128]{2,1,0:T(8,128)S(1)}, f32[2,192,128]{2,1,0:T(8,128)S(1)}...) custom-call(bf16[192,960]{1,0:T(8,128)(2,1)S(1)} %get-tuple-element., ...), custom_call_target="tpu_custom_call" | custom-call | flops 849346560 | bytes 3719168 | tf_op jit(solution)/shard_map/pallas_call | solution.py:449
  20.6 0.7 %collective-permute-start.2 = (f32[128,128]{1,0:T(8,128)S(1)}, f32[128,128]{1,0:T(8,128)S(1)}, u32[]{:S(2)}, u32[]{:S(2)}) collective-permute-start(f32[128,128]{1,0:T(8,128)S(1)} %get-tuple-element.50), channel_id=1, source_target_pairs={{1,2},{2,1},{5,6},{6,5},{9,10},{10,9},{13,14},{14,13},{17,18},{18,... | collective-permute-start | bytes 196616 | tf_op jit(solution)/shard_map/ppermute | solution.py:475
  21.2 4.4 %collective-permute-start.3 = (f32[128,128]{1,0:T(8,128)S(1)}, f32[128,128]{1,0:T(8,128)S(1)}, u32[]{:S(2)}, u32[]{:S(2)}) collective-permute-start(f32[128,128]{1,0:T(8,128)S(1)} %get-tuple-element.51), channel_id=1, source_target_pairs={{0,1},{2,3},{1,0},{3,2},{4,5},{6,7},{5,4},{7,6},{8,9},{10,11},{9,8... | collective-permute-start | bytes 196616 | tf_op jit(solution)/shard_map/ppermute | solution.py:475
  25.6 0.0 copy-done
  25.6 0.1 shard_map.140.rest_1_
  25.7 0.0 collective-permute-done.2.across_in
  25.7 0.8 %collective-permute-done.3.inside_in = f32[128,128]{1,0:T(8,128)S(1)} collective-permute-done((f32[128,128]{1,0:T(8,128)S(1)}, f32[128,128]{1,0:T(8,128)S(1)}, u32[]{:S(2)}, u32[]{:S(2)}) %collective-permute-start.3) | collective-permute-done | bytes 65568 | tf_op jit(solution)/shard_map/ppermute | solution.py:475
  26.5 0.7 %copy-done.9 = s32[256]{0:T(256)S(1)} copy-done((s32[256]{0:T(256)S(1)}, s32[256]{0:T(256)}, u32[]{:S(2)}) %copy-start.9) | copy-done | bytes 1048
  27.2 2.4 %shard_map.141 = (f32[2,192,128]{2,1,0:T(8,128)S(1)}, f32[2,192,128]{2,1,0:T(8,128)S(1)}, f32[64,128]{1,0:T(8,128)S(1)}, f32[64,128]{1,0:T(8,128)S(1)}) custom-call(bf16[192,960]{1,0:T(8,128)(2,1)S(1)} %get-tuple-element.35.table, f32[2,192,128]{2,1,0:T(8,128)S(1)} %get-tuple-element.45.end_e.e, f32[2,192,128]{2,1,0:T(8,128)S(1)} %get-tuple-element.46.h, ...), custom_call_target="tpu_custom_call" | custom-call | flops 566231040 | bytes 3286016 | tf_op jit(solution)/shard_map/pallas_call | solution.py:449
  29.6 2.7 %collective-permute-start.4 = (f32[64,128]{1,0:T(8,128)S(1)}, f32[64,128]{1,0:T(8,128)S(1)}, u32[]{:S(2)}, u32[]{:S(2)}) collective-permute-start(f32[64,128]{1,0:T(8,128)S(1)} %get-tuple-element.59), channel_id=1, source_target_pairs={{0,16},{4,20},{8,24},{12,28},{16,0},{20,4},{24,8},{28,12},{1,17},{... | collective-permute-start | bytes 98312 | tf_op jit(solution)/shard_map/ppermute | solution.py:542
  32.2 2.6 %collective-permute-done.4.came = f32[64,128]{1,0:T(8,128)S(1)} collective-permute-done((f32[64,128]{1,0:T(8,128)S(1)}, f32[64,128]{1,0:T(8,128)S(1)}, u32[]{:S(2)}, u32[]{:S(2)}) %collective-permute-start.4) | collective-permute-done | bytes 32800 | tf_op jit(solution)/shard_map/ppermute | solution.py:542
  34.8 1.6 %collective-permute-start.5 = (f32[32,128]{1,0:T(8,128)S(1)}, f32[32,128]{1,0:T(8,128)S(1)}, u32[]{:S(2)}, u32[]{:S(2)}) collective-permute-start(f32[32,128]{1,0:T(8,128)S(1)} %get-tuple-element.61), channel_id=1, source_target_pairs={{0,8},{4,12},{8,0},{12,4},{16,24},{20,28},{24,16},{28,20},{1,9},{5... | collective-permute-start | bytes 49160 | tf_op jit(solution)/shard_map/ppermute | solution.py:542
  36.5 2.2 %collective-permute-done.5.came = f32[32,128]{1,0:T(8,128)S(1)} collective-permute-done((f32[32,128]{1,0:T(8,128)S(1)}, f32[32,128]{1,0:T(8,128)S(1)}, u32[]{:S(2)}, u32[]{:S(2)}) %collective-permute-start.5) | collective-permute-done | bytes 16416 | tf_op jit(solution)/shard_map/ppermute | solution.py:542
  38.6 1.5 %collective-permute-start.6 = (f32[16,128]{1,0:T(8,128)S(1)}, f32[16,128]{1,0:T(8,128)S(1)}, u32[]{:S(2)}, u32[]{:S(2)}) collective-permute-start(f32[16,128]{1,0:T(8,128)S(1)} %get-tuple-element.63), channel_id=1, source_target_pairs={{0,4},{4,0},{8,12},{12,8},{16,20},{20,16},{24,28},{28,24},{1,5},{5... | collective-permute-start | bytes 24584 | tf_op jit(solution)/shard_map/ppermute | solution.py:542
  40.1 0.8 %shard_map.142 = (f32[192,256]{1,0:T(8,128)}, f32[192,256]{1,0:T(8,128)}) custom-call(f32[2,192,128]{2,1,0:T(8,128)S(1)} %get-tuple-element.54.e, f32[2,192,128]{2,1,0:T(8,128)S(1)} %get-tuple-element.55.h), custom_call_target="tpu_custom_call" | custom-call | bytes 786432 | tf_op jit(solution)/shard_map/pallas_call | solution.py:449
  40.9 1.4 %collective-permute-done.6.came = f32[16,128]{1,0:T(8,128)S(1)} collective-permute-done((f32[16,128]{1,0:T(8,128)S(1)}, f32[16,128]{1,0:T(8,128)S(1)}, u32[]{:S(2)}, u32[]{:S(2)}) %collective-permute-start.6) | collective-permute-done | bytes 8224 | tf_op jit(solution)/shard_map/ppermute | solution.py:542
  42.3 0.7 %shard_map.145 = (f32[16,64]{1,0:T(8,128)}, f32[16,64]{1,0:T(8,128)}) custom-call(f32[16,128]{1,0:T(8,128)S(1)} %get-tuple-element.62.kept, f32[16,128]{1,0:T(8,128)S(1)} %collective-permute-done.6.came), custom_call_target="tpu_custom_call" | custom-call | bytes 24576 | tf_op jit(solution)/shard_map/pallas_call | solution.py:449
  (12 shorter events, 0.0 us)
Async XLA Ops:
  0.6 0.7 %copy-start.10 = (s32[1,128]{1,0:T(1,128)S(1)}, s32[1,128]{1,0:T(1,128)}, u32[]{:S(2)}) copy-start(s32[1,128]{1,0:T(1,128)} %ports_in.1) | copy-start | bytes 1540
  1.3 1.0 %copy-start.1 = (bf16[192,960]{1,0:T(8,128)(2,1)S(1)}, bf16[192,960]{1,0:T(8,128)(2,1)}, u32[]{:S(2)}) copy-start(bf16[192,960]{1,0:T(8,128)(2,1)} %constant.2.clone.table_in) | copy-start | bytes 1105924
  2.3 0.9 %copy-start.2 = (f32[1,192,256]{2,1,0:T(8,128)S(1)}, f32[1,192,256]{2,1,0:T(8,128)}, u32[]{:S(2)}) copy-start(f32[1,192,256]{2,1,0:T(8,128)} %param.11) | copy-start | bytes 589828
  3.2 0.9 %copy-start.3 = (f32[1,192,256]{2,1,0:T(8,128)S(1)}, f32[1,192,256]{2,1,0:T(8,128)}, u32[]{:S(2)}) copy-start(f32[1,192,256]{2,1,0:T(8,128)} %param.12) | copy-start | bytes 589828
  4.1 0.9 %copy-start.4 = (f32[1,192,256]{2,1,0:T(8,128)S(1)}, f32[1,192,256]{2,1,0:T(8,128)}, u32[]{:S(2)}) copy-start(f32[1,192,256]{2,1,0:T(8,128)} %param.13) | copy-start | bytes 589828
  5.1 0.9 %copy-start.5 = (f32[1,192,128]{2,1,0:T(8,128)S(1)}, f32[1,192,128]{2,1,0:T(8,128)}, u32[]{:S(2)}) copy-start(f32[1,192,128]{2,1,0:T(8,128)} %param.20) | copy-start | bytes 294916
  6.0 0.8 %copy-start.6 = (f32[64,256]{1,0:T(8,128)S(1)}, f32[64,256]{1,0:T(8,128)}, u32[]{:S(2)}) copy-start(f32[64,256]{1,0:T(8,128)} %v_in.1) | copy-start | bytes 196612
  6.8 0.8 %copy-start.7 = (f32[64,256]{1,0:T(8,128)S(1)}, f32[64,256]{1,0:T(8,128)}, u32[]{:S(2)}) copy-start(f32[64,256]{1,0:T(8,128)} %w_in.1) | copy-start | bytes 196612
  7.6 0.7 %copy-start.8 = (s32[6,256]{1,0:T(8,128)S(1)}, s32[6,256]{1,0:T(8,128)}, u32[]{:S(2)}) copy-start(s32[6,256]{1,0:T(8,128)} %near_in.1) | copy-start | bytes 18436
  10.8 5.0 %collective-permute-start = (f32[200,128]{1,0:T(8,128)S(1)}, f32[200,128]{1,0:T(8,128)S(1)}, u32[]{:S(2)}, u32[]{:S(2)}) collective-permute-start(f32[200,128]{1,0:T(8,128)S(1)} %get-tuple-element.43), channel_id=1, source_target_pairs={{1,2},{2,1},{5,6},{6,5},{9,10},{10,9},{13,14},{14,13},{17,18},{18,... | collective-permute-start | bytes 307208 | tf_op jit(solution)/shard_map/ppermute | solution.py:475
  11.5 5.3 %collective-permute-start.1 = (f32[200,128]{1,0:T(8,128)S(1)}, f32[200,128]{1,0:T(8,128)S(1)}, u32[]{:S(2)}, u32[]{:S(2)}) collective-permute-start(f32[200,128]{1,0:T(8,128)S(1)} %get-tuple-element.44), channel_id=1, source_target_pairs={{0,1},{2,3},{1,0},{3,2},{4,5},{6,7},{5,4},{7,6},{8,9},{10,11},{9,8... | collective-permute-start | bytes 307208 | tf_op jit(solution)/shard_map/ppermute | solution.py:475
  16.8 8.8 %copy-start = (bf16[1,5,192,256]{3,2,1,0:T(8,128)(2,1)S(1)}, bf16[1,5,192,256]{3,2,1,0:T(8,128)(2,1)}, u32[]{:S(2)}) copy-start(bf16[1,5,192,256]{3,2,1,0:T(8,128)(2,1)} %param.14) | copy-start | bytes 1474564
  20.6 5.1 %collective-permute-start.2 = (f32[128,128]{1,0:T(8,128)S(1)}, f32[128,128]{1,0:T(8,128)S(1)}, u32[]{:S(2)}, u32[]{:S(2)}) collective-permute-start(f32[128,128]{1,0:T(8,128)S(1)} %get-tuple-element.50), channel_id=1, source_target_pairs={{1,2},{2,1},{5,6},{6,5},{9,10},{10,9},{13,14},{14,13},{17,18},{18,... | collective-permute-start | bytes 196616 | tf_op jit(solution)/shard_map/ppermute | solution.py:475
  21.2 5.3 %collective-permute-start.3 = (f32[128,128]{1,0:T(8,128)S(1)}, f32[128,128]{1,0:T(8,128)S(1)}, u32[]{:S(2)}, u32[]{:S(2)}) collective-permute-start(f32[128,128]{1,0:T(8,128)S(1)} %get-tuple-element.51), channel_id=1, source_target_pairs={{0,1},{2,3},{1,0},{3,2},{4,5},{6,7},{5,4},{7,6},{8,9},{10,11},{9,8... | collective-permute-start | bytes 196616 | tf_op jit(solution)/shard_map/ppermute | solution.py:475
  26.5 0.7 %copy-start.9 = (s32[256]{0:T(256)S(1)}, s32[256]{0:T(256)}, u32[]{:S(2)}) copy-start(s32[256]{0:T(256)} %param.18) | copy-start | bytes 3076
  29.6 5.2 %collective-permute-start.4 = (f32[64,128]{1,0:T(8,128)S(1)}, f32[64,128]{1,0:T(8,128)S(1)}, u32[]{:S(2)}, u32[]{:S(2)}) collective-permute-start(f32[64,128]{1,0:T(8,128)S(1)} %get-tuple-element.59), channel_id=1, source_target_pairs={{0,16},{4,20},{8,24},{12,28},{16,0},{20,4},{24,8},{28,12},{1,17},{... | collective-permute-start | bytes 98312 | tf_op jit(solution)/shard_map/ppermute | solution.py:542
  34.8 3.8 %collective-permute-start.5 = (f32[32,128]{1,0:T(8,128)S(1)}, f32[32,128]{1,0:T(8,128)S(1)}, u32[]{:S(2)}, u32[]{:S(2)}) collective-permute-start(f32[32,128]{1,0:T(8,128)S(1)} %get-tuple-element.61), channel_id=1, source_target_pairs={{0,8},{4,12},{8,0},{12,4},{16,24},{20,28},{24,16},{28,20},{1,9},{5... | collective-permute-start | bytes 49160 | tf_op jit(solution)/shard_map/ppermute | solution.py:542
  38.6 3.7 %collective-permute-start.6 = (f32[16,128]{1,0:T(8,128)S(1)}, f32[16,128]{1,0:T(8,128)S(1)}, u32[]{:S(2)}, u32[]{:S(2)}) collective-permute-start(f32[16,128]{1,0:T(8,128)S(1)} %get-tuple-element.63), channel_id=1, source_target_pairs={{0,4},{4,0},{8,12},{12,8},{16,20},{20,16},{24,28},{28,24},{1,5},{5... | collective-permute-start | bytes 24584 | tf_op jit(solution)/shard_map/ppermute | solution.py:542
where the time goes:
time: 43.4 us; the launch traced here: 43 us
  starting transfers between devices  15.9 us (37%)
  Pallas kernels  10.2 us (24%)
  local copies, waits for them, and re-layouts  8.37 us (19%)
  waiting for transfers between devices  7.84 us (18%)
  between operations  0.71 us (2%)
    pallas_call x8, Pallas kernels, call(): pl.pallas_call(kernel, out_shape=outs, in_specs=[pl.BlockSpec(memory_spac...  10.2 us
    ppermute x2, starting transfers between devices, exchange(): lax.ppermute(inside, 'space', pairs(0))  8.72 us
    unnamed x22, local copies, waits for them, and re-layouts  8.37 us
    ppermute x3, waiting for transfers between devices, swap(): return lax.ppermute(give, 'exc', [(i, i ^ bit) for i in range(owners)])  6.09 us
    ppermute x3, starting transfers between devices, swap(): return lax.ppermute(give, 'exc', [(i, i ^ bit) for i in range(owners)])  5.82 us
    ppermute x2, waiting for transfers between devices, exchange(): lax.ppermute(inside, 'space', pairs(0))  1.74 us
    ppermute x2, starting transfers between devices, exchange(): lax.ppermute(across, 'space', pairs(1))  1.33 us
  transfers between devices with their start and end apart: 7, of which 5 were waited for; matrix products, arithmetic and copies ran while one was open for 0% of the time, Pallas kernels for 2%

commit v1 on v0

--- a/solution.py
+++ b/solution.py
@@ -218,7 +218,9 @@
     return sign * both[16:32], -sign * both[0:16]
 
 
-def two_steps(table, x, hots, fe, fh, e, h, j, source, v, w, v_near, sent_a, sent_b):
+def two_steps(
+    table, x, hots, fe, fh, e, h, j, source, v, w, v_near, sent_a, sent_b, when_h=lambda: None
+):
     own, wide = (L0, L1), (A1, L0, L1, B1)
     for i in range(2):
         fe[L0 + i] = e[i]
@@ -261,6 +263,7 @@
 
     for layer, change in zip(wide, rate(table, x, hots, fe, wide, outer_of(fe, E_FIRST))):
         fh[layer] += TIME_STEP * change
+    when_h()
     second_j = [KEEP * first_j[i] + weight[i] * first_e[i] for i in range(2)]
     changes = rate(table, x, hots, fh, own, outer_of(fh, H_SECOND))
     for i in range(2):
@@ -376,7 +379,9 @@
     send(across, inside, 0, up, down)
 
 
-def early_kernel(mid_e, mid_j, end_e, end_j, levels, out):
+def early_kernel(mid_e, mid_j, end_e, end_j, levels, design, out, pixels):
+    pixel = jnp.bitwise_and(design[...], PIX_DEV - 1)
+    pixels[...] = one_hot(lax.broadcasted_iota(jnp.int32, pixels.shape, 0), pixel)
     for i in range(2):
         columns = slice(i * LAYER, (i + 1) * LAYER)
         start, middle, end = (levels[k, :, columns].astype(F32) for k in range(3))
@@ -386,71 +391,64 @@
         out[NODES : 2 * NODES, columns] = folded(mid_j[i] * start + end_j[i] * middle)
 
 
-def split(total, keep, give, bit):
-    half = total.shape[0] // 2
-    side = lax.rem(lax.axis_index("exc") // bit, 2)
-    keep[...] = total[pl.ds(pl.multiple_of(side * half, half), half), :]
-    give[...] = total[pl.ds(pl.multiple_of((1 - side) * half, half), half), :]
-
-
 def last_kernel(
-    bit, table, e, h, j, v, w, source, hot, v_near, hot_near, across_in, inside_in, *rest
+    table, e, h, j, v, w, source, hot, v_near, hot_near, across_in, inside_in, *rest
 ):
-    levels, early, design, out_e, out_h, keep, give = rest[:7]
-    fe, fh, x, sent_a, sent_b, sums = rest[7:]
+    levels, early, pixels, out_e, out_h, sums = rest[:6]
+    fe, fh, x, sent_a, sent_b, sems = rest[6:]
     sides(across_in, inside_in, sent_a, sent_b, SECOND)
 
     def hots(layer, face):
         at = hot_at(layer, face)
         return hot[at] if at < 12 else hot_near[at - 12]
 
-    first_e, first_j, second_e, second_j, magnetic = two_steps(
-        table, x, hots, fe, fh, e, h, j, source, v, w, v_near, sent_a, sent_b
-    )
+    copies = []
+
+    def write(field, target):
+        for i in range(2):
+            columns = pl.ds(i * LAYER, LAYER)
+            sem = sems.at[len(copies)]
+            copies.append(pltpu.make_async_copy(field.at[L0 + i], target.at[:, columns], sem))
+            copies[-1].start()
+
+    first_e, first_j, second_e, second_j, _ = two_steps(
+        table, x, hots, fe, fh, e, h, j, source, v, w, v_near, sent_a, sent_b,
+        lambda: write(fh, out_h),
+    )
+    write(fe, out_e)
     parts = []
     for i in range(2):
-        out_e[i] = second_e[i]
-        out_h[i] = magnetic[i]
         columns = slice(i * LAYER, (i + 1) * LAYER)
         start, middle, end = (levels[k, :, columns].astype(F32) for k in range(2, 5))
         eps = folded(first_e[i] * (middle - start) + second_e[i] * (end - middle))
         drude = folded(first_j[i] * start + second_j[i] * middle)
         parts.append(jnp.concatenate([eps, drude], axis=0) + early[:, columns])
     both = jnp.concatenate(parts, axis=1)
-    pixel = jnp.bitwise_and(design[...], PIX_DEV - 1)
-    pixels = one_hot(lax.broadcasted_iota(jnp.int32, (PIX_DEV, both.shape[1]), 0), pixel)
     high, low = halves(both)
-    sums[...] = dot_t(pixels, high) + dot_t(pixels, low)
-    split(sums, keep, give, bit)
-
-
-def write_kernel(e, h, out_e, out_h):
-    for i in range(2):
-        columns = slice(i * LAYER, (i + 1) * LAYER)
-        out_e[:, columns] = e[i]
-        out_h[:, columns] = h[i]
-
-
-def halve_kernel(bit, kept, came, keep, give, sums):
-    sums[...] = kept[...] + came[...]
-    split(sums, keep, give, bit)
-
-
-def total_kernel(owners, kept, came, eps, drude):
-    total = (kept[...] + came[...]) * (1.0 / owners)
+    sums[...] = dot_t(pixels[...], high) + dot_t(pixels[...], low)
+    for copy in copies:
+        copy.wait()
+
+
+def total_kernel(owners, parts, eps, drude):
+    share = parts.shape[0] // owners
+    total = parts[0:share]
+    for owner in range(1, owners):
+        total = total + parts[owner * share : (owner + 1) * share]
+    total = total * (1.0 / owners)
     eps[...] = total[:, 0:NODES]
     drude[...] = total[:, NODES : 2 * NODES]
 
 
-def call(kernel, outs, args, scratch=(), flops=0, space=pltpu.VMEM):
+def call(kernel, outs, args, scratch=(), flops=0, spaces=None, out_spaces=None):
     moved = sum(4 * int(np.prod(o.shape)) for o in outs) + sum(
         a.dtype.itemsize * int(np.prod(a.shape)) for a in args
     )
     return pl.pallas_call(
         kernel,
         out_shape=outs,
-        in_specs=[pl.BlockSpec(memory_space=space)] * len(args),
-        out_specs=[pl.BlockSpec(memory_space=pltpu.VMEM)] * len(outs),
+        in_specs=[pl.BlockSpec(memory_space=s) for s in spaces or [pltpu.VMEM] * len(args)],
+        out_specs=[pl.BlockSpec(memory_space=s) for s in out_spaces or [pltpu.VMEM] * len(outs)],
         scratch_shapes=list(scratch),
         compiler_params=pltpu.CompilerParams(vmem_limit_bytes=24 * 1024 * 1024),
         cost_estimate=pl.CostEstimate(flops=flops, bytes_accessed=moved, transcendentals=0),
@@ -497,6 +495,8 @@
         pltpu.VMEM((4, ROWS, LAYER), F32),
         pltpu.VMEM((5 * ROWS, 4 * LAYER), BF16),
     ]
+    given = [table, adj_e[0], adj_h[0], adj_j[0], inv_eps, drude_weight]
+    given += [neighbor, port_elems, port_profile[0]]
     once = 2 * ROWS * 5 * ROWS * LAYER
 
     table, e, h, j, v, w, _, source, hot, across, inside = call(
@@ -504,8 +504,7 @@
         [bf16(*table.shape), field, field, field, nodal, nodal]
         + [jax.ShapeDtypeStruct(neighbor.shape, jnp.int32), field, bf16(12, LAYER, LAYER)]
         + [f32(FIRST, LAYER)] * 2,
-        [table, adj_e[0], adj_h[0], adj_j[0], inv_eps, drude_weight]
-        + [neighbor, port_elems, port_profile[0]],
+        [pltpu.with_memory_space_constraint(a, pltpu.HBM) for a in given],
         work
         + [
             pltpu.VMEM(port_elems.shape, jnp.int32),
@@ -513,7 +512,7 @@
             pltpu.SemaphoreType.DMA((14,)),
         ],
         6 * once,
-        pltpu.HBM,
+        [pltpu.HBM] * len(given),
     )
     across, inside = exchange(across, inside)
     e2, h2, j2, e1, j1, v_near, hot_near, across, inside = call(
@@ -524,38 +523,26 @@
         18 * once,
     )
     across, inside = exchange(across, inside)
-    (early,) = call(early_kernel, [f32(2 * NODES, count)], [e1, j1, e2, j2, levels])
-    bit = owners // 2
-    size = PIX_DEV // 2
-    e4, h4, keep, give = call(
-        functools.partial(last_kernel, bit),
-        [field, field] + [f32(size, 2 * NODES)] * 2,
+    early, pixels = call(
+        early_kernel,
+        [f32(2 * NODES, count), bf16(PIX_DEV, count)],
+        [e1, j1, e2, j2, levels, design_map.reshape(1, count)],
+    )
+    out_e, out_h, sums = call(
+        last_kernel,
+        [f32(ROWS, count)] * 2 + [f32(PIX_DEV, 2 * NODES)],
         [table, e2, h2, j2, v, w, source, hot, v_near, hot_near, across, inside]
-        + [levels, early, design_map.reshape(1, count)],
-        work
-        + [pltpu.VMEM((SECOND, LAYER), F32)] * 2
-        + [pltpu.VMEM((PIX_DEV, 2 * NODES), F32)],
+        + [levels, early, pixels],
+        work + [pltpu.VMEM((SECOND, LAYER), F32)] * 2 + [pltpu.SemaphoreType.DMA((4,))],
         12 * once,
-    )
-
-    def swap(give, bit):
-        return lax.ppermute(give, "exc", [(i, i ^ bit) for i in range(owners)])
-
-    came = swap(give, bit)
-    out_e, out_h = call(write_kernel, [f32(ROWS, count)] * 2, [e4, h4])
-    while bit > 1:
-        bit, size = bit // 2, size // 2
-        keep, give = call(
-            functools.partial(halve_kernel, bit),
-            [f32(size, 2 * NODES)] * 2,
-            [keep, came],
-            [pltpu.VMEM((2 * size, 2 * NODES), F32)],
-        )
-        came = swap(give, bit)
+        None,
+        [pltpu.HBM, pltpu.HBM, pltpu.VMEM],
+    )
+    parts = lax.all_to_all(sums, "exc", split_axis=0, concat_axis=0, tiled=True)
     eps, drude = call(
         functools.partial(total_kernel, owners),
-        [f32(size, NODES)] * 2,
-        [keep, came],
+        [f32(PIX_DEV // owners, NODES)] * 2,
+        [parts],
     )
     return out_e[None], out_h[None], eps.T, drude.T
 

time: 43.4 us -> 36.1 us (0.83)
  blocking collectives: 0 us -> 12.8 us
  local copies, waits for them, and re-layouts: 8.37 us -> 0.68 us
  waiting for transfers between devices: 7.84 us -> 1.06 us
  starting transfers between devices: 15.9 us -> 10.1 us
    all_to_all x0 -> x1, blocking collectives: none -> 12.8 us  [local(): parts = lax.all_to_all(sums, 'exc', split_axis=0, concat_axis=0, tiled=True)]
    unnamed x22 -> x4, local copies, waits for them, and re-layouts: 8.37 us -> 0.68 us
    ppermute x3 -> x0, waiting for transfers between devices: 6.09 us -> none  [swap(): return lax.ppermute(give, 'exc', [(i, i ^ bit) for i in range(owners)])]
    ppermute x3 -> x0, starting transfers between devices: 5.82 us -> none  [swap(): return lax.ppermute(give, 'exc', [(i, i ^ bit) for i in range(owners)])]
    ppermute x2, waiting for transfers between devices: 1.74 us -> 1.05 us  [exchange(): lax.ppermute(inside, 'space', pairs(0))]
    pallas_call x8 -> x5, Pallas kernels: 10.2 us -> 10.5 us  [call(): pl.pallas_call(kernel, out_shape=outs, in_specs=[pl.BlockSpec(memory_spac...]
  transfers between devices with their start and end apart: 7 -> 4, of which waited for: 5 -> 2; matrix products, arithmetic and copies ran while one was open for 0% -> 0% of each run, Pallas kernels for 2% -> 0%
where the time goes in v1:
time: 36.1 us; the launch traced here: 35.8 us
  blocking collectives  12.8 us (35%)
  Pallas kernels  10.5 us (29%)
  starting transfers between devices  10.1 us (28%)
  waiting for transfers between devices  1.06 us (3%)
  between operations  0.69 us (2%)
  local copies, waits for them, and re-layouts  0.68 us (2%)
    all_to_all x1, blocking collectives, local(): parts = lax.all_to_all(sums, 'exc', split_axis=0, concat_axis=0, tiled=True)  12.8 us
    pallas_call x5, Pallas kernels, call(): pl.pallas_call(kernel, out_shape=outs, in_specs=[pl.BlockSpec(memory_spac...  10.5 us
    ppermute x2, starting transfers between devices, exchange(): lax.ppermute(inside, 'space', pairs(0))  8.72 us
    ppermute x2, starting transfers between devices, exchange(): lax.ppermute(across, 'space', pairs(1))  1.33 us
    ppermute x2, waiting for transfers between devices, exchange(): lax.ppermute(inside, 'space', pairs(0))  1.05 us
  transfers between devices with their start and end apart: 4, of which 2 were waited for; matrix products, arithmetic and copies ran while one was open for 0% of the time, Pallas kernels for 0%

profile of v1, /device:TPU:0, one launch (start us, length us, event | category | flops | bytes accessed | tf_op | source)
XLA Modules:
  0.0 35.8 jit_solution(15017158425174948278)
XLA Ops:
  0.6 3.0 %shard_map.138 = (bf16[192,960]{1,0:T(8,128)(2,1)S(1)}, f32[2,192,128]{2,1,0:T(8,128)S(1)}, f32[2,192,128]{2,1,0:T(8,128)S(1)}, f32[2,192,128]{2,1,0:T(8,128)S(1...) custom-call(bf16[192,960]{1,0:T(8,128)(2,1)} %constant.2.clone.table, ...), custom_call_target="tpu_custom_call" | custom-call | flops 283115520 | bytes 3846656 | tf_op jit(solution)/shard_map/pallas_call | solution.py:447
  3.7 0.7 %collective-permute-start = (f32[200,128]{1,0:T(8,128)S(1)}, f32[200,128]{1,0:T(8,128)S(1)}, u32[]{:S(2)}, u32[]{:S(2)}) collective-permute-start(f32[200,128]{1,0:T(8,128)S(1)} %get-tuple-element.38), channel_id=1, source_target_pairs={{1,2},{2,1},{5,6},{6,5},{9,10},{10,9},{13,14},{14,13},{17,18},{18,... | collective-permute-start | bytes 307208 | tf_op jit(solution)/shard_map/ppermute | solution.py:473
  4.4 4.4 %collective-permute-start.1 = (f32[200,128]{1,0:T(8,128)S(1)}, f32[200,128]{1,0:T(8,128)S(1)}, u32[]{:S(2)}, u32[]{:S(2)}) collective-permute-start(f32[200,128]{1,0:T(8,128)S(1)} %get-tuple-element.39), channel_id=1, source_target_pairs={{0,1},{2,3},{1,0},{3,2},{4,5},{6,7},{5,4},{7,6},{8,9},{10,11},{9,8... | collective-permute-start | bytes 307208 | tf_op jit(solution)/shard_map/ppermute | solution.py:473
  8.7 0.0 collective-permute-done.across_in
  8.7 0.9 %collective-permute-done.1.inside_in = f32[200,128]{1,0:T(8,128)S(1)} collective-permute-done((f32[200,128]{1,0:T(8,128)S(1)}, f32[200,128]{1,0:T(8,128)S(1)}, u32[]{:S(2)}, u32[]{:S(2)}) %collective-permute-start.1) | collective-permute-done | bytes 102432 | tf_op jit(solution)/shard_map/ppermute | solution.py:473
  9.7 0.0 copy-start
  9.7 3.7 %shard_map.139 = (f32[2,192,128]{2,1,0:T(8,128)S(1)}, f32[2,192,128]{2,1,0:T(8,128)S(1)}, f32[2,192,128]{2,1,0:T(8,128)S(1)}, f32[2,192,128]{2,1,0:T(8,128)S(1)}...) custom-call(bf16[192,960]{1,0:T(8,128)(2,1)S(1)} %get-tuple-element., ...), custom_call_target="tpu_custom_call" | custom-call | flops 849346560 | bytes 3719168 | tf_op jit(solution)/shard_map/pallas_call | solution.py:447
  13.4 0.7 %collective-permute-start.2 = (f32[128,128]{1,0:T(8,128)S(1)}, f32[128,128]{1,0:T(8,128)S(1)}, u32[]{:S(2)}, u32[]{:S(2)}) collective-permute-start(f32[128,128]{1,0:T(8,128)S(1)} %get-tuple-element.45), channel_id=1, source_target_pairs={{1,2},{2,1},{5,6},{6,5},{9,10},{10,9},{13,14},{14,13},{17,18},{18,... | collective-permute-start | bytes 196616 | tf_op jit(solution)/shard_map/ppermute | solution.py:473
  14.1 4.4 %collective-permute-start.3 = (f32[128,128]{1,0:T(8,128)S(1)}, f32[128,128]{1,0:T(8,128)S(1)}, u32[]{:S(2)}, u32[]{:S(2)}) collective-permute-start(f32[128,128]{1,0:T(8,128)S(1)} %get-tuple-element.46), channel_id=1, source_target_pairs={{0,1},{2,3},{1,0},{3,2},{4,5},{6,7},{5,4},{7,6},{8,9},{10,11},{9,8... | collective-permute-start | bytes 196616 | tf_op jit(solution)/shard_map/ppermute | solution.py:473
  18.5 0.0 copy-start.1
  18.5 0.0 copy-done
  18.5 0.7 %copy-done.1 = s32[256]{0:T(256)S(1)} copy-done((s32[256]{0:T(256)S(1)}, s32[256]{0:T(256)}, u32[]{:S(2)}) %copy-start.1) | copy-done | bytes 1048
  19.1 0.1 shard_map.140
  19.2 0.0 collective-permute-done.2.across_in
  19.3 0.1 collective-permute-done.3.inside_in
  19.4 3.0 %shard_map.141 = (f32[192,256]{1,0:T(8,128)}, f32[192,256]{1,0:T(8,128)}, f32[128,128]{1,0:T(8,128)S(1)}) custom-call(bf16[192,960]{1,0:T(8,128)(2,1)S(1)} %get-tuple-element.30.table, f32[2,192,128]{2,1,0:T(8,128)S(1)} %get-tuple-element.40.end_e.e, f32[2,192,128]{2,1,0:T(8,128)S(1)} %get-tuple-element.41.h, f32[2,192,128]{2,1,0:T(8,128)S(1)} %get-tuple-element.42.end_j.j, ...), custom_call_target="tpu_custom_call" | custom-call | flops 566231040 | bytes 3350528 | tf_op jit(solution)/shard_map/pallas_call | solution.py:447
  22.3 12.8 %all_to_all.11 = f32[8,16,128]{2,1,0:T(8,128)S(1)} all-to-all(f32[8,16,128]{2,1,0:T(8,128)S(1)} %bitcast.15), channel_id=1, replica_groups=mesh['exc'=8,'space'=4] {'exc'}, dimensions={0} | all-to-all | bytes 131072 | tf_op jit(solution)/shard_map/all_to_all | solution.py:541
  35.1 0.7 %shard_map.142 = (f32[16,64]{1,0:T(8,128)}, f32[16,64]{1,0:T(8,128)}) custom-call(f32[128,128]{1,0:T(8,128)S(1)} %bitcast.14), custom_call_target="tpu_custom_call" | custom-call | bytes 73728 | tf_op jit(solution)/shard_map/pallas_call | solution.py:447
Async XLA Ops:
  3.7 5.0 %collective-permute-start = (f32[200,128]{1,0:T(8,128)S(1)}, f32[200,128]{1,0:T(8,128)S(1)}, u32[]{:S(2)}, u32[]{:S(2)}) collective-permute-start(f32[200,128]{1,0:T(8,128)S(1)} %get-tuple-element.38), channel_id=1, source_target_pairs={{1,2},{2,1},{5,6},{6,5},{9,10},{10,9},{13,14},{14,13},{17,18},{18,... | collective-permute-start | bytes 307208 | tf_op jit(solution)/shard_map/ppermute | solution.py:473
  4.4 5.3 %collective-permute-start.1 = (f32[200,128]{1,0:T(8,128)S(1)}, f32[200,128]{1,0:T(8,128)S(1)}, u32[]{:S(2)}, u32[]{:S(2)}) collective-permute-start(f32[200,128]{1,0:T(8,128)S(1)} %get-tuple-element.39), channel_id=1, source_target_pairs={{0,1},{2,3},{1,0},{3,2},{4,5},{6,7},{5,4},{7,6},{8,9},{10,11},{9,8... | collective-permute-start | bytes 307208 | tf_op jit(solution)/shard_map/ppermute | solution.py:473
  9.7 8.8 %copy-start = (bf16[1,5,192,256]{3,2,1,0:T(8,128)(2,1)S(1)}, bf16[1,5,192,256]{3,2,1,0:T(8,128)(2,1)}, u32[]{:S(2)}) copy-start(bf16[1,5,192,256]{3,2,1,0:T(8,128)(2,1)} %param.14) | copy-start | bytes 1474564
  13.4 5.8 %collective-permute-start.2 = (f32[128,128]{1,0:T(8,128)S(1)}, f32[128,128]{1,0:T(8,128)S(1)}, u32[]{:S(2)}, u32[]{:S(2)}) collective-permute-start(f32[128,128]{1,0:T(8,128)S(1)} %get-tuple-element.45), channel_id=1, source_target_pairs={{1,2},{2,1},{5,6},{6,5},{9,10},{10,9},{13,14},{14,13},{17,18},{18,... | collective-permute-start | bytes 196616 | tf_op jit(solution)/shard_map/ppermute | solution.py:473
  14.1 5.3 %collective-permute-start.3 = (f32[128,128]{1,0:T(8,128)S(1)}, f32[128,128]{1,0:T(8,128)S(1)}, u32[]{:S(2)}, u32[]{:S(2)}) collective-permute-start(f32[128,128]{1,0:T(8,128)S(1)} %get-tuple-element.46), channel_id=1, source_target_pairs={{0,1},{2,3},{1,0},{3,2},{4,5},{6,7},{5,4},{7,6},{8,9},{10,11},{9,8... | collective-permute-start | bytes 196616 | tf_op jit(solution)/shard_map/ppermute | solution.py:473
  18.5 0.7 %copy-start.1 = (s32[256]{0:T(256)S(1)}, s32[256]{0:T(256)}, u32[]{:S(2)}) copy-start(s32[256]{0:T(256)} %param.18) | copy-start | bytes 3076

commit v2 on v1

v2 whole, which is shorter than its diff:
```python
import functools

import jax
import jax.numpy as jnp
import ml_dtypes
import numpy as np
from jax import lax
from jax.experimental import pallas as pl
from jax.experimental.pallas import tpu as pltpu
from jax.sharding import PartitionSpec as P

NODES = 64
ROWS = 3 * NODES
LAYER = 128
PIX_DEV = 128

TIME_STEP = 0.025
DAMPING = 0.5
KEEP = 1.0 - TIME_STEP * DAMPING

TANGENT = 32
E_START = 0
H_FIRST = 32
E_FIRST = 64
H_SECOND = 96
SECOND = 128
V_NEAR = 128
N_NEAR = V_NEAR + NODES
FIRST = N_NEAR + 8

A1, L0, L1, B1 = range(4)

BASE = (NODES, 0, 2 * NODES)

BF16 = jnp.bfloat16
F32 = jnp.float32


def parity(c, face, other):
    d = face // 2
    sign = 1.0 if face % 2 else -1.0
    return 6.0 * sign * (c - d) * (d - other) * (other - c) / 2.0


def own_rate():
    points = np.array([-1.0, -1.0 / np.sqrt(5.0), 1.0 / np.sqrt(5.0), 1.0])
    barycentric = np.array(
        [1.0 / np.prod([points[j] - points[k] for k in range(4) if k != j]) for j in range(4)]
    )
    deriv = np.zeros((4, 4))
    for row in range(4):
        for column in range(4):
            if row != column:
                deriv[row, column] = (
                    barycentric[column] / barycentric[row] / (points[row] - points[column])
                )
        deriv[row, row] = -np.sum(deriv[row])
    identity = np.eye(4)
    along_x = 2.0 * np.kron(np.kron(deriv, identity), identity)
    along_y = 2.0 * np.kron(np.kron(identity, deriv), identity)
    along_z = 2.0 * np.kron(np.kron(identity, identity), deriv)
    curl = np.zeros((192, 192))
    curl[0:64, 64:128] = -along_z
    curl[0:64, 128:192] = along_y
    curl[64:128, 0:64] = along_z
    curl[64:128, 128:192] = -along_x
    curl[128:192, 0:64] = -along_y
    curl[128:192, 64:128] = along_x
    numbers = np.arange(64).reshape(4, 4, 4)
    faces = np.stack(
        [
            numbers[0].ravel(),
            numbers[3].ravel(),
            numbers[:, 0].ravel(),
            numbers[:, 3].ravel(),
            numbers[:, :, 0].ravel(),
            numbers[:, :, 3].ravel(),
        ]
    )
    inner = np.zeros((192, 192))
    for face in range(6):
        for c in range(3):
            for other in range(3):
                value = parity(c, face, other)
                if value != 0:
                    for node in faces[face]:
                        inner[c * 64 + node, other * 64 + node] += value
    return inner - curl


def step_tables():
    order = np.concatenate([np.arange(64) + 64 * c for c in (1, 0, 2)])
    own = own_rate()[order][:, order]
    high = own.astype(ml_dtypes.bfloat16)
    low = (own - high.astype(np.float64)).astype(ml_dtypes.bfloat16)
    table = np.concatenate([high, high, low], axis=1)
    ends = [table[BASE[c] + 16 * i : BASE[c] + 16 * i + 16] for i in (0, 3) for c in (1, 2)]
    return table, np.concatenate(ends, axis=0)


def halves(x):
    high = x.astype(BF16)
    return high, (x - high.astype(F32)).astype(BF16)


def dot(a, b):
    return jnp.dot(a, b, preferred_element_type=F32)


def dot_t(a, b):
    return lax.dot_general(a, b, (((1,), (1,)), ((), ())), preferred_element_type=F32)


def thrice(x):
    return jnp.concatenate([x, x, x], axis=0)


def folded(x):
    return x[0:NODES] + x[NODES : 2 * NODES] + x[2 * NODES : ROWS]


def stored(x):
    return jnp.concatenate([x[NODES : 2 * NODES], x[0:NODES], x[2 * NODES : ROWS]], axis=0)


def one_hot(rows, targets):
    return (rows == targets).astype(F32).astype(BF16)


def picked(x, index):
    rows = x.shape[0]
    if rows < 8:
        index = index[0:rows]
    elif rows > 8:
        index = jnp.concatenate([index] * (rows // 8), axis=0)
    along = lax.GatherDimensionNumbers(
        offset_dims=(),
        collapsed_slice_dims=(1,),
        start_index_map=(1,),
        operand_batching_dims=(0,),
        start_indices_batching_dims=(0,),
    )
    mode = lax.GatherScatterMode.PROMISE_IN_BOUNDS
    return lax.gather(x, index[..., None], along, (1, 1), mode=mode)


def at_end(face):
    return 3 if face % 2 else 0


def x_traces(field, layer, face):
    at = 16 * at_end(face)
    return [field[layer, BASE[c] + at : BASE[c] + at + 16, :] for c in (1, 2)]


def lift_x(target, layer, face, scale, y, z):
    at = 16 * at_end(face)
    rows = slice(BASE[1] + at, BASE[1] + at + 16)
    target[layer, rows, :] += (-scale * parity(1, face, 2)) * z
    rows = slice(BASE[2] + at, BASE[2] + at + 16)
    target[layer, rows, :] += (-scale * parity(2, face, 1)) * y


def lift_inside(target, field, layer, index, scale):
    first = lax.broadcasted_iota(jnp.int32, (8, LAYER), 0) < 4
    for face in (2, 3):
        factor = jnp.where(first, -scale * parity(0, face, 2), -scale * parity(2, face, 0))
        for k in range(4):
            at = BASE[0] + 4 * at_end(face ^ 1) + k
            got = picked(field[layer, pl.ds(at, 8, stride=16), :], index(layer, face))
            at = BASE[0] + 4 * at_end(face) + k
            turned = pltpu.roll(got, 4, 0)
            target[layer, pl.ds(at, 8, stride=16), :] += factor * turned
    for face in (4, 5):
        here, there = at_end(face), at_end(face ^ 1)
        x, y = (
            picked(field[layer, pl.ds(BASE[c] + there, 16, stride=4), :], index(layer, face))
            for c in (0, 1)
        )
        target[layer, pl.ds(BASE[0] + here, 16, stride=4), :] += (-scale * parity(0, face, 1)) * y
        target[layer, pl.ds(BASE[1] + here, 16, stride=4), :] += (-scale * parity(1, face, 0)) * x


def lift_end(target, field, layer, i, index, scale, to_x):
    for face in (2, 3):
        source, sink = (2, 0) if to_x else (0, 2)
        at = BASE[source] + 16 * i + 4 * at_end(face ^ 1)
        got = picked(field[layer, at : at + 4, :], index(layer, face))
        at = BASE[sink] + 16 * i + 4 * at_end(face)
        target[layer, at : at + 4, :] += (-scale * parity(sink, face, source)) * got
    for face in (4, 5):
        source, sink = (1, 0) if to_x else (0, 1)
        at = BASE[source] + 16 * i + at_end(face ^ 1)
        got = picked(field[layer, pl.ds(at, 4, stride=4), :], index(layer, face))
        at = BASE[sink] + 16 * i + at_end(face)
        target[layer, pl.ds(at, 4, stride=4), :] += (-scale * parity(sink, face, source)) * got


def own_parts(table, x, values):
    for i, value in enumerate(values):
        here = slice(i * LAYER, (i + 1) * LAYER)
        high, low = halves(value)
        x[0:ROWS, here] = high
        x[ROWS : 2 * ROWS, here] = low
        x[2 * ROWS : 3 * ROWS, here] = high
    found = dot(table[...], x[...])
    return [found[:, i * LAYER : (i + 1) * LAYER] for i in range(2)]


def near_parts(table, a, b):
    both = jnp.concatenate([a.astype(BF16), b.astype(BF16)], axis=1)
    found = dot(table[:, 0:ROWS], both)
    return found[:, 0:LAYER], found[:, LAYER : 2 * LAYER]


def lonely(table, ends, x, index, fe, fh, acc, electric, drive, v):
    own = (L0, L1)

    def between(target, field, scale):
        for layer, face in ((L0, 1), (L1, 0)):
            y, z = x_traces(field, L0 + L1 - layer, face ^ 1)
            got = [picked(t, index(layer, face)) for t in (y, z)]
            lift_x(target, layer, face, scale, *got)

    def ends_of(field):
        return x_traces(field, L1, 1), x_traces(field, L0, 0)

    found = [ends_of(fe)]
    parts = own_parts(table, x, electric)
    between(fh, fe, TIME_STEP)
    magnetic = []
    for i, layer in enumerate(own):
        lift_inside(fh, fe, layer, index, TIME_STEP)
        magnetic.append(fh[layer] + TIME_STEP * parts[i])
        fh[layer] = magnetic[i]
    found.append(ends_of(fh))
    parts = own_parts(table, x, magnetic)
    for i, layer in enumerate(own):
        acc[layer] = drive[i]
    between(acc, fh, 1.0)
    for i, layer in enumerate(own):
        lift_inside(acc, fh, layer, index, 1.0)
        electric[i] = electric[i] - TIME_STEP * thrice(v[i]) * (parts[i] + acc[layer])
        fe[layer] = electric[i]
    found.append(ends_of(fe))
    parts = own_parts(ends, x, electric)
    for i, layer in enumerate(own):
        face = i
        lift_end(fh, fe, layer, at_end(face), index, TIME_STEP, False)
        for place, c in enumerate((1, 2)):
            at = BASE[c] + 16 * at_end(face)
            part = parts[i][32 * i + 16 * place : 32 * i + 16 * place + 16]
            fh[layer, at : at + 16, :] += TIME_STEP * part
    found.append(ends_of(fh))
    return [jnp.concatenate(sum(traces, []), axis=0) for traces in zip(*found)]


def two_steps(
    tables, x, index, valid, fe, fh, acc, e, h, j, source, v, w, v_near, sent_a, sent_b, when_h
):
    table, ends = tables
    own = (L0, L1)
    sides = ((A1, 1, L0, sent_a), (B1, 0, L1, sent_b))
    electric = [e[0], e[1]]
    magnetic = [h[0], h[1]]
    for i, layer in enumerate(own):
        fe[layer] = electric[i]
        fh[layer] = magnetic[i]

    def between(target, field, scale, start, answered=True):
        for layer, face in ((L0, 1), (L1, 0)):
            y, z = x_traces(field, L0 + L1 - layer, face ^ 1)
            got = [picked(t, index(layer, face)) for t in (y, z)]
            lift_x(target, layer, face, scale, *got)
        for side, (near, face, layer, sent) in enumerate(sides):
            traces = [sent[start + 16 * t : start + 16 * t + 16, :] for t in range(2)]
            if answered:
                traces = [a + b for a, b in zip(traces, x_traces(field, near, face))]
            mask = jnp.concatenate([valid[side]] * 2, axis=0)
            got = [picked(t, index(layer, face ^ 1)) * mask for t in traces]
            lift_x(target, layer, face ^ 1, scale, *got)

    def outward(target, field, scale):
        for near, face, layer, _ in sides:
            y, z = x_traces(field, layer, face ^ 1)
            got = [picked(t, index(near, face)) for t in (y, z)]
            lift_x(target, near, face, scale, *got)

    weight = [TIME_STEP * thrice(w[i]) for i in range(2)]
    blank = jnp.zeros((ROWS, LAYER), F32)

    parts = own_parts(table, x, electric)
    for near, _, _, _ in sides:
        fh[near] = blank
        acc[near] = blank
    outward(fh, fe, TIME_STEP)
    between(fh, fe, TIME_STEP, E_START, False)
    for i, layer in enumerate(own):
        lift_inside(fh, fe, layer, index, TIME_STEP)
        magnetic[i] = fh[layer] + TIME_STEP * parts[i]
        fh[layer] = magnetic[i]

    first_j = [KEEP * j[i] + weight[i] * electric[i] for i in range(2)]
    parts = own_parts(table, x, magnetic)
    near_found = near_parts(table, fh[A1], fh[B1])
    for i, layer in enumerate(own):
        acc[layer] = first_j[i] + source[i]
    between(acc, fh, 1.0, H_FIRST)
    outward(acc, fh, 1.0)
    for i, layer in enumerate(own):
        lift_inside(acc, fh, layer, index, 1.0)
        electric[i] = electric[i] - TIME_STEP * thrice(v[i]) * (parts[i] + acc[layer])
        fe[layer] = electric[i]
    first_e = list(electric)
    near_e = []
    for side, (near, face, _, _) in enumerate(sides):
        lift_end(acc, fh, near, at_end(face), index, 1.0, True)
        near_e.append(-TIME_STEP * thrice(v_near[side]) * (near_found[side] + acc[near]))
        fe[near] = near_e[side]

    parts = own_parts(table, x, electric)
    near_found = near_parts(ends, *near_e)
    between(fh, fe, TIME_STEP, E_FIRST)
    outward(fh, fe, TIME_STEP)
    for i, layer in enumerate(own):
        lift_inside(fh, fe, layer, index, TIME_STEP)
        magnetic[i] = fh[layer] + TIME_STEP * parts[i]
        fh[layer] = magnetic[i]
    when_h()
    for side, (near, face, _, _) in enumerate(sides):
        lift_end(fh, fe, near, at_end(face), index, TIME_STEP, False)
        for place, c in enumerate((1, 2)):
            at = BASE[c] + 16 * at_end(face)
            start = 32 * face + 16 * place
            fh[near, at : at + 16, :] += TIME_STEP * near_found[side][start : start + 16]

    second_j = [KEEP * first_j[i] + weight[i] * electric[i] for i in range(2)]
    parts = own_parts(table, x, magnetic)
    for i, layer in enumerate(own):
        acc[layer] = second_j[i] + source[i]
    between(acc, fh, 1.0, H_SECOND)
    for i, layer in enumerate(own):
        lift_inside(acc, fh, layer, index, 1.0)
        electric[i] = electric[i] - TIME_STEP * thrice(v[i]) * (parts[i] + acc[layer])
        fe[layer] = electric[i]
    return first_e, first_j, electric, second_j, magnetic


def odd_rank():
    return lax.rem(lax.axis_index("space"), 2) == 1


def send(across, inside, at, up, down):
    odd = odd_rank()
    rows = slice(at, at + up.shape[0])
    across[rows, :] = jnp.where(odd, up, down)
    inside[rows, :] = jnp.where(odd, down, up)


def sides_of(across, inside, a, b, rows):
    odd = odd_rank()
    from_across, from_inside = across[0:rows, :], inside[0:rows, :]
    a[...] = jnp.where(odd, from_inside, from_across)
    b[...] = jnp.where(odd, from_across, from_inside)


def first_kernel(
    table_in, ends_in, e_in, h_in, j_in, v_in, w_in, near_in, ports_in, profile_in, *rest
):
    table, ends, e, h, j, v, w, source, places, valid, across, inside = rest[:12]
    fe, fh, acc, x, neighbor, ports, profile, sems = rest[12:]
    copies = []

    def fetch(origin, target):
        copies.append(pltpu.make_async_copy(origin, target, sems.at[len(copies)]))
        copies[-1].start()
        return copies[-1]

    early = [fetch(near_in, neighbor), fetch(ports_in, ports), fetch(profile_in, profile)]
    fields = []
    for origin, target in ((e_in, e), (h_in, h), (j_in, j), (w_in, w), (v_in, v)):
        for i in range(2):
            fields.append(fetch(origin.at[:, pl.ds(i * LAYER, LAYER)], target.at[i]))
    last = [fetch(table_in, table), fetch(ends_in, ends)]

    for copy in early:
        copy.wait()
    found = neighbor[...]
    place = jnp.where(found < 0, 0, jnp.bitwise_and(found, LAYER - 1))
    for i in range(2):
        columns = slice(i * LAYER, (i + 1) * LAYER)
        for face in range(6):
            places[6 * i + face] = jnp.broadcast_to(place[face : face + 1, columns], (8, LAYER))
        there = (found[i : i + 1, columns] >= 0).astype(F32)
        valid[i] = jnp.broadcast_to(there, (8, LAYER))
    count = 2 * LAYER
    targets = lax.broadcasted_iota(jnp.int32, (count, ports.shape[1]), 0)
    spread_hot = one_hot(targets, jnp.bitwise_and(ports[...], count - 1))
    high, low = halves(profile[...])
    spread = dot_t(high, spread_hot) + dot_t(low, spread_hot)
    for i in range(2):
        source[i] = stored(spread[:, i * LAYER : (i + 1) * LAYER])
    for copy in fields:
        copy.wait()
    electric, drive = [], []
    for i in range(2):
        electric.append(stored(e[i]))
        fe[L0 + i] = electric[i]
        fh[L0 + i] = stored(h[i])
        weight = TIME_STEP * thrice(w[i])
        drive.append(KEEP * stored(j[i]) + weight * electric[i] + source[i])
    for copy in last:
        copy.wait()

    def index(layer, face):
        return places[6 * (layer - L0) + face]

    up, down = lonely(table, ends, x, index, fe, fh, acc, electric, drive, v)
    send(across, inside, 0, up, down)
    send(across, inside, V_NEAR, v[1], v[0])
    blank = jnp.zeros((2, LAYER), F32)
    place = place.astype(F32)
    send(
        across,
        inside,
        N_NEAR,
        jnp.concatenate([place[:, LAYER : 2 * LAYER], blank], axis=0),
        jnp.concatenate([place[:, 0:LAYER], blank], axis=0),
    )


def index_of(places, near_places):
    def index(layer, face):
        if layer in (L0, L1):
            return places[6 * (layer - L0) + face]
        return near_places[6 * (layer == B1) + face]

    return index


def middle_kernel(
    table, ends, e, h, j, v, w, source, places, valid, across_in, inside_in, *rest
):
    out_e, out_h, out_j, mid_e, mid_j, v_near, near_places, across, inside = rest[:9]
    fe, fh, acc, x, sent_a, sent_b = rest[9:]
    sides_of(across_in, inside_in, sent_a, sent_b, FIRST)
    for side, sent in enumerate((sent_a, sent_b)):
        v_near[side] = sent[V_NEAR : V_NEAR + NODES, :]
        place = sent[N_NEAR : N_NEAR + 8, :].astype(jnp.int32)
        for face in range(6):
            near_places[6 * side + face] = jnp.broadcast_to(place[face : face + 1], (8, LAYER))
    index = index_of(places, near_places)
    start = [[stored(field[i]) for i in range(2)] for field in (e, h, j)]
    first_e, first_j, second_e, second_j, magnetic = two_steps(
        (table, ends), x, index, valid, fe, fh, acc, *start, source, v, w, v_near,
        sent_a, sent_b, lambda: None,
    )
    drive = []
    for i in range(2):
        mid_e[i] = first_e[i]
        mid_j[i] = first_j[i]
        out_e[i] = second_e[i]
        out_j[i] = second_j[i]
        out_h[i] = magnetic[i]
        weight = TIME_STEP * thrice(w[i])
        drive.append(KEEP * second_j[i] + weight * second_e[i] + source[i])
    up, down = lonely(table, ends, x, index, fe, fh, acc, list(second_e), drive, v)
    send(across, inside, 0, up, down)


def early_kernel(mid_e, mid_j, end_e, end_j, levels, design, out, pixels):
    pixel = jnp.bitwise_and(design[...], PIX_DEV - 1)
    pixels[...] = one_hot(lax.broadcasted_iota(jnp.int32, pixels.shape, 0), pixel)
    for i in range(2):
        columns = slice(i * LAYER, (i + 1) * LAYER)
        start, middle, end = (stored(levels[k, :, columns].astype(F32)) for k in range(3))
        out[0:NODES, columns] = folded(
            mid_e[i] * (middle - start) + end_e[i] * (end - middle)
        )
        out[NODES : 2 * NODES, columns] = folded(mid_j[i] * start + end_j[i] * middle)


def last_kernel(
    table, ends, e, h, j, v, w, source, places, valid, v_near, near_places,
    across_in, inside_in, levels, early, pixels, *rest
):
    out_e, out_h, sums = rest[:3]
    fe, fh, acc, x, sent_a, sent_b, sems = rest[3:]
    sides_of(across_in, inside_in, sent_a, sent_b, SECOND)
    copies = []

    def write(field, target):
        for i in range(2):
            for c in range(3):
                origin = field.at[L0 + i, pl.ds(BASE[c], NODES), :]
                there = target.at[pl.ds(c * NODES, NODES), pl.ds(i * LAYER, LAYER)]
                copies.append(pltpu.make_async_copy(origin, there, sems.at[len(copies)]))
                copies[-1].start()

    first_e, first_j, second_e, second_j, _ = two_steps(
        (table, ends), x, index_of(places, near_places), valid, fe, fh, acc,
        e, h, j, source, v, w, v_near, sent_a, sent_b, lambda: write(fh, out_h),
    )
    write(fe, out_e)
    parts = []
    for i in range(2):
        columns = slice(i * LAYER, (i + 1) * LAYER)
        start, middle, end = (stored(levels[k, :, columns].astype(F32)) for k in range(2, 5))
        eps = folded(first_e[i] * (middle - start) + second_e[i] * (end - middle))
        drude = folded(first_j[i] * start + second_j[i] * middle)
        parts.append(jnp.concatenate([eps, drude], axis=0) + early[:, columns])
    both = jnp.concatenate(parts, axis=1)
    high, low = halves(both)
    sums[...] = dot_t(pixels[...], high) + dot_t(pixels[...], low)
    for copy in copies:
        copy.wait()


def total_kernel(owners, parts, eps, drude):
    share = parts.shape[0] // owners
    total = parts[0:share]
    for owner in range(1, owners):
        total = total + parts[owner * share : (owner + 1) * share]
    total = total * (1.0 / owners)
    eps[...] = total[:, 0:NODES]
    drude[...] = total[:, NODES : 2 * NODES]


def call(kernel, outs, args, scratch=(), flops=0, spaces=None, out_spaces=None):
    moved = sum(4 * int(np.prod(o.shape)) for o in outs) + sum(
        a.dtype.itemsize * int(np.prod(a.shape)) for a in args
    )
    return pl.pallas_call(
        kernel,
        out_shape=outs,
        in_specs=[pl.BlockSpec(memory_space=s) for s in spaces or [pltpu.VMEM] * len(args)],
        out_specs=[pl.BlockSpec(memory_space=s) for s in out_spaces or [pltpu.VMEM] * len(outs)],
        scratch_shapes=list(scratch),
        compiler_params=pltpu.CompilerParams(vmem_limit_bytes=24 * 1024 * 1024),
        cost_estimate=pl.CostEstimate(flops=flops, bytes_accessed=moved, transcendentals=0),
    )(*args)


def f32(*shape):
    return jax.ShapeDtypeStruct(shape, F32)


def bf16(*shape):
    return jax.ShapeDtypeStruct(shape, BF16)


def exchange(across, inside):
    size = lax.axis_size("space")

    def pairs(start):
        found = [(i, i + 1) for i in range(start, size - 1, 2)]
        return found + [(j, i) for i, j in found]

    return lax.ppermute(across, "space", pairs(1)), lax.ppermute(inside, "space", pairs(0))


def local(
    adj_e,
    adj_h,
    adj_j,
    fwd_e,
    inv_eps,
    drude_weight,
    neighbor,
    design_map,
    port_elems,
    port_profile,
):
    count = adj_e.shape[2]
    owners = lax.axis_size("exc")
    table, ends = (jnp.asarray(t) for t in step_tables())
    levels = fwd_e[0]
    field, nodal = f32(2, ROWS, LAYER), f32(2, NODES, LAYER)
    indices = jax.ShapeDtypeStruct((12, 8, LAYER), jnp.int32)
    work = [pltpu.VMEM((4, ROWS, LAYER), F32)] * 3
    work += [pltpu.VMEM((3 * ROWS, 2 * LAYER), BF16)]
    given = [table, ends, adj_e[0], adj_h[0], adj_j[0], inv_eps, drude_weight]
    given += [neighbor, port_elems, port_profile[0]]
    once = 2 * ROWS * 3 * ROWS * LAYER

    table, ends, e, h, j, v, w, source, places, valid, across, inside = call(
        first_kernel,
        [bf16(*table.shape), bf16(*ends.shape), field, field, field, nodal, nodal]
        + [field, indices, f32(2, 8, LAYER)]
        + [f32(FIRST, LAYER)] * 2,
        [pltpu.with_memory_space_constraint(a, pltpu.HBM) for a in given],
        work
        + [
            pltpu.VMEM(neighbor.shape, jnp.int32),
            pltpu.VMEM(port_elems.shape, jnp.int32),
            pltpu.VMEM(port_profile.shape[1:], F32),
            pltpu.SemaphoreType.DMA((15,)),
        ],
        6 * once,
        [pltpu.HBM] * len(given),
    )
    across, inside = exchange(across, inside)
    e2, h2, j2, e1, j1, v_near, near_places, across, inside = call(
        middle_kernel,
        [field] * 5 + [nodal, indices] + [f32(SECOND, LAYER)] * 2,
        [table, ends, e, h, j, v, w, source, places, valid, across, inside],
        work + [pltpu.VMEM((FIRST, LAYER), F32)] * 2,
        18 * once,
    )
    across, inside = exchange(across, inside)
    early, pixels = call(
        early_kernel,
        [f32(2 * NODES, count), bf16(PIX_DEV, count)],
        [e1, j1, e2, j2, levels, design_map.reshape(1, count)],
    )
    out_e, out_h, sums = call(
        last_kernel,
        [f32(ROWS, count)] * 2 + [f32(PIX_DEV, 2 * NODES)],
        [table, ends, e2, h2, j2, v, w, source, places, valid, v_near, near_places]
        + [across, inside, levels, early, pixels],
        work + [pltpu.VMEM((SECOND, LAYER), F32)] * 2 + [pltpu.SemaphoreType.DMA((12,))],
        12 * once,
        None,
        [pltpu.HBM, pltpu.HBM, pltpu.VMEM],
    )
    parts = lax.all_to_all(sums, "exc", split_axis=0, concat_axis=0, tiled=True)
    eps, drude = call(
        functools.partial(total_kernel, owners),
        [f32(PIX_DEV // owners, NODES)] * 2,
        [parts],
    )
    return out_e[None], out_h[None], eps.T, drude.T


def solution(mesh):
    return jax.shard_map(
        local,
        mesh=mesh,
        in_specs=(
            P("exc", None, "space"),
            P("exc", None, "space"),
            P("exc", None, "space"),
            P("exc", None, None, "space"),
            P(None, "space"),
            P(None, "space"),
            P(None, "space"),
            P("space"),
            P("exc", "space"),
            P("exc", None, "space"),
        ),
        out_specs=(
            P("exc", None, "space"),
            P("exc", None, "space"),
            P(None, ("space", "exc")),
            P(None, ("space", "exc")),
        ),
        check_vma=False,
    )
```

time: 36.1 us -> 33.1 us (0.917)
  Pallas kernels: 10.5 us -> 7.6 us
    pallas_call x5, Pallas kernels: 10.5 us -> 7.6 us  [call(): pl.pallas_call(kernel, out_shape=outs, in_specs=[pl.BlockSpec(memory_spac...]
where the time goes in v2:
time: 33.1 us; the launch traced here: 32.9 us
  blocking collectives  12.8 us (39%)
  starting transfers between devices  10.1 us (31%)
  Pallas kernels  7.6 us (23%)
  waiting for transfers between devices  1.06 us (3%)
  between operations  0.69 us (2%)
  local copies, waits for them, and re-layouts  0.68 us (2%)
    all_to_all x1, blocking collectives, local(): parts = lax.all_to_all(sums, 'exc', split_axis=0, concat_axis=0, tiled=True)  12.8 us
    ppermute x2, starting transfers between devices, exchange(): lax.ppermute(inside, 'space', pairs(0))  8.72 us
    pallas_call x5, Pallas kernels, call(): pl.pallas_call(kernel, out_shape=outs, in_specs=[pl.BlockSpec(memory_spac...  7.6 us
    ppermute x2, starting transfers between devices, exchange(): lax.ppermute(across, 'space', pairs(1))  1.33 us
    ppermute x2, waiting for transfers between devices, exchange(): lax.ppermute(inside, 'space', pairs(0))  1.05 us
    unnamed x4, local copies, waits for them, and re-layouts  0.68 us
  transfers between devices with their start and end apart: 4, of which 2 were waited for; matrix products, arithmetic and copies ran while one was open for 0% of the time, Pallas kernels for 0%

profile of v2, /device:TPU:0, one launch (start us, length us, event | category | flops | bytes accessed | tf_op | source)
XLA Modules:
  0.0 32.9 jit_solution(8374448070061299640)
XLA Ops:
  0.6 2.4 %shard_map.147 = (bf16[192,576]{1,0:T(8,128)(2,1)S(1)}, bf16[64,576]{1,0:T(8,128)(2,1)S(1)}, f32[2,192,128]{2,1,0:T(8,128)S(1)}, f32[2,192,128]{2,1,0:T(8,128)S(...) custom-call(bf16[192,576]{1,0:T(8,128)(2,1)} %constant.4.clone.table, ...), custom_call_target="tpu_custom_call" | custom-call | flops 169869312 | bytes 2890240 | tf_op jit(solution)/shard_map/pallas_call | solution.py:533
  3.0 0.7 %collective-permute-start = (f32[200,128]{1,0:T(8,128)S(1)}, f32[200,128]{1,0:T(8,128)S(1)}, u32[]{:S(2)}, u32[]{:S(2)}) collective-permute-start(f32[200,128]{1,0:T(8,128)S(1)} %get-tuple-element.42), channel_id=1, source_target_pairs={{1,2},{2,1},{5,6},{6,5},{9,10},{10,9},{13,14},{14,13},{17,18},{18,... | collective-permute-start | bytes 307208 | tf_op jit(solution)/shard_map/ppermute | solution.py:559
  3.7 4.4 %collective-permute-start.1 = (f32[200,128]{1,0:T(8,128)S(1)}, f32[200,128]{1,0:T(8,128)S(1)}, u32[]{:S(2)}, u32[]{:S(2)}) collective-permute-start(f32[200,128]{1,0:T(8,128)S(1)} %get-tuple-element.43), channel_id=1, source_target_pairs={{0,1},{2,3},{1,0},{3,2},{4,5},{6,7},{5,4},{7,6},{8,9},{10,11},{9,8... | collective-permute-start | bytes 307208 | tf_op jit(solution)/shard_map/ppermute | solution.py:559
  8.1 0.0 collective-permute-done.across_in
  8.1 0.9 %collective-permute-done.1.inside_in = f32[200,128]{1,0:T(8,128)S(1)} collective-permute-done((f32[200,128]{1,0:T(8,128)S(1)}, f32[200,128]{1,0:T(8,128)S(1)}, u32[]{:S(2)}, u32[]{:S(2)}) %collective-permute-start.1) | collective-permute-done | bytes 102432 | tf_op jit(solution)/shard_map/ppermute | solution.py:559
  9.0 0.0 copy-start
  9.0 2.3 %shard_map.148 = (f32[2,192,128]{2,1,0:T(8,128)S(1)}, f32[2,192,128]{2,1,0:T(8,128)S(1)}, f32[2,192,128]{2,1,0:T(8,128)S(1)}, f32[2,192,128]{2,1,0:T(8,128)S(1)}...) custom-call(bf16[192,576]{1,0:T(8,128)(2,1)S(1)} %get-tuple-element., ...), custom_call_target="tpu_custom_call" | custom-call | flops 509607936 | bytes 2703360 | tf_op jit(solution)/shard_map/pallas_call | solution.py:533
  11.3 0.7 %collective-permute-start.2 = (f32[128,128]{1,0:T(8,128)S(1)}, f32[128,128]{1,0:T(8,128)S(1)}, u32[]{:S(2)}, u32[]{:S(2)}) collective-permute-start(f32[128,128]{1,0:T(8,128)S(1)} %get-tuple-element.49), channel_id=1, source_target_pairs={{1,2},{2,1},{5,6},{6,5},{9,10},{10,9},{13,14},{14,13},{17,18},{18,... | collective-permute-start | bytes 196616 | tf_op jit(solution)/shard_map/ppermute | solution.py:559
  11.9 4.4 %collective-permute-start.3 = (f32[128,128]{1,0:T(8,128)S(1)}, f32[128,128]{1,0:T(8,128)S(1)}, u32[]{:S(2)}, u32[]{:S(2)}) collective-permute-start(f32[128,128]{1,0:T(8,128)S(1)} %get-tuple-element.50), channel_id=1, source_target_pairs={{0,1},{2,3},{1,0},{3,2},{4,5},{6,7},{5,4},{7,6},{8,9},{10,11},{9,8... | collective-permute-start | bytes 196616 | tf_op jit(solution)/shard_map/ppermute | solution.py:559
  16.3 0.0 copy-start.1
  16.3 0.0 copy-done
  16.3 0.7 %copy-done.1 = s32[256]{0:T(256)S(1)} copy-done((s32[256]{0:T(256)S(1)}, s32[256]{0:T(256)}, u32[]{:S(2)}) %copy-start.1) | copy-done | bytes 1048
  17.0 0.1 shard_map.149
  17.1 0.0 collective-permute-done.2.across_in
  17.1 0.1 collective-permute-done.3.inside_in
  17.2 2.2 %shard_map.150 = (f32[192,256]{1,0:T(8,128)}, f32[192,256]{1,0:T(8,128)}, f32[128,128]{1,0:T(8,128)S(1)}) custom-call(bf16[192,576]{1,0:T(8,128)(2,1)S(1)} %get-tuple-element.32.table, bf16[64,576]{1,0:T(8,128)(2,1)S(1)} %get-tuple-element.33.ends, f32[2,192,128]{2,1,0:T(8,128)S(1)} %get-tuple-element.44.end_e.e, f32[2,192,128]{2,1,0:T(8,128)S(1)} %get-tuple-element.45.h, ...), custom_call_target="tpu_custom_call" | custom-call | flops 339738624 | bytes 2662400 | tf_op jit(solution)/shard_map/pallas_call | solution.py:533
  19.4 12.8 %all_to_all.11 = f32[8,16,128]{2,1,0:T(8,128)S(1)} all-to-all(f32[8,16,128]{2,1,0:T(8,128)S(1)} %bitcast.15), channel_id=1, replica_groups=mesh['exc'=8,'space'=4] {'exc'}, dimensions={0} | all-to-all | bytes 131072 | tf_op jit(solution)/shard_map/all_to_all | solution.py:626
  32.2 0.7 %shard_map.151 = (f32[16,64]{1,0:T(8,128)}, f32[16,64]{1,0:T(8,128)}) custom-call(f32[128,128]{1,0:T(8,128)S(1)} %bitcast.14), custom_call_target="tpu_custom_call" | custom-call | bytes 73728 | tf_op jit(solution)/shard_map/pallas_call | solution.py:533
Async XLA Ops:
  3.0 5.0 %collective-permute-start = (f32[200,128]{1,0:T(8,128)S(1)}, f32[200,128]{1,0:T(8,128)S(1)}, u32[]{:S(2)}, u32[]{:S(2)}) collective-permute-start(f32[200,128]{1,0:T(8,128)S(1)} %get-tuple-element.42), channel_id=1, source_target_pairs={{1,2},{2,1},{5,6},{6,5},{9,10},{10,9},{13,14},{14,13},{17,18},{18,... | collective-permute-start | bytes 307208 | tf_op jit(solution)/shard_map/ppermute | solution.py:559
  3.7 5.3 %collective-permute-start.1 = (f32[200,128]{1,0:T(8,128)S(1)}, f32[200,128]{1,0:T(8,128)S(1)}, u32[]{:S(2)}, u32[]{:S(2)}) collective-permute-start(f32[200,128]{1,0:T(8,128)S(1)} %get-tuple-element.43), channel_id=1, source_target_pairs={{0,1},{2,3},{1,0},{3,2},{4,5},{6,7},{5,4},{7,6},{8,9},{10,11},{9,8... | collective-permute-start | bytes 307208 | tf_op jit(solution)/shard_map/ppermute | solution.py:559
  9.0 7.3 %copy-start = (bf16[1,5,192,256]{3,2,1,0:T(8,128)(2,1)S(1)}, bf16[1,5,192,256]{3,2,1,0:T(8,128)(2,1)}, u32[]{:S(2)}) copy-start(bf16[1,5,192,256]{3,2,1,0:T(8,128)(2,1)} %param.15) | copy-start | bytes 1474564
  11.3 5.8 %collective-permute-start.2 = (f32[128,128]{1,0:T(8,128)S(1)}, f32[128,128]{1,0:T(8,128)S(1)}, u32[]{:S(2)}, u32[]{:S(2)}) collective-permute-start(f32[128,128]{1,0:T(8,128)S(1)} %get-tuple-element.49), channel_id=1, source_target_pairs={{1,2},{2,1},{5,6},{6,5},{9,10},{10,9},{13,14},{14,13},{17,18},{18,... | collective-permute-start | bytes 196616 | tf_op jit(solution)/shard_map/ppermute | solution.py:559
  11.9 5.3 %collective-permute-start.3 = (f32[128,128]{1,0:T(8,128)S(1)}, f32[128,128]{1,0:T(8,128)S(1)}, u32[]{:S(2)}, u32[]{:S(2)}) collective-permute-start(f32[128,128]{1,0:T(8,128)S(1)} %get-tuple-element.50), channel_id=1, source_target_pairs={{0,1},{2,3},{1,0},{3,2},{4,5},{6,7},{5,4},{7,6},{8,9},{10,11},{9,8... | collective-permute-start | bytes 196616 | tf_op jit(solution)/shard_map/ppermute | solution.py:559
  16.3 0.7 %copy-start.1 = (s32[256]{0:T(256)S(1)}, s32[256]{0:T(256)}, u32[]{:S(2)}) copy-start(s32[256]{0:T(256)} %param.19) | copy-start | bytes 3076

commit v3 on v2

--- a/solution.py
+++ b/solution.py
@@ -213,7 +213,7 @@
     return found[:, 0:LAYER], found[:, LAYER : 2 * LAYER]
 
 
-def lonely(table, ends, x, index, fe, fh, acc, electric, drive, v):
+def lonely(table, ends, x, index, fe, fh, acc, electric, drive_of, v, before_h=lambda: None):
     own = (L0, L1)
 
     def between(target, field, scale):
@@ -227,6 +227,7 @@
 
     found = [ends_of(fe)]
     parts = own_parts(table, x, electric)
+    before_h()
     between(fh, fe, TIME_STEP)
     magnetic = []
     for i, layer in enumerate(own):
@@ -235,6 +236,7 @@
         fh[layer] = magnetic[i]
     found.append(ends_of(fh))
     parts = own_parts(table, x, magnetic)
+    drive = drive_of()
     for i, layer in enumerate(own):
         acc[layer] = drive[i]
     between(acc, fh, 1.0)
@@ -256,7 +258,7 @@
 
 
 def two_steps(
-    tables, x, index, valid, fe, fh, acc, e, h, j, source, v, w, v_near, sent_a, sent_b, when_h
+    tables, x, index, valid, fe, fh, acc, e, h, j, source, v, w, v_near, sent_a, sent_b
 ):
     table, ends = tables
     own = (L0, L1)
@@ -326,7 +328,6 @@
         lift_inside(fh, fe, layer, index, TIME_STEP)
         magnetic[i] = fh[layer] + TIME_STEP * parts[i]
         fh[layer] = magnetic[i]
-    when_h()
     for side, (near, face, _, _) in enumerate(sides):
         lift_end(fh, fe, near, at_end(face), index, TIME_STEP, False)
         for place, c in enumerate((1, 2)):
@@ -369,22 +370,28 @@
 ):
     table, ends, e, h, j, v, w, source, places, valid, across, inside = rest[:12]
     fe, fh, acc, x, neighbor, ports, profile, sems = rest[12:]
-    copies = []
+    started = []
 
     def fetch(origin, target):
-        copies.append(pltpu.make_async_copy(origin, target, sems.at[len(copies)]))
-        copies[-1].start()
-        return copies[-1]
-
-    early = [fetch(near_in, neighbor), fetch(ports_in, ports), fetch(profile_in, profile)]
-    fields = []
-    for origin, target in ((e_in, e), (h_in, h), (j_in, j), (w_in, w), (v_in, v)):
-        for i in range(2):
-            fields.append(fetch(origin.at[:, pl.ds(i * LAYER, LAYER)], target.at[i]))
-    last = [fetch(table_in, table), fetch(ends_in, ends)]
-
-    for copy in early:
-        copy.wait()
+        started.append(pltpu.make_async_copy(origin, target, sems.at[len(started)]))
+        started[-1].start()
+        return [started[-1]]
+
+    def fetch_layers(origin, target):
+        return [
+            fetch(origin.at[:, pl.ds(i * LAYER, LAYER)], target.at[i])[0] for i in range(2)
+        ]
+
+    def wait(copies):
+        for copy in copies:
+            copy.wait()
+
+    start = fetch_layers(e_in, e) + fetch(table_in, table) + fetch(near_in, neighbor)
+    second = fetch_layers(h_in, h) + fetch(ports_in, ports) + fetch(profile_in, profile)
+    third = fetch_layers(w_in, w) + fetch_layers(j_in, j) + fetch_layers(v_in, v)
+    third += fetch(ends_in, ends)
+
+    wait(start)
     found = neighbor[...]
     place = jnp.where(found < 0, 0, jnp.bitwise_and(found, LAYER - 1))
     for i in range(2):
@@ -393,29 +400,38 @@
             places[6 * i + face] = jnp.broadcast_to(place[face : face + 1, columns], (8, LAYER))
         there = (found[i : i + 1, columns] >= 0).astype(F32)
         valid[i] = jnp.broadcast_to(there, (8, LAYER))
-    count = 2 * LAYER
-    targets = lax.broadcasted_iota(jnp.int32, (count, ports.shape[1]), 0)
-    spread_hot = one_hot(targets, jnp.bitwise_and(ports[...], count - 1))
-    high, low = halves(profile[...])
-    spread = dot_t(high, spread_hot) + dot_t(low, spread_hot)
+    electric = [stored(e[i]) for i in range(2)]
     for i in range(2):
-        source[i] = stored(spread[:, i * LAYER : (i + 1) * LAYER])
-    for copy in fields:
-        copy.wait()
-    electric, drive = [], []
-    for i in range(2):
-        electric.append(stored(e[i]))
         fe[L0 + i] = electric[i]
-        fh[L0 + i] = stored(h[i])
-        weight = TIME_STEP * thrice(w[i])
-        drive.append(KEEP * stored(j[i]) + weight * electric[i] + source[i])
-    for copy in last:
-        copy.wait()
+
+    def before_h():
+        wait(second)
+        for i in range(2):
+            fh[L0 + i] = stored(h[i])
+        count = 2 * LAYER
+        targets = lax.broadcasted_iota(jnp.int32, (count, ports.shape[1]), 0)
+        spread_hot = one_hot(targets, jnp.bitwise_and(ports[...], count - 1))
+        high, low = halves(profile[...])
+        spread = dot_t(high, spread_hot) + dot_t(low, spread_hot)
+        for i in range(2):
+            source[i] = stored(spread[:, i * LAYER : (i + 1) * LAYER])
+
+    first_e = list(electric)
+
+    def drive_of():
+        wait(third)
+        drive = []
+        for i in range(2):
+            weight = TIME_STEP * thrice(w[i])
+            drive.append(KEEP * stored(j[i]) + weight * first_e[i] + source[i])
+        return drive
 
     def index(layer, face):
         return places[6 * (layer - L0) + face]
 
-    up, down = lonely(table, ends, x, index, fe, fh, acc, electric, drive, v)
+    up, down = lonely(
+        table, ends, x, index, fe, fh, acc, electric, drive_of, v, before_h
+    )
     send(across, inside, 0, up, down)
     send(across, inside, V_NEAR, v[1], v[0])
     blank = jnp.zeros((2, LAYER), F32)
@@ -453,7 +469,7 @@
     start = [[stored(field[i]) for i in range(2)] for field in (e, h, j)]
     first_e, first_j, second_e, second_j, magnetic = two_steps(
         (table, ends), x, index, valid, fe, fh, acc, *start, source, v, w, v_near,
-        sent_a, sent_b, lambda: None,
+        sent_a, sent_b,
     )
     drive = []
     for i in range(2):
@@ -464,7 +480,7 @@
         out_h[i] = magnetic[i]
         weight = TIME_STEP * thrice(w[i])
         drive.append(KEEP * second_j[i] + weight * second_e[i] + source[i])
-    up, down = lonely(table, ends, x, index, fe, fh, acc, list(second_e), drive, v)
+    up, down = lonely(table, ends, x, index, fe, fh, acc, list(second_e), lambda: drive, v)
     send(across, inside, 0, up, down)
 
 
@@ -485,23 +501,15 @@
     across_in, inside_in, levels, early, pixels, *rest
 ):
     out_e, out_h, sums = rest[:3]
-    fe, fh, acc, x, sent_a, sent_b, sems = rest[3:]
+    fe, fh, acc, x, sent_a, sent_b = rest[3:]
     sides_of(across_in, inside_in, sent_a, sent_b, SECOND)
-    copies = []
-
-    def write(field, target):
-        for i in range(2):
-            for c in range(3):
-                origin = field.at[L0 + i, pl.ds(BASE[c], NODES), :]
-                there = target.at[pl.ds(c * NODES, NODES), pl.ds(i * LAYER, LAYER)]
-                copies.append(pltpu.make_async_copy(origin, there, sems.at[len(copies)]))
-                copies[-1].start()
-
-    first_e, first_j, second_e, second_j, _ = two_steps(
+    first_e, first_j, second_e, second_j, magnetic = two_steps(
         (table, ends), x, index_of(places, near_places), valid, fe, fh, acc,
-        e, h, j, source, v, w, v_near, sent_a, sent_b, lambda: write(fh, out_h),
-    )
-    write(fe, out_e)
+        e, h, j, source, v, w, v_near, sent_a, sent_b,
+    )
+    for i in range(2):
+        out_e[i] = second_e[i]
+        out_h[i] = magnetic[i]
     parts = []
     for i in range(2):
         columns = slice(i * LAYER, (i + 1) * LAYER)
@@ -512,18 +520,31 @@
     both = jnp.concatenate(parts, axis=1)
     high, low = halves(both)
     sums[...] = dot_t(pixels[...], high) + dot_t(pixels[...], low)
-    for copy in copies:
-        copy.wait()
-
-
-def total_kernel(owners, parts, eps, drude):
+
+
+def total_kernel(owners, parts, e, h, out_e, out_h, eps, drude, sums, sems):
+    copies = []
+
+    def write(origin, target):
+        copies.append(pltpu.make_async_copy(origin, target, sems.at[len(copies)]))
+        copies[-1].start()
+
+    for field, target in ((e, out_e), (h, out_h)):
+        for i in range(2):
+            for c in range(3):
+                there = target.at[pl.ds(c * NODES, NODES), pl.ds(i * LAYER, LAYER)]
+                write(field.at[i, pl.ds(BASE[c], NODES), :], there)
     share = parts.shape[0] // owners
     total = parts[0:share]
     for owner in range(1, owners):
         total = total + parts[owner * share : (owner + 1) * share]
     total = total * (1.0 / owners)
-    eps[...] = total[:, 0:NODES]
-    drude[...] = total[:, NODES : 2 * NODES]
+    sums[0] = total[:, 0:NODES]
+    sums[1] = total[:, NODES : 2 * NODES]
+    write(sums.at[0], eps)
+    write(sums.at[1], drude)
+    for copy in copies:
+        copy.wait()
 
 
 def call(kernel, outs, args, scratch=(), flops=0, spaces=None, out_spaces=None):
@@ -613,21 +634,22 @@
         [f32(2 * NODES, count), bf16(PIX_DEV, count)],
         [e1, j1, e2, j2, levels, design_map.reshape(1, count)],
     )
-    out_e, out_h, sums = call(
+    e4, h4, sums = call(
         last_kernel,
-        [f32(ROWS, count)] * 2 + [f32(PIX_DEV, 2 * NODES)],
+        [field, field, f32(PIX_DEV, 2 * NODES)],
         [table, ends, e2, h2, j2, v, w, source, places, valid, v_near, near_places]
         + [across, inside, levels, early, pixels],
-        work + [pltpu.VMEM((SECOND, LAYER), F32)] * 2 + [pltpu.SemaphoreType.DMA((12,))],
+        work + [pltpu.VMEM((SECOND, LAYER), F32)] * 2,
         12 * once,
-        None,
-        [pltpu.HBM, pltpu.HBM, pltpu.VMEM],
     )
     parts = lax.all_to_all(sums, "exc", split_axis=0, concat_axis=0, tiled=True)
-    eps, drude = call(
+    share = PIX_DEV // owners
+    out_e, out_h, eps, drude = call(
         functools.partial(total_kernel, owners),
-        [f32(PIX_DEV // owners, NODES)] * 2,
-        [parts],
+        [f32(ROWS, count)] * 2 + [f32(share, NODES)] * 2,
+        [parts, e4, h4],
+        [pltpu.VMEM((2, share, NODES), F32), pltpu.SemaphoreType.DMA((14,))],
+        out_spaces=[pltpu.HBM] * 4,
     )
     return out_e[None], out_h[None], eps.T, drude.T
 

time: 33.1 us -> 32.7 us (0.988)
  no operation moved by 1% of the time
where the time goes in v3:
time: 32.7 us; the launch traced here: 32.5 us
  blocking collectives  12.8 us (39%)
  starting transfers between devices  10.1 us (31%)
  Pallas kernels  7.27 us (22%)
  waiting for transfers between devices  1.06 us (3%)
  between operations  0.69 us (2%)
  local copies, waits for them, and re-layouts  0.68 us (2%)
    all_to_all x1, blocking collectives, local(): parts = lax.all_to_all(sums, 'exc', split_axis=0, concat_axis=0, tiled=True)  12.8 us
    ppermute x2, starting transfers between devices, exchange(): lax.ppermute(inside, 'space', pairs(0))  8.72 us
    pallas_call x5, Pallas kernels, call(): pl.pallas_call(kernel, out_shape=outs, in_specs=[pl.BlockSpec(memory_spac...  7.27 us
    ppermute x2, starting transfers between devices, exchange(): lax.ppermute(across, 'space', pairs(1))  1.33 us
    ppermute x2, waiting for transfers between devices, exchange(): lax.ppermute(inside, 'space', pairs(0))  1.05 us
    unnamed x4, local copies, waits for them, and re-layouts  0.68 us
  transfers between devices with their start and end apart: 4, of which 2 were waited for; matrix products, arithmetic and copies ran while one was open for 0% of the time, Pallas kernels for 0%

profile of v3, /device:TPU:0, one launch (start us, length us, event | category | flops | bytes accessed | tf_op | source)
XLA Modules:
  0.0 32.5 jit_solution(5116348329648828507)
XLA Ops:
  0.6 2.5 %shard_map.147 = (bf16[192,576]{1,0:T(8,128)(2,1)S(1)}, bf16[64,576]{1,0:T(8,128)(2,1)S(1)}, f32[2,192,128]{2,1,0:T(8,128)S(1)}, f32[2,192,128]{2,1,0:T(8,128)S(...) custom-call(bf16[192,576]{1,0:T(8,128)(2,1)} %constant.4.clone.table, ...), custom_call_target="tpu_custom_call" | custom-call | flops 169869312 | bytes 2890240 | tf_op jit(solution)/shard_map/pallas_call | solution.py:554
  3.1 0.7 %collective-permute-start = (f32[200,128]{1,0:T(8,128)S(1)}, f32[200,128]{1,0:T(8,128)S(1)}, u32[]{:S(2)}, u32[]{:S(2)}) collective-permute-start(f32[200,128]{1,0:T(8,128)S(1)} %get-tuple-element.44), channel_id=1, source_target_pairs={{1,2},{2,1},{5,6},{6,5},{9,10},{10,9},{13,14},{14,13},{17,18},{18,... | collective-permute-start | bytes 307208 | tf_op jit(solution)/shard_map/ppermute | solution.py:580
  3.8 4.4 %collective-permute-start.1 = (f32[200,128]{1,0:T(8,128)S(1)}, f32[200,128]{1,0:T(8,128)S(1)}, u32[]{:S(2)}, u32[]{:S(2)}) collective-permute-start(f32[200,128]{1,0:T(8,128)S(1)} %get-tuple-element.45), channel_id=1, source_target_pairs={{0,1},{2,3},{1,0},{3,2},{4,5},{6,7},{5,4},{7,6},{8,9},{10,11},{9,8... | collective-permute-start | bytes 307208 | tf_op jit(solution)/shard_map/ppermute | solution.py:580
  8.2 0.0 collective-permute-done.across_in
  8.2 0.9 %collective-permute-done.1.inside_in = f32[200,128]{1,0:T(8,128)S(1)} collective-permute-done((f32[200,128]{1,0:T(8,128)S(1)}, f32[200,128]{1,0:T(8,128)S(1)}, u32[]{:S(2)}, u32[]{:S(2)}) %collective-permute-start.1) | collective-permute-done | bytes 102432 | tf_op jit(solution)/shard_map/ppermute | solution.py:580
  9.1 0.0 copy-start
  9.1 2.2 %shard_map.148 = (f32[2,192,128]{2,1,0:T(8,128)S(1)}, f32[2,192,128]{2,1,0:T(8,128)S(1)}, f32[2,192,128]{2,1,0:T(8,128)S(1)}, f32[2,192,128]{2,1,0:T(8,128)S(1)}...) custom-call(bf16[192,576]{1,0:T(8,128)(2,1)S(1)} %get-tuple-element., ...), custom_call_target="tpu_custom_call" | custom-call | flops 509607936 | bytes 2703360 | tf_op jit(solution)/shard_map/pallas_call | solution.py:554
  11.4 0.7 %collective-permute-start.2 = (f32[128,128]{1,0:T(8,128)S(1)}, f32[128,128]{1,0:T(8,128)S(1)}, u32[]{:S(2)}, u32[]{:S(2)}) collective-permute-start(f32[128,128]{1,0:T(8,128)S(1)} %get-tuple-element.51), channel_id=1, source_target_pairs={{1,2},{2,1},{5,6},{6,5},{9,10},{10,9},{13,14},{14,13},{17,18},{18,... | collective-permute-start | bytes 196616 | tf_op jit(solution)/shard_map/ppermute | solution.py:580
  12.0 4.4 %collective-permute-start.3 = (f32[128,128]{1,0:T(8,128)S(1)}, f32[128,128]{1,0:T(8,128)S(1)}, u32[]{:S(2)}, u32[]{:S(2)}) collective-permute-start(f32[128,128]{1,0:T(8,128)S(1)} %get-tuple-element.52), channel_id=1, source_target_pairs={{0,1},{2,3},{1,0},{3,2},{4,5},{6,7},{5,4},{7,6},{8,9},{10,11},{9,8... | collective-permute-start | bytes 196616 | tf_op jit(solution)/shard_map/ppermute | solution.py:580
  16.4 0.0 copy-start.1
  16.4 0.0 copy-done
  16.4 0.7 %copy-done.1 = s32[256]{0:T(256)S(1)} copy-done((s32[256]{0:T(256)S(1)}, s32[256]{0:T(256)}, u32[]{:S(2)}) %copy-start.1) | copy-done | bytes 1048
  17.1 0.1 shard_map.149
  17.2 0.0 collective-permute-done.2.across_in
  17.2 0.1 collective-permute-done.3.inside_in
  17.3 1.6 %shard_map.150 = (f32[2,192,128]{2,1,0:T(8,128)S(1)}, f32[2,192,128]{2,1,0:T(8,128)S(1)}, f32[128,128]{1,0:T(8,128)S(1)}) custom-call(bf16[192,576]{1,0:T(8,128)(2,1)S(1)} %get-tuple-element.34.table, bf16[64,576]{1,0:T(8,128)(2,1)S(1)} %get-tuple-element.35.ends, f32[2,192,128]{2,1,0:T(8,128)S(1)} %get-tuple-element.46.end_e.e, ...), custom_call_target="tpu_custom_call" | custom-call | flops 339738624 | bytes 2662400 | tf_op jit(solution)/shard_map/pallas_call | solution.py:554
  18.9 12.8 %all_to_all.11 = f32[8,16,128]{2,1,0:T(8,128)S(1)} all-to-all(f32[8,16,128]{2,1,0:T(8,128)S(1)} %bitcast.15), channel_id=1, replica_groups=mesh['exc'=8,'space'=4] {'exc'}, dimensions={0} | all-to-all | bytes 131072 | tf_op jit(solution)/shard_map/all_to_all | solution.py:645
  31.7 0.9 %shard_map.151 = (f32[192,256]{1,0:T(8,128)}, f32[192,256]{1,0:T(8,128)}, f32[16,64]{1,0:T(8,128)}, f32[16,64]{1,0:T(8,128)}) custom-call(f32[128,128]{1,0:T(8,128)S(1)} %bitcast.14, f32[2,192,128]{2,1,0:T(8,128)S(1)} %get-tuple-element.58.e, f32[2,192,128]{2,1,0:T(8,128)S(1)} %get-tuple-element.59.h), custom_call_target="tpu_custom_call" | custom-call | bytes 860160 | tf_op jit(solution)/shard_map/pallas_call | solution.py:554
Async XLA Ops:
  3.1 5.0 %collective-permute-start = (f32[200,128]{1,0:T(8,128)S(1)}, f32[200,128]{1,0:T(8,128)S(1)}, u32[]{:S(2)}, u32[]{:S(2)}) collective-permute-start(f32[200,128]{1,0:T(8,128)S(1)} %get-tuple-element.44), channel_id=1, source_target_pairs={{1,2},{2,1},{5,6},{6,5},{9,10},{10,9},{13,14},{14,13},{17,18},{18,... | collective-permute-start | bytes 307208 | tf_op jit(solution)/shard_map/ppermute | solution.py:580
  3.8 5.3 %collective-permute-start.1 = (f32[200,128]{1,0:T(8,128)S(1)}, f32[200,128]{1,0:T(8,128)S(1)}, u32[]{:S(2)}, u32[]{:S(2)}) collective-permute-start(f32[200,128]{1,0:T(8,128)S(1)} %get-tuple-element.45), channel_id=1, source_target_pairs={{0,1},{2,3},{1,0},{3,2},{4,5},{6,7},{5,4},{7,6},{8,9},{10,11},{9,8... | collective-permute-start | bytes 307208 | tf_op jit(solution)/shard_map/ppermute | solution.py:580
  9.1 7.3 %copy-start = (bf16[1,5,192,256]{3,2,1,0:T(8,128)(2,1)S(1)}, bf16[1,5,192,256]{3,2,1,0:T(8,128)(2,1)}, u32[]{:S(2)}) copy-start(bf16[1,5,192,256]{3,2,1,0:T(8,128)(2,1)} %param.15) | copy-start | bytes 1474564
  11.4 5.8 %collective-permute-start.2 = (f32[128,128]{1,0:T(8,128)S(1)}, f32[128,128]{1,0:T(8,128)S(1)}, u32[]{:S(2)}, u32[]{:S(2)}) collective-permute-start(f32[128,128]{1,0:T(8,128)S(1)} %get-tuple-element.51), channel_id=1, source_target_pairs={{1,2},{2,1},{5,6},{6,5},{9,10},{10,9},{13,14},{14,13},{17,18},{18,... | collective-permute-start | bytes 196616 | tf_op jit(solution)/shard_map/ppermute | solution.py:580
  12.0 5.3 %collective-permute-start.3 = (f32[128,128]{1,0:T(8,128)S(1)}, f32[128,128]{1,0:T(8,128)S(1)}, u32[]{:S(2)}, u32[]{:S(2)}) collective-permute-start(f32[128,128]{1,0:T(8,128)S(1)} %get-tuple-element.52), channel_id=1, source_target_pairs={{0,1},{2,3},{1,0},{3,2},{4,5},{6,7},{5,4},{7,6},{8,9},{10,11},{9,8... | collective-permute-start | bytes 196616 | tf_op jit(solution)/shard_map/ppermute | solution.py:580
  16.4 0.7 %copy-start.1 = (s32[256]{0:T(256)S(1)}, s32[256]{0:T(256)}, u32[]{:S(2)}) copy-start(s32[256]{0:T(256)} %param.19) | copy-start | bytes 3076

commit v4 on v3

--- a/solution.py
+++ b/solution.py
@@ -203,50 +203,61 @@
         x[0:ROWS, here] = high
         x[ROWS : 2 * ROWS, here] = low
         x[2 * ROWS : 3 * ROWS, here] = high
-    found = dot(table[...], x[...])
-    return [found[:, i * LAYER : (i + 1) * LAYER] for i in range(2)]
-
-
-def near_parts(table, a, b):
-    both = jnp.concatenate([a.astype(BF16), b.astype(BF16)], axis=1)
-    found = dot(table[:, 0:ROWS], both)
-    return found[:, 0:LAYER], found[:, LAYER : 2 * LAYER]
-
-
-def lonely(table, ends, x, index, fe, fh, acc, electric, drive_of, v, before_h=lambda: None):
-    own = (L0, L1)
-
-    def between(target, field, scale):
-        for layer, face in ((L0, 1), (L1, 0)):
-            y, z = x_traces(field, L0 + L1 - layer, face ^ 1)
-            got = [picked(t, index(layer, face)) for t in (y, z)]
-            lift_x(target, layer, face, scale, *got)
-
-    def ends_of(field):
-        return x_traces(field, L1, 1), x_traces(field, L0, 0)
-
-    found = [ends_of(fe)]
+    return layers_of(dot(table[...], x[...]))
+
+
+def rough_parts(table, values):
+    both = jnp.concatenate([value.astype(BF16) for value in values], axis=1)
+    return layers_of(dot(table[:, 0:ROWS], both))
+
+
+def layers_of(x):
+    return [x[:, at : at + LAYER] for at in range(0, x.shape[1], LAYER)]
+
+
+def lift_between(target, field, index, scale):
+    for layer, face in ((L0, 1), (L1, 0)):
+        got = [picked(t, index(layer, face)) for t in x_traces(field, L0 + L1 - layer, face ^ 1)]
+        lift_x(target, layer, face, scale, *got)
+
+
+def lone_h(table, x, index, fe, fh, electric, before=lambda: None):
     parts = own_parts(table, x, electric)
-    before_h()
-    between(fh, fe, TIME_STEP)
+    before()
+    lift_between(fh, fe, index, TIME_STEP)
     magnetic = []
-    for i, layer in enumerate(own):
+    for i, layer in enumerate((L0, L1)):
         lift_inside(fh, fe, layer, index, TIME_STEP)
         magnetic.append(fh[layer] + TIME_STEP * parts[i])
         fh[layer] = magnetic[i]
-    found.append(ends_of(fh))
+    return magnetic
+
+
+def lone_e(table, x, index, fe, fh, acc, electric, magnetic, drive_of, v):
     parts = own_parts(table, x, magnetic)
     drive = drive_of()
-    for i, layer in enumerate(own):
+    for i, layer in enumerate((L0, L1)):
         acc[layer] = drive[i]
-    between(acc, fh, 1.0)
-    for i, layer in enumerate(own):
+    lift_between(acc, fh, index, 1.0)
+    found = []
+    for i, layer in enumerate((L0, L1)):
         lift_inside(acc, fh, layer, index, 1.0)
-        electric[i] = electric[i] - TIME_STEP * thrice(v[i]) * (parts[i] + acc[layer])
-        fe[layer] = electric[i]
+        found.append(electric[i] - TIME_STEP * thrice(v[i]) * (parts[i] + acc[layer]))
+        fe[layer] = found[i]
+    return found
+
+
+def lonely(table, ends, x, index, fe, fh, acc, electric, drive_of, v, before_h=lambda: None):
+    def ends_of(field):
+        return x_traces(field, L1, 1), x_traces(field, L0, 0)
+
+    found = [ends_of(fe)]
+    magnetic = lone_h(table, x, index, fe, fh, electric, before_h)
+    found.append(ends_of(fh))
+    electric = lone_e(table, x, index, fe, fh, acc, electric, magnetic, drive_of, v)
     found.append(ends_of(fe))
     parts = own_parts(ends, x, electric)
-    for i, layer in enumerate(own):
+    for i, layer in enumerate((L0, L1)):
         face = i
         lift_end(fh, fe, layer, at_end(face), index, TIME_STEP, False)
         for place, c in enumerate((1, 2)):
@@ -254,26 +265,18 @@
             part = parts[i][32 * i + 16 * place : 32 * i + 16 * place + 16]
             fh[layer, at : at + 16, :] += TIME_STEP * part
     found.append(ends_of(fh))
-    return [jnp.concatenate(sum(traces, []), axis=0) for traces in zip(*found)]
-
-
-def two_steps(
-    tables, x, index, valid, fe, fh, acc, e, h, j, source, v, w, v_near, sent_a, sent_b
-):
+    traces = [jnp.concatenate(sum(pairs, []), axis=0) for pairs in zip(*found)]
+    return electric, magnetic, *traces
+
+
+def respond(tables, index, valid, fe, fh, acc, lone, v, w, v_near, sent_a, sent_b):
     table, ends = tables
-    own = (L0, L1)
+    start_e, lone_h1, lone_e1 = lone
+    own, wide = (L0, L1), (A1, L0, L1, B1)
     sides = ((A1, 1, L0, sent_a), (B1, 0, L1, sent_b))
-    electric = [e[0], e[1]]
-    magnetic = [h[0], h[1]]
-    for i, layer in enumerate(own):
-        fe[layer] = electric[i]
-        fh[layer] = magnetic[i]
-
-    def between(target, field, scale, start, answered=True):
-        for layer, face in ((L0, 1), (L1, 0)):
-            y, z = x_traces(field, L0 + L1 - layer, face ^ 1)
-            got = [picked(t, index(layer, face)) for t in (y, z)]
-            lift_x(target, layer, face, scale, *got)
+    blank = jnp.zeros((ROWS, LAYER), F32)
+
+    def inward(target, field, scale, start, answered=True):
         for side, (near, face, layer, sent) in enumerate(sides):
             traces = [sent[start + 16 * t : start + 16 * t + 16, :] for t in range(2)]
             if answered:
@@ -282,51 +285,39 @@
             got = [picked(t, index(layer, face ^ 1)) * mask for t in traces]
             lift_x(target, layer, face ^ 1, scale, *got)
 
-    def outward(target, field, scale):
+    def outward(target, field, alone, scale, answered=True):
         for near, face, layer, _ in sides:
-            y, z = x_traces(field, layer, face ^ 1)
-            got = [picked(t, index(near, face)) for t in (y, z)]
+            traces = x_traces(alone, layer - L0, face ^ 1)
+            if answered:
+                traces = [a + b for a, b in zip(traces, x_traces(field, layer, face ^ 1))]
+            got = [picked(t, index(near, face)) for t in traces]
             lift_x(target, near, face, scale, *got)
 
-    weight = [TIME_STEP * thrice(w[i]) for i in range(2)]
-    blank = jnp.zeros((ROWS, LAYER), F32)
-
-    parts = own_parts(table, x, electric)
-    for near, _, _, _ in sides:
-        fh[near] = blank
-        acc[near] = blank
-    outward(fh, fe, TIME_STEP)
-    between(fh, fe, TIME_STEP, E_START, False)
+    for layer in wide:
+        fh[layer] = blank
+        acc[layer] = blank
+    inward(fh, fe, TIME_STEP, E_START, False)
+    outward(fh, fe, start_e, TIME_STEP, False)
+
+    parts = rough_parts(table, [fh[layer] for layer in wide])
+    inward(acc, fh, 1.0, H_FIRST)
+    outward(acc, fh, lone_h1, 1.0)
+    scales = [v_near[0], v[0], v[1], v_near[1]]
+    first_e = []
+    for i, layer in enumerate(wide):
+        lift_end(acc, fh, layer, 3 if layer in (A1, L1) else 0, index, 1.0, True)
+        first_e.append(-TIME_STEP * thrice(scales[i]) * (parts[i] + acc[layer]))
+        fe[layer] = first_e[i]
+
+    parts = rough_parts(table, first_e[1:3])
+    near_found = rough_parts(ends, [first_e[0], first_e[3]])
+    inward(fh, fe, TIME_STEP, E_FIRST)
+    outward(fh, fe, lone_e1, TIME_STEP)
+    lift_between(fh, fe, index, TIME_STEP)
+    magnetic = []
     for i, layer in enumerate(own):
         lift_inside(fh, fe, layer, index, TIME_STEP)
-        magnetic[i] = fh[layer] + TIME_STEP * parts[i]
-        fh[layer] = magnetic[i]
-
-    first_j = [KEEP * j[i] + weight[i] * electric[i] for i in range(2)]
-    parts = own_parts(table, x, magnetic)
-    near_found = near_parts(table, fh[A1], fh[B1])
-    for i, layer in enumerate(own):
-        acc[layer] = first_j[i] + source[i]
-    between(acc, fh, 1.0, H_FIRST)
-    outward(acc, fh, 1.0)
-    for i, layer in enumerate(own):
-        lift_inside(acc, fh, layer, index, 1.0)
-        electric[i] = electric[i] - TIME_STEP * thrice(v[i]) * (parts[i] + acc[layer])
-        fe[layer] = electric[i]
-    first_e = list(electric)
-    near_e = []
-    for side, (near, face, _, _) in enumerate(sides):
-        lift_end(acc, fh, near, at_end(face), index, 1.0, True)
-        near_e.append(-TIME_STEP * thrice(v_near[side]) * (near_found[side] + acc[near]))
-        fe[near] = near_e[side]
-
-    parts = own_parts(table, x, electric)
-    near_found = near_parts(ends, *near_e)
-    between(fh, fe, TIME_STEP, E_FIRST)
-    outward(fh, fe, TIME_STEP)
-    for i, layer in enumerate(own):
-        lift_inside(fh, fe, layer, index, TIME_STEP)
-        magnetic[i] = fh[layer] + TIME_STEP * parts[i]
+        magnetic.append(fh[layer] + TIME_STEP * parts[i])
         fh[layer] = magnetic[i]
     for side, (near, face, _, _) in enumerate(sides):
         lift_end(fh, fe, near, at_end(face), index, TIME_STEP, False)
@@ -335,16 +326,18 @@
             start = 32 * face + 16 * place
             fh[near, at : at + 16, :] += TIME_STEP * near_found[side][start : start + 16]
 
-    second_j = [KEEP * first_j[i] + weight[i] * electric[i] for i in range(2)]
-    parts = own_parts(table, x, magnetic)
+    parts = rough_parts(table, magnetic)
+    current = [TIME_STEP * thrice(w[i]) * first_e[1 + i] for i in range(2)]
     for i, layer in enumerate(own):
-        acc[layer] = second_j[i] + source[i]
-    between(acc, fh, 1.0, H_SECOND)
+        acc[layer] = current[i]
+    inward(acc, fh, 1.0, H_SECOND)
+    lift_between(acc, fh, index, 1.0)
+    second_e = []
     for i, layer in enumerate(own):
         lift_inside(acc, fh, layer, index, 1.0)
-        electric[i] = electric[i] - TIME_STEP * thrice(v[i]) * (parts[i] + acc[layer])
-        fe[layer] = electric[i]
-    return first_e, first_j, electric, second_j, magnetic
+        change = TIME_STEP * thrice(v[i]) * (parts[i] + acc[layer])
+        second_e.append(first_e[1 + i] - change)
+    return first_e[1:3], magnetic, second_e, current
 
 
 def odd_rank():
@@ -368,30 +361,22 @@
 def first_kernel(
     table_in, ends_in, e_in, h_in, j_in, v_in, w_in, near_in, ports_in, profile_in, *rest
 ):
-    table, ends, e, h, j, v, w, source, places, valid, across, inside = rest[:12]
-    fe, fh, acc, x, neighbor, ports, profile, sems = rest[12:]
+    table, ends, start_e, lone_h1, lone_e1, first_j, v, w = rest[:8]
+    source, places, valid, across, inside = rest[8:13]
+    fe, fh, acc, x, neighbor, ports, profile, e, h, j, v_all, w_all, sems = rest[13:]
     started = []
 
     def fetch(origin, target):
         started.append(pltpu.make_async_copy(origin, target, sems.at[len(started)]))
         started[-1].start()
-        return [started[-1]]
-
-    def fetch_layers(origin, target):
-        return [
-            fetch(origin.at[:, pl.ds(i * LAYER, LAYER)], target.at[i])[0] for i in range(2)
-        ]
-
-    def wait(copies):
-        for copy in copies:
-            copy.wait()
-
-    start = fetch_layers(e_in, e) + fetch(table_in, table) + fetch(near_in, neighbor)
-    second = fetch_layers(h_in, h) + fetch(ports_in, ports) + fetch(profile_in, profile)
-    third = fetch_layers(w_in, w) + fetch_layers(j_in, j) + fetch_layers(v_in, v)
-    third += fetch(ends_in, ends)
-
-    wait(start)
+        return started[-1]
+
+    scatter = [fetch(near_in, neighbor), fetch(ports_in, ports), fetch(profile_in, profile)]
+    fields = [fetch(e_in, e), fetch(table_in, table), fetch(h_in, h)]
+    rest = [fetch(j_in, j), fetch(w_in, w_all), fetch(v_in, v_all), fetch(ends_in, ends)]
+
+    for copy in scatter:
+        copy.wait()
     found = neighbor[...]
     place = jnp.where(found < 0, 0, jnp.bitwise_and(found, LAYER - 1))
     for i in range(2):
@@ -400,38 +385,38 @@
             places[6 * i + face] = jnp.broadcast_to(place[face : face + 1, columns], (8, LAYER))
         there = (found[i : i + 1, columns] >= 0).astype(F32)
         valid[i] = jnp.broadcast_to(there, (8, LAYER))
-    electric = [stored(e[i]) for i in range(2)]
+    targets = lax.broadcasted_iota(jnp.int32, (2 * LAYER, ports.shape[1]), 0)
+    spread_hot = one_hot(targets, jnp.bitwise_and(ports[...], 2 * LAYER - 1))
+    high, low = halves(profile[...])
+    spread = layers_of(dot_t(high, spread_hot) + dot_t(low, spread_hot))
+    for copy in fields + rest:
+        copy.wait()
+    electric = [stored(part) for part in layers_of(e[...])]
+    magnetic = [stored(part) for part in layers_of(h[...])]
+    current = [stored(part) for part in layers_of(j[...])]
+    weight = layers_of(w_all[...])
+    scale = layers_of(v_all[...])
+    drive = []
     for i in range(2):
+        source[i] = stored(spread[i])
+        w[i] = weight[i]
+        v[i] = scale[i]
+        start_e[i] = electric[i]
         fe[L0 + i] = electric[i]
-
-    def before_h():
-        wait(second)
-        for i in range(2):
-            fh[L0 + i] = stored(h[i])
-        count = 2 * LAYER
-        targets = lax.broadcasted_iota(jnp.int32, (count, ports.shape[1]), 0)
-        spread_hot = one_hot(targets, jnp.bitwise_and(ports[...], count - 1))
-        high, low = halves(profile[...])
-        spread = dot_t(high, spread_hot) + dot_t(low, spread_hot)
-        for i in range(2):
-            source[i] = stored(spread[:, i * LAYER : (i + 1) * LAYER])
-
-    first_e = list(electric)
-
-    def drive_of():
-        wait(third)
-        drive = []
-        for i in range(2):
-            weight = TIME_STEP * thrice(w[i])
-            drive.append(KEEP * stored(j[i]) + weight * first_e[i] + source[i])
-        return drive
+        fh[L0 + i] = magnetic[i]
+        now = KEEP * current[i] + TIME_STEP * thrice(weight[i]) * electric[i]
+        first_j[i] = now
+        drive.append(now + source[i])
 
     def index(layer, face):
         return places[6 * (layer - L0) + face]
 
-    up, down = lonely(
-        table, ends, x, index, fe, fh, acc, electric, drive_of, v, before_h
-    )
+    electric, magnetic, up, down = lonely(
+        table, ends, x, index, fe, fh, acc, electric, lambda: drive, v
+    )
+    for i in range(2):
+        lone_e1[i] = electric[i]
+        lone_h1[i] = magnetic[i]
     send(across, inside, 0, up, down)
     send(across, inside, V_NEAR, v[1], v[0])
     blank = jnp.zeros((2, LAYER), F32)
@@ -445,6 +430,39 @@
     )
 
 
+def own_index(places):
+    def index(layer, face):
+        return places[6 * (layer - L0) + face]
+
+    return index
+
+
+def second_lone_step(table, lone_h1, lone_e1, first_j, v, w, source, places, work):
+    fe, fh, acc, x = work
+    index = own_index(places)
+    electric = [lone_e1[i] for i in range(2)]
+    for i in range(2):
+        fe[L0 + i] = electric[i]
+        fh[L0 + i] = lone_h1[i]
+    current = [
+        KEEP * first_j[i] + TIME_STEP * thrice(w[i]) * electric[i] for i in range(2)
+    ]
+    magnetic = lone_h(table, x, index, fe, fh, electric)
+    electric = lone_e(
+        table, x, index, fe, fh, acc, electric, magnetic,
+        lambda: [current[i] + source[i] for i in range(2)], v,
+    )
+    return magnetic, electric, current
+
+
+def lone_kernel(table, lone_h1, lone_e1, first_j, v, w, source, places, *rest):
+    lone_h2, lone_e2, lone_j2 = rest[:3]
+    found = second_lone_step(table, lone_h1, lone_e1, first_j, v, w, source, places, rest[3:])
+    for out, values in zip((lone_h2, lone_e2, lone_j2), found):
+        for i in range(2):
+            out[i] = values[i]
+
+
 def index_of(places, near_places):
     def index(layer, face):
         if layer in (L0, L1):
@@ -455,10 +473,12 @@
 
 
 def middle_kernel(
-    table, ends, e, h, j, v, w, source, places, valid, across_in, inside_in, *rest
+    table, ends, start_e, lone_h1, lone_e1, lone_h2, lone_e2, lone_j2, v, w, source,
+    places, valid, across_in, inside_in, *rest
 ):
-    out_e, out_h, out_j, mid_e, mid_j, v_near, near_places, across, inside = rest[:9]
-    fe, fh, acc, x, sent_a, sent_b = rest[9:]
+    end_e, next_h, next_e, next_j, answer_e, answer_j, v_near, near_places = rest[:8]
+    across, inside = rest[8:10]
+    fe, fh, acc, x, sent_a, sent_b = rest[10:]
     sides_of(across_in, inside_in, sent_a, sent_b, FIRST)
     for side, sent in enumerate((sent_a, sent_b)):
         v_near[side] = sent[V_NEAR : V_NEAR + NODES, :]
@@ -466,56 +486,75 @@
         for face in range(6):
             near_places[6 * side + face] = jnp.broadcast_to(place[face : face + 1], (8, LAYER))
     index = index_of(places, near_places)
-    start = [[stored(field[i]) for i in range(2)] for field in (e, h, j)]
-    first_e, first_j, second_e, second_j, magnetic = two_steps(
-        (table, ends), x, index, valid, fe, fh, acc, *start, source, v, w, v_near,
-        sent_a, sent_b,
-    )
-    drive = []
+    first_e, magnetic, second_e, current = respond(
+        (table, ends), index, valid, fe, fh, acc, (start_e, lone_h1, lone_e1),
+        v, w, v_near, sent_a, sent_b,
+    )
+    electric, drive = [], []
     for i in range(2):
-        mid_e[i] = first_e[i]
-        mid_j[i] = first_j[i]
-        out_e[i] = second_e[i]
-        out_j[i] = second_j[i]
-        out_h[i] = magnetic[i]
-        weight = TIME_STEP * thrice(w[i])
-        drive.append(KEEP * second_j[i] + weight * second_e[i] + source[i])
-    up, down = lonely(table, ends, x, index, fe, fh, acc, list(second_e), lambda: drive, v)
+        answer_e[i] = first_e[i]
+        answer_j[i] = current[i]
+        electric.append(lone_e2[i] + second_e[i])
+        end_e[i] = electric[i]
+        fe[L0 + i] = electric[i]
+        fh[L0 + i] = lone_h2[i] + magnetic[i]
+        before = lone_j2[i] + current[i]
+        now = KEEP * before + TIME_STEP * thrice(w[i]) * electric[i]
+        next_j[i] = now
+        drive.append(now + source[i])
+    electric, magnetic, up, down = lonely(
+        table, ends, x, index, fe, fh, acc, electric, lambda: drive, v
+    )
+    for i in range(2):
+        next_e[i] = electric[i]
+        next_h[i] = magnetic[i]
     send(across, inside, 0, up, down)
 
 
-def early_kernel(mid_e, mid_j, end_e, end_j, levels, design, out, pixels):
+def early_kernel(
+    table, lone_e1, answer_e, lone_j1, lone_j2, answer_j, end_e, next_h, next_e, next_j,
+    v, w, source, places, levels, design, *rest
+):
+    last_h, last_e, last_j, out, pixels = rest[:5]
     pixel = jnp.bitwise_and(design[...], PIX_DEV - 1)
     pixels[...] = one_hot(lax.broadcasted_iota(jnp.int32, pixels.shape, 0), pixel)
+    magnetic, electric, current = second_lone_step(
+        table, next_h, next_e, next_j, v, w, source, places, rest[5:]
+    )
     for i in range(2):
+        last_h[i] = magnetic[i]
+        last_e[i] = electric[i]
+        last_j[i] = current[i]
         columns = slice(i * LAYER, (i + 1) * LAYER)
-        start, middle, end = (stored(levels[k, :, columns].astype(F32)) for k in range(3))
-        out[0:NODES, columns] = folded(
-            mid_e[i] * (middle - start) + end_e[i] * (end - middle)
-        )
-        out[NODES : 2 * NODES, columns] = folded(mid_j[i] * start + end_j[i] * middle)
+        level = [stored(levels[k, :, columns].astype(F32)) for k in range(5)]
+        eps = (lone_e1[i] + answer_e[i]) * (level[1] - level[0])
+        eps += end_e[i] * (level[2] - level[1]) + next_e[i] * (level[3] - level[2])
+        eps += electric[i] * (level[4] - level[3])
+        drude = lone_j1[i] * level[0] + (lone_j2[i] + answer_j[i]) * level[1]
+        drude += next_j[i] * level[2] + current[i] * level[3]
+        out[0:NODES, columns] = folded(eps)
+        out[NODES : 2 * NODES, columns] = folded(drude)
 
 
 def last_kernel(
-    table, ends, e, h, j, v, w, source, places, valid, v_near, near_places,
-    across_in, inside_in, levels, early, pixels, *rest
+    table, ends, start_e, lone_h1, lone_e1, lone_h2, lone_e2, v, w, places, valid,
+    v_near, near_places, across_in, inside_in, levels, early, pixels, *rest
 ):
     out_e, out_h, sums = rest[:3]
-    fe, fh, acc, x, sent_a, sent_b = rest[3:]
+    fe, fh, acc, sent_a, sent_b = rest[3:]
     sides_of(across_in, inside_in, sent_a, sent_b, SECOND)
-    first_e, first_j, second_e, second_j, magnetic = two_steps(
-        (table, ends), x, index_of(places, near_places), valid, fe, fh, acc,
-        e, h, j, source, v, w, v_near, sent_a, sent_b,
-    )
-    for i in range(2):
-        out_e[i] = second_e[i]
-        out_h[i] = magnetic[i]
+    first_e, magnetic, second_e, current = respond(
+        (table, ends), index_of(places, near_places), valid, fe, fh, acc,
+        (start_e, lone_h1, lone_e1), v, w, v_near, sent_a, sent_b,
+    )
     parts = []
     for i in range(2):
+        out_e[i] = lone_e2[i] + second_e[i]
+        out_h[i] = lone_h2[i] + magnetic[i]
         columns = slice(i * LAYER, (i + 1) * LAYER)
         start, middle, end = (stored(levels[k, :, columns].astype(F32)) for k in range(2, 5))
         eps = folded(first_e[i] * (middle - start) + second_e[i] * (end - middle))
-        drude = folded(first_j[i] * start + second_j[i] * middle)
+        drude = folded(current[i] * middle)
         parts.append(jnp.concatenate([eps, drude], axis=0) + early[:, columns])
     both = jnp.concatenate(parts, axis=1)
     high, low = halves(both)
@@ -604,43 +643,50 @@
     given += [neighbor, port_elems, port_profile[0]]
     once = 2 * ROWS * 3 * ROWS * LAYER
 
-    table, ends, e, h, j, v, w, source, places, valid, across, inside = call(
+    received = [pltpu.VMEM((FIRST, LAYER), F32)] * 2
+    table, ends, start_e, h1, e1, j1, v, w, source, places, valid, across, inside = call(
         first_kernel,
-        [bf16(*table.shape), bf16(*ends.shape), field, field, field, nodal, nodal]
-        + [field, indices, f32(2, 8, LAYER)]
+        [bf16(*table.shape), bf16(*ends.shape)]
+        + [field] * 4
+        + [nodal, nodal, field, indices, f32(2, 8, LAYER)]
         + [f32(FIRST, LAYER)] * 2,
         [pltpu.with_memory_space_constraint(a, pltpu.HBM) for a in given],
         work
-        + [
-            pltpu.VMEM(neighbor.shape, jnp.int32),
-            pltpu.VMEM(port_elems.shape, jnp.int32),
-            pltpu.VMEM(port_profile.shape[1:], F32),
-            pltpu.SemaphoreType.DMA((15,)),
-        ],
+        + [pltpu.VMEM(a.shape, a.dtype) for a in [neighbor, port_elems, port_profile[0]]]
+        + [pltpu.VMEM((ROWS, count), F32)] * 3
+        + [pltpu.VMEM((NODES, count), F32)] * 2
+        + [pltpu.SemaphoreType.DMA((10,))],
         6 * once,
         [pltpu.HBM] * len(given),
     )
     across, inside = exchange(across, inside)
-    e2, h2, j2, e1, j1, v_near, near_places, across, inside = call(
+    h2, e2, j2 = call(
+        lone_kernel, [field] * 3, [table, h1, e1, j1, v, w, source, places], work, 4 * once
+    )
+    end_e, h3, e3, j3, answer_e, answer_j, v_near, near_places, across, inside = call(
         middle_kernel,
-        [field] * 5 + [nodal, indices] + [f32(SECOND, LAYER)] * 2,
-        [table, ends, e, h, j, v, w, source, places, valid, across, inside],
-        work + [pltpu.VMEM((FIRST, LAYER), F32)] * 2,
-        18 * once,
+        [field] * 6 + [nodal, indices] + [f32(SECOND, LAYER)] * 2,
+        [table, ends, start_e, h1, e1, h2, e2, j2, v, w, source]
+        + [places, valid, across, inside],
+        work + received,
+        10 * once,
     )
     across, inside = exchange(across, inside)
-    early, pixels = call(
+    h4, e4, _, early, pixels = call(
         early_kernel,
-        [f32(2 * NODES, count), bf16(PIX_DEV, count)],
-        [e1, j1, e2, j2, levels, design_map.reshape(1, count)],
+        [field] * 3 + [f32(2 * NODES, count), bf16(PIX_DEV, count)],
+        [table, e1, answer_e, j1, j2, answer_j, end_e, h3, e3, j3, v, w, source, places]
+        + [levels, design_map.reshape(1, count)],
+        work,
+        4 * once,
     )
     e4, h4, sums = call(
         last_kernel,
         [field, field, f32(PIX_DEV, 2 * NODES)],
-        [table, ends, e2, h2, j2, v, w, source, places, valid, v_near, near_places]
+        [table, ends, end_e, h3, e3, h4, e4, v, w, places, valid, v_near, near_places]
         + [across, inside, levels, early, pixels],
-        work + [pltpu.VMEM((SECOND, LAYER), F32)] * 2,
-        12 * once,
+        work[:3] + [pltpu.VMEM((SECOND, LAYER), F32)] * 2,
+        4 * once,
     )
     parts = lax.all_to_all(sums, "exc", split_axis=0, concat_axis=0, tiled=True)
     share = PIX_DEV // owners

time: 32.7 us -> 32.4 us (level)
  waiting for transfers between devices: 1.06 us -> 0.22 us
  Pallas kernels: 7.27 us -> 7.96 us
    ppermute x2, waiting for transfers between devices: 1.05 us -> 0.22 us  [exchange(): lax.ppermute(inside, 'space', pairs(0))]
    pallas_call x5 -> x6, Pallas kernels: 7.27 us -> 7.96 us  [call(): pl.pallas_call(kernel, out_shape=outs, in_specs=[pl.BlockSpec(memory_spac...]
  transfers between devices with their start and end apart: 4 -> 4, of which waited for: 2 -> 1; matrix products, arithmetic and copies ran while one was open for 0% -> 0% of each run, Pallas kernels for 0% -> 6%
where the time goes in v4:
time: 32.4 us; the launch traced here: 32.1 us
  blocking collectives  12.5 us (39%)
  starting transfers between devices  10.1 us (31%)
  Pallas kernels  7.96 us (25%)
  between operations  0.69 us (2%)
  local copies, waits for them, and re-layouts  0.68 us (2%)
    all_to_all x1, blocking collectives, local(): parts = lax.all_to_all(sums, 'exc', split_axis=0, concat_axis=0, tiled=True)  12.5 us
    ppermute x2, starting transfers between devices, exchange(): lax.ppermute(inside, 'space', pairs(0))  8.72 us
    pallas_call x6, Pallas kernels, call(): pl.pallas_call(kernel, out_shape=outs, in_specs=[pl.BlockSpec(memory_spac...  7.96 us
    ppermute x2, starting transfers between devices, exchange(): lax.ppermute(across, 'space', pairs(1))  1.33 us
    unnamed x4, local copies, waits for them, and re-layouts  0.68 us
  transfers between devices with their start and end apart: 4, of which 1 were waited for; matrix products, arithmetic and copies ran while one was open for 0% of the time, Pallas kernels for 6%

profile of v4, /device:TPU:0, one launch (start us, length us, event | category | flops | bytes accessed | tf_op | source)
XLA Modules:
  0.0 32.1 jit_solution(14261174187795776892)
XLA Ops:
  0.6 2.4 %shard_map.147 = (bf16[192,576]{1,0:T(8,128)(2,1)S(1)}, bf16[64,576]{1,0:T(8,128)(2,1)S(1)}, f32[2,192,128]{2,1,0:T(8,128)S(1)}, f32[2,192,128]{2,1,0:T(8,128)S(...) custom-call(bf16[192,576]{1,0:T(8,128)(2,1)} %constant.4.clone.table, ...), custom_call_target="tpu_custom_call" | custom-call | flops 169869312 | bytes 3086848 | tf_op jit(solution)/shard_map/pallas_call | solution.py:593
  3.1 0.7 %collective-permute-start = (f32[200,128]{1,0:T(8,128)S(1)}, f32[200,128]{1,0:T(8,128)S(1)}, u32[]{:S(2)}, u32[]{:S(2)}) collective-permute-start(f32[200,128]{1,0:T(8,128)S(1)} %get-tuple-element.55), channel_id=1, source_target_pairs={{1,2},{2,1},{5,6},{6,5},{9,10},{10,9},{13,14},{14,13},{17,18},{18,... | collective-permute-start | bytes 307208 | tf_op jit(solution)/shard_map/ppermute | solution.py:619
  3.7 4.4 %collective-permute-start.1 = (f32[200,128]{1,0:T(8,128)S(1)}, f32[200,128]{1,0:T(8,128)S(1)}, u32[]{:S(2)}, u32[]{:S(2)}) collective-permute-start(f32[200,128]{1,0:T(8,128)S(1)} %get-tuple-element.56), channel_id=1, source_target_pairs={{0,1},{2,3},{1,0},{3,2},{4,5},{6,7},{5,4},{7,6},{8,9},{10,11},{9,8... | collective-permute-start | bytes 307208 | tf_op jit(solution)/shard_map/ppermute | solution.py:619
  8.1 0.7 %shard_map.148 = (f32[2,192,128]{2,1,0:T(8,128)S(1)}, f32[2,192,128]{2,1,0:T(8,128)S(1)}, f32[2,192,128]{2,1,0:T(8,128)S(1)}) custom-call(bf16[192,576]{1,0:T(8,128)(2,1)S(1)} %get-tuple-element.41.table, f32[2,192,128]{2,1,0:T(8,128)S(1)} %get-tuple-element.44.lone_h1, f32[2,192,128]{2,1,0:T(8,128)S(1)} %get-tuple-element.45.lone_e1, ...), custom_call_target="tpu_custom_call" | custom-call | flops 113246208 | bytes 1777664 | tf_op jit(solution)/shard_map/pallas_call | solution.py:593
  8.8 0.0 collective-permute-done.across_in
  8.8 0.2 collective-permute-done.1.inside_in
  9.0 0.0 copy-start
  9.0 1.8 %shard_map.149 = (f32[2,192,128]{2,1,0:T(8,128)S(1)}, f32[2,192,128]{2,1,0:T(8,128)S(1)}, f32[2,192,128]{2,1,0:T(8,128)S(1)}, f32[2,192,128]{2,1,0:T(8,128)S(1)}...) custom-call(bf16[192,576]{1,0:T(8,128)(2,1)S(1)} %get-tuple-element., ...), custom_call_target="tpu_custom_call" | custom-call | flops 283115520 | bytes 3489792 | tf_op jit(solution)/shard_map/pallas_call | solution.py:593
  10.8 0.7 %collective-permute-start.2 = (f32[128,128]{1,0:T(8,128)S(1)}, f32[128,128]{1,0:T(8,128)S(1)}, u32[]{:S(2)}, u32[]{:S(2)}) collective-permute-start(f32[128,128]{1,0:T(8,128)S(1)} %get-tuple-element.67), channel_id=1, source_target_pairs={{1,2},{2,1},{5,6},{6,5},{9,10},{10,9},{13,14},{14,13},{17,18},{18,... | collective-permute-start | bytes 196616 | tf_op jit(solution)/shard_map/ppermute | solution.py:619
  11.5 4.4 %collective-permute-start.3 = (f32[128,128]{1,0:T(8,128)S(1)}, f32[128,128]{1,0:T(8,128)S(1)}, u32[]{:S(2)}, u32[]{:S(2)}) collective-permute-start(f32[128,128]{1,0:T(8,128)S(1)} %get-tuple-element.68), channel_id=1, source_target_pairs={{0,1},{2,3},{1,0},{3,2},{4,5},{6,7},{5,4},{7,6},{8,9},{10,11},{9,8... | collective-permute-start | bytes 196616 | tf_op jit(solution)/shard_map/ppermute | solution.py:619
  15.8 0.0 copy-start.1
  15.8 0.0 copy-done
  15.8 0.7 %copy-done.1 = s32[256]{0:T(256)S(1)} copy-done((s32[256]{0:T(256)S(1)}, s32[256]{0:T(256)}, u32[]{:S(2)}) %copy-start.1) | copy-done | bytes 1048
  16.5 1.1 %shard_map.150 = (f32[2,192,128]{2,1,0:T(8,128)S(1)}, f32[2,192,128]{2,1,0:T(8,128)S(1)}, f32[2,192,128]{2,1,0:T(8,128)}, f32[128,256]{1,0:T(8,128)S(1)}, bf16[128,256]{1,0:T(8,128)(2,1)S(1)}) custom-call(bf16[192,576]{1,0:T(8,128)(2,1)S(1)} %get-tuple-element.41.table, f32[2,192,128]{2,1,0:T(8,128)S(1)} %get-tuple-element.45.lone_e1, ...), custom_call_target="tpu_custom_call" | custom-call | flops 113246208 | bytes 3712000 | tf_op jit(solution)/shard_map/pallas_call | solution.py:593
  17.7 0.0 collective-permute-done.2.across_in
  17.7 0.0 collective-permute-done.3.inside_in
  17.7 1.1 %shard_map.151 = (f32[2,192,128]{2,1,0:T(8,128)S(1)}, f32[2,192,128]{2,1,0:T(8,128)S(1)}, f32[128,128]{1,0:T(8,128)S(1)}) custom-call(bf16[192,576]{1,0:T(8,128)(2,1)S(1)} %get-tuple-element.41.table, bf16[64,576]{1,0:T(8,128)(2,1)S(1)} %get-tuple-element.42.ends, f32[2,192,128]{2,1,0:T(8,128)S(1)} %get-tuple-element.57.end_e.start_e, ...), custom_call_target="tpu_custom_call" | custom-call | flops 113246208 | bytes 2859008 | tf_op jit(solution)/shard_map/pallas_call | solution.py:593
  18.7 12.5 %all_to_all.11 = f32[8,16,128]{2,1,0:T(8,128)S(1)} all-to-all(f32[8,16,128]{2,1,0:T(8,128)S(1)} %bitcast.15), channel_id=1, replica_groups=mesh['exc'=8,'space'=4] {'exc'}, dimensions={0} | all-to-all | bytes 131072 | tf_op jit(solution)/shard_map/all_to_all | solution.py:691
  31.3 0.9 %shard_map.152 = (f32[192,256]{1,0:T(8,128)}, f32[192,256]{1,0:T(8,128)}, f32[16,64]{1,0:T(8,128)}, f32[16,64]{1,0:T(8,128)}) custom-call(f32[128,128]{1,0:T(8,128)S(1)} %bitcast.14, f32[2,192,128]{2,1,0:T(8,128)S(1)} %get-tuple-element.72.e, f32[2,192,128]{2,1,0:T(8,128)S(1)} %get-tuple-element.73.h), custom_call_target="tpu_custom_call" | custom-call | bytes 860160 | tf_op jit(solution)/shard_map/pallas_call | solution.py:593
Async XLA Ops:
  3.1 5.8 %collective-permute-start = (f32[200,128]{1,0:T(8,128)S(1)}, f32[200,128]{1,0:T(8,128)S(1)}, u32[]{:S(2)}, u32[]{:S(2)}) collective-permute-start(f32[200,128]{1,0:T(8,128)S(1)} %get-tuple-element.55), channel_id=1, source_target_pairs={{1,2},{2,1},{5,6},{6,5},{9,10},{10,9},{13,14},{14,13},{17,18},{18,... | collective-permute-start | bytes 307208 | tf_op jit(solution)/shard_map/ppermute | solution.py:619
  3.7 5.3 %collective-permute-start.1 = (f32[200,128]{1,0:T(8,128)S(1)}, f32[200,128]{1,0:T(8,128)S(1)}, u32[]{:S(2)}, u32[]{:S(2)}) collective-permute-start(f32[200,128]{1,0:T(8,128)S(1)} %get-tuple-element.56), channel_id=1, source_target_pairs={{0,1},{2,3},{1,0},{3,2},{4,5},{6,7},{5,4},{7,6},{8,9},{10,11},{9,8... | collective-permute-start | bytes 307208 | tf_op jit(solution)/shard_map/ppermute | solution.py:619
  9.0 6.8 %copy-start = (bf16[1,5,192,256]{3,2,1,0:T(8,128)(2,1)S(1)}, bf16[1,5,192,256]{3,2,1,0:T(8,128)(2,1)}, u32[]{:S(2)}) copy-start(bf16[1,5,192,256]{3,2,1,0:T(8,128)(2,1)} %param.15) | copy-start | bytes 1474564
  10.8 6.9 %collective-permute-start.2 = (f32[128,128]{1,0:T(8,128)S(1)}, f32[128,128]{1,0:T(8,128)S(1)}, u32[]{:S(2)}, u32[]{:S(2)}) collective-permute-start(f32[128,128]{1,0:T(8,128)S(1)} %get-tuple-element.67), channel_id=1, source_target_pairs={{1,2},{2,1},{5,6},{6,5},{9,10},{10,9},{13,14},{14,13},{17,18},{18,... | collective-permute-start | bytes 196616 | tf_op jit(solution)/shard_map/ppermute | solution.py:619
  11.5 6.2 %collective-permute-start.3 = (f32[128,128]{1,0:T(8,128)S(1)}, f32[128,128]{1,0:T(8,128)S(1)}, u32[]{:S(2)}, u32[]{:S(2)}) collective-permute-start(f32[128,128]{1,0:T(8,128)S(1)} %get-tuple-element.68), channel_id=1, source_target_pairs={{0,1},{2,3},{1,0},{3,2},{4,5},{6,7},{5,4},{7,6},{8,9},{10,11},{9,8... | collective-permute-start | bytes 196616 | tf_op jit(solution)/shard_map/ppermute | solution.py:619
  15.8 0.7 %copy-start.1 = (s32[256]{0:T(256)S(1)}, s32[256]{0:T(256)}, u32[]{:S(2)}) copy-start(s32[256]{0:T(256)} %param.19) | copy-start | bytes 3076

commit v5 on v4

--- a/solution.py
+++ b/solution.py
@@ -94,8 +94,11 @@
     high = own.astype(ml_dtypes.bfloat16)
     low = (own - high.astype(np.float64)).astype(ml_dtypes.bfloat16)
     table = np.concatenate([high, high, low], axis=1)
-    ends = [table[BASE[c] + 16 * i : BASE[c] + 16 * i + 16] for i in (0, 3) for c in (1, 2)]
-    return table, np.concatenate(ends, axis=0)
+    rows = [
+        np.concatenate([BASE[c] + 16 * i + np.arange(16) for c in (1, 2)]) for i in (0, 3)
+    ]
+    edges = [part[:, r] for r in rows for part in (high, high, low)]
+    return table, table[np.concatenate(rows)], np.concatenate(edges, axis=1)
 
 
 def halves(x):
@@ -211,6 +214,17 @@
     return layers_of(dot(table[:, 0:ROWS], both))
 
 
+def edge_parts(edges, x, values):
+    nothing = jnp.zeros((96, LAYER), BF16)
+    for at, (side, value) in enumerate(values):
+        here = slice(at * LAYER, (at + 1) * LAYER)
+        high, low = halves(value)
+        both = jnp.concatenate([high, low, high], axis=0)
+        x[96 * side : 96 * side + 96, here] = both
+        x[96 - 96 * side : 192 - 96 * side, here] = nothing
+    return layers_of(dot(edges[...], x[...]))
+
+
 def layers_of(x):
     return [x[:, at : at + LAYER] for at in range(0, x.shape[1], LAYER)]
 
@@ -269,8 +283,8 @@
     return electric, magnetic, *traces
 
 
-def respond(tables, index, valid, fe, fh, acc, lone, v, w, v_near, sent_a, sent_b):
-    table, ends = tables
+def respond(tables, x, index, valid, fe, fh, acc, lone, v, w, v_near, sent_a, sent_b):
+    table, ends, edges = tables
     start_e, lone_h1, lone_e1 = lone
     own, wide = (L0, L1), (A1, L0, L1, B1)
     sides = ((A1, 1, L0, sent_a), (B1, 0, L1, sent_b))
@@ -299,7 +313,11 @@
     inward(fh, fe, TIME_STEP, E_START, False)
     outward(fh, fe, start_e, TIME_STEP, False)
 
-    parts = rough_parts(table, [fh[layer] for layer in wide])
+    edge = []
+    for layer in wide:
+        side = 1 if layer in (A1, L1) else 0
+        edge.append((side, jnp.concatenate(x_traces(fh, layer, side), axis=0)))
+    parts = edge_parts(edges, x, edge)
     inward(acc, fh, 1.0, H_FIRST)
     outward(acc, fh, lone_h1, 1.0)
     scales = [v_near[0], v[0], v[1], v_near[1]]
@@ -359,11 +377,12 @@
 
 
 def first_kernel(
-    table_in, ends_in, e_in, h_in, j_in, v_in, w_in, near_in, ports_in, profile_in, *rest
+    table_in, ends_in, edges_in, e_in, h_in, j_in, v_in, w_in, near_in, ports_in, profile_in,
+    design_in, *rest
 ):
-    table, ends, start_e, lone_h1, lone_e1, first_j, v, w = rest[:8]
-    source, places, valid, across, inside = rest[8:13]
-    fe, fh, acc, x, neighbor, ports, profile, e, h, j, v_all, w_all, sems = rest[13:]
+    table, ends, edges, design, start_e, lone_h1, lone_e1, first_j, v, w = rest[:10]
+    source, places, valid, across, inside = rest[10:15]
+    fe, fh, acc, x, neighbor, ports, profile, e, h, j, v_all, w_all, sems = rest[15:]
     started = []
 
     def fetch(origin, target):
@@ -374,6 +393,7 @@
     scatter = [fetch(near_in, neighbor), fetch(ports_in, ports), fetch(profile_in, profile)]
     fields = [fetch(e_in, e), fetch(table_in, table), fetch(h_in, h)]
     rest = [fetch(j_in, j), fetch(w_in, w_all), fetch(v_in, v_all), fetch(ends_in, ends)]
+    later = [fetch(edges_in, edges), fetch(design_in, design)]
 
     for copy in scatter:
         copy.wait()
@@ -417,6 +437,8 @@
     for i in range(2):
         lone_e1[i] = electric[i]
         lone_h1[i] = magnetic[i]
+    for copy in later:
+        copy.wait()
     send(across, inside, 0, up, down)
     send(across, inside, V_NEAR, v[1], v[0])
     blank = jnp.zeros((2, LAYER), F32)
@@ -455,9 +477,11 @@
     return magnetic, electric, current
 
 
-def lone_kernel(table, lone_h1, lone_e1, first_j, v, w, source, places, *rest):
-    lone_h2, lone_e2, lone_j2 = rest[:3]
-    found = second_lone_step(table, lone_h1, lone_e1, first_j, v, w, source, places, rest[3:])
+def lone_kernel(table, lone_h1, lone_e1, first_j, v, w, source, places, design, *rest):
+    lone_h2, lone_e2, lone_j2, pixels = rest[:4]
+    pixel = jnp.bitwise_and(design[...], PIX_DEV - 1)
+    pixels[...] = one_hot(lax.broadcasted_iota(jnp.int32, pixels.shape, 0), pixel)
+    found = second_lone_step(table, lone_h1, lone_e1, first_j, v, w, source, places, rest[4:])
     for out, values in zip((lone_h2, lone_e2, lone_j2), found):
         for i in range(2):
             out[i] = values[i]
@@ -473,12 +497,12 @@
 
 
 def middle_kernel(
-    table, ends, start_e, lone_h1, lone_e1, lone_h2, lone_e2, lone_j2, v, w, source,
+    table, ends, edges, start_e, lone_h1, lone_e1, lone_h2, lone_e2, lone_j2, v, w, source,
     places, valid, across_in, inside_in, *rest
 ):
     end_e, next_h, next_e, next_j, answer_e, answer_j, v_near, near_places = rest[:8]
     across, inside = rest[8:10]
-    fe, fh, acc, x, sent_a, sent_b = rest[10:]
+    fe, fh, acc, x, y, sent_a, sent_b = rest[10:]
     sides_of(across_in, inside_in, sent_a, sent_b, FIRST)
     for side, sent in enumerate((sent_a, sent_b)):
         v_near[side] = sent[V_NEAR : V_NEAR + NODES, :]
@@ -487,7 +511,7 @@
             near_places[6 * side + face] = jnp.broadcast_to(place[face : face + 1], (8, LAYER))
     index = index_of(places, near_places)
     first_e, magnetic, second_e, current = respond(
-        (table, ends), index, valid, fe, fh, acc, (start_e, lone_h1, lone_e1),
+        (table, ends, edges), y, index, valid, fe, fh, acc, (start_e, lone_h1, lone_e1),
         v, w, v_near, sent_a, sent_b,
     )
     electric, drive = [], []
@@ -513,18 +537,15 @@
 
 def early_kernel(
     table, lone_e1, answer_e, lone_j1, lone_j2, answer_j, end_e, next_h, next_e, next_j,
-    v, w, source, places, levels, design, *rest
+    v, w, source, places, levels, *rest
 ):
-    last_h, last_e, last_j, out, pixels = rest[:5]
-    pixel = jnp.bitwise_and(design[...], PIX_DEV - 1)
-    pixels[...] = one_hot(lax.broadcasted_iota(jnp.int32, pixels.shape, 0), pixel)
+    last_h, last_e, out = rest[:3]
     magnetic, electric, current = second_lone_step(
-        table, next_h, next_e, next_j, v, w, source, places, rest[5:]
+        table, next_h, next_e, next_j, v, w, source, places, rest[3:]
     )
     for i in range(2):
         last_h[i] = magnetic[i]
         last_e[i] = electric[i]
-        last_j[i] = current[i]
         columns = slice(i * LAYER, (i + 1) * LAYER)
         level = [stored(levels[k, :, columns].astype(F32)) for k in range(5)]
         eps = (lone_e1[i] + answer_e[i]) * (level[1] - level[0])
@@ -537,14 +558,14 @@
 
 
 def last_kernel(
-    table, ends, start_e, lone_h1, lone_e1, lone_h2, lone_e2, v, w, places, valid,
+    table, ends, edges, start_e, lone_h1, lone_e1, lone_h2, lone_e2, v, w, places, valid,
     v_near, near_places, across_in, inside_in, levels, early, pixels, *rest
 ):
     out_e, out_h, sums = rest[:3]
-    fe, fh, acc, sent_a, sent_b = rest[3:]
+    fe, fh, acc, y, sent_a, sent_b = rest[3:]
     sides_of(across_in, inside_in, sent_a, sent_b, SECOND)
     first_e, magnetic, second_e, current = respond(
-        (table, ends), index_of(places, near_places), valid, fe, fh, acc,
+        (table, ends, edges), y, index_of(places, near_places), valid, fe, fh, acc,
         (start_e, lone_h1, lone_e1), v, w, v_near, sent_a, sent_b,
     )
     parts = []
@@ -633,20 +654,22 @@
 ):
     count = adj_e.shape[2]
     owners = lax.axis_size("exc")
-    table, ends = (jnp.asarray(t) for t in step_tables())
+    table, ends, edges = (jnp.asarray(t) for t in step_tables())
     levels = fwd_e[0]
     field, nodal = f32(2, ROWS, LAYER), f32(2, NODES, LAYER)
     indices = jax.ShapeDtypeStruct((12, 8, LAYER), jnp.int32)
     work = [pltpu.VMEM((4, ROWS, LAYER), F32)] * 3
     work += [pltpu.VMEM((3 * ROWS, 2 * LAYER), BF16)]
-    given = [table, ends, adj_e[0], adj_h[0], adj_j[0], inv_eps, drude_weight]
-    given += [neighbor, port_elems, port_profile[0]]
+    given = [table, ends, edges, adj_e[0], adj_h[0], adj_j[0], inv_eps, drude_weight]
+    given += [neighbor, port_elems, port_profile[0], design_map.reshape(1, count)]
+    edge_work = [pltpu.VMEM((ROWS, 4 * LAYER), BF16)]
     once = 2 * ROWS * 3 * ROWS * LAYER
 
     received = [pltpu.VMEM((FIRST, LAYER), F32)] * 2
-    table, ends, start_e, h1, e1, j1, v, w, source, places, valid, across, inside = call(
+    table, ends, edges, design, start_e, h1, e1, j1, v, w, source, places, valid, *sent = call(
         first_kernel,
-        [bf16(*table.shape), bf16(*ends.shape)]
+        [bf16(*table.shape), bf16(*ends.shape), bf16(*edges.shape)]
+        + [jax.ShapeDtypeStruct((1, count), jnp.int32)]
         + [field] * 4
         + [nodal, nodal, field, indices, f32(2, 8, LAYER)]
         + [f32(FIRST, LAYER)] * 2,
@@ -655,37 +678,41 @@
         + [pltpu.VMEM(a.shape, a.dtype) for a in [neighbor, port_elems, port_profile[0]]]
         + [pltpu.VMEM((ROWS, count), F32)] * 3
         + [pltpu.VMEM((NODES, count), F32)] * 2
-        + [pltpu.SemaphoreType.DMA((10,))],
+        + [pltpu.SemaphoreType.DMA((12,))],
         6 * once,
         [pltpu.HBM] * len(given),
     )
-    across, inside = exchange(across, inside)
-    h2, e2, j2 = call(
-        lone_kernel, [field] * 3, [table, h1, e1, j1, v, w, source, places], work, 4 * once
+    across, inside = exchange(*sent)
+    h2, e2, j2, pixels = call(
+        lone_kernel,
+        [field] * 3 + [bf16(PIX_DEV, count)],
+        [table, h1, e1, j1, v, w, source, places, design],
+        work,
+        4 * once,
     )
     end_e, h3, e3, j3, answer_e, answer_j, v_near, near_places, across, inside = call(
         middle_kernel,
         [field] * 6 + [nodal, indices] + [f32(SECOND, LAYER)] * 2,
-        [table, ends, start_e, h1, e1, h2, e2, j2, v, w, source]
+        [table, ends, edges, start_e, h1, e1, h2, e2, j2, v, w, source]
         + [places, valid, across, inside],
-        work + received,
+        work + edge_work + received,
         10 * once,
     )
     across, inside = exchange(across, inside)
-    h4, e4, _, early, pixels = call(
+    h4, e4, early = call(
         early_kernel,
-        [field] * 3 + [f32(2 * NODES, count), bf16(PIX_DEV, count)],
+        [field] * 2 + [f32(2 * NODES, count)],
         [table, e1, answer_e, j1, j2, answer_j, end_e, h3, e3, j3, v, w, source, places]
-        + [levels, design_map.reshape(1, count)],
+        + [levels],
         work,
         4 * once,
     )
     e4, h4, sums = call(
         last_kernel,
         [field, field, f32(PIX_DEV, 2 * NODES)],
-        [table, ends, end_e, h3, e3, h4, e4, v, w, places, valid, v_near, near_places]
+        [table, ends, edges, end_e, h3, e3, h4, e4, v, w, places, valid, v_near, near_places]
         + [across, inside, levels, early, pixels],
-        work[:3] + [pltpu.VMEM((SECOND, LAYER), F32)] * 2,
+        work[:3] + edge_work + [pltpu.VMEM((SECOND, LAYER), F32)] * 2,
         4 * once,
     )
     parts = lax.all_to_all(sums, "exc", split_axis=0, concat_axis=0, tiled=True)

time: 32.4 us -> 31.7 us (0.978)
  local copies, waits for them, and re-layouts: 0.68 us -> 0.01 us
  Pallas kernels: 7.96 us -> 7.58 us
    unnamed x4 -> x2, local copies, waits for them, and re-layouts: 0.68 us -> 0.01 us
    pallas_call x6, Pallas kernels: 7.96 us -> 7.58 us  [call(): pl.pallas_call(kernel, out_shape=outs, in_specs=[pl.BlockSpec(memory_spac...]
  transfers between devices with their start and end apart: 4 -> 4, of which waited for: 1 -> 2; matrix products, arithmetic and copies ran while one was open for 0% -> 0% of each run, Pallas kernels for 6% -> 5%
where the time goes in v5:
time: 31.7 us; the launch traced here: 31.5 us
  blocking collectives  12.8 us (40%)
  starting transfers between devices  10.1 us (32%)
  Pallas kernels  7.58 us (24%)
  between operations  0.71 us (2%)
  waiting for transfers between devices  0.35 us (1%)
    all_to_all x1, blocking collectives, local(): parts = lax.all_to_all(sums, 'exc', split_axis=0, concat_axis=0, tiled=True)  12.8 us
    ppermute x2, starting transfers between devices, exchange(): lax.ppermute(inside, 'space', pairs(0))  8.72 us
    pallas_call x6, Pallas kernels, call(): pl.pallas_call(kernel, out_shape=outs, in_specs=[pl.BlockSpec(memory_spac...  7.58 us
    ppermute x2, starting transfers between devices, exchange(): lax.ppermute(across, 'space', pairs(1))  1.33 us
  transfers between devices with their start and end apart: 4, of which 2 were waited for; matrix products, arithmetic and copies ran while one was open for 0% of the time, Pallas kernels for 5%

profile of v5, /device:TPU:0, one launch (start us, length us, event | category | flops | bytes accessed | tf_op | source)
XLA Modules:
  0.0 31.5 jit_solution(12326126189984497031)
XLA Ops:
  0.6 2.4 %shard_map.156 = (bf16[192,576]{1,0:T(8,128)(2,1)S(1)}, bf16[64,576]{1,0:T(8,128)(2,1)S(1)}, bf16[192,192]{1,0:T(8,128)(2,1)S(1)}, s32[1,256]{1,0:T(1,128)S(1)},...) custom-call(bf16[192,576]{1,0:T(8,128)(2,1)} %constant.6.clone.table, ...), custom_call_target="tpu_custom_call" | custom-call | flops 169869312 | bytes 3310080 | tf_op jit(solution)/shard_map/pallas_call | solution.py:614
  3.1 0.7 %collective-permute-start = (f32[200,128]{1,0:T(8,128)S(1)}, f32[200,128]{1,0:T(8,128)S(1)}, u32[]{:S(2)}, u32[]{:S(2)}) collective-permute-start(f32[200,128]{1,0:T(8,128)S(1)} %get-tuple-element.59), channel_id=1, source_target_pairs={{1,2},{2,1},{5,6},{6,5},{9,10},{10,9},{13,14},{14,13},{17,18},{18,... | collective-permute-start | bytes 307208 | tf_op jit(solution)/shard_map/ppermute | solution.py:640
  3.8 4.4 %collective-permute-start.1 = (f32[200,128]{1,0:T(8,128)S(1)}, f32[200,128]{1,0:T(8,128)S(1)}, u32[]{:S(2)}, u32[]{:S(2)}) collective-permute-start(f32[200,128]{1,0:T(8,128)S(1)} %get-tuple-element.60), channel_id=1, source_target_pairs={{0,1},{2,3},{1,0},{3,2},{4,5},{6,7},{5,4},{7,6},{8,9},{10,11},{9,8... | collective-permute-start | bytes 307208 | tf_op jit(solution)/shard_map/ppermute | solution.py:640
  8.1 0.7 %shard_map.157 = (f32[2,192,128]{2,1,0:T(8,128)S(1)}, f32[2,192,128]{2,1,0:T(8,128)S(1)}, f32[2,192,128]{2,1,0:T(8,128)S(1)}, bf16[128,256]{1,0:T(8,128)(2,1)S(1)}) custom-call(bf16[192,576]{1,0:T(8,128)(2,1)S(1)} %get-tuple-element.43.table, f32[2,192,128]{2,1,0:T(8,128)S(1)} %get-tuple-element.47.lone_h1, f32[2,192,128]{2,1,0:T(8,128)S(1)} %get-tuple-element.48.lone_e1, ...), custom_call_target="tpu_custom_call" | custom-call | flops 113246208 | bytes 1909760 | tf_op jit(solution)/shard_map/pallas_call | solution.py:614
  8.8 0.0 collective-permute-done.across_in
  8.8 0.2 collective-permute-done.1.inside_in
  9.1 0.0 copy-start
  9.1 1.8 %shard_map.158 = (f32[2,192,128]{2,1,0:T(8,128)S(1)}, f32[2,192,128]{2,1,0:T(8,128)S(1)}, f32[2,192,128]{2,1,0:T(8,128)S(1)}, f32[2,192,128]{2,1,0:T(8,128)S(1)}...) custom-call(bf16[192,576]{1,0:T(8,128)(2,1)S(1)} %get-tuple-element., ...), custom_call_target="tpu_custom_call" | custom-call | flops 283115520 | bytes 3563520 | tf_op jit(solution)/shard_map/pallas_call | solution.py:614
  10.8 0.7 %collective-permute-start.2 = (f32[128,128]{1,0:T(8,128)S(1)}, f32[128,128]{1,0:T(8,128)S(1)}, u32[]{:S(2)}, u32[]{:S(2)}) collective-permute-start(f32[128,128]{1,0:T(8,128)S(1)} %get-tuple-element.71), channel_id=1, source_target_pairs={{1,2},{2,1},{5,6},{6,5},{9,10},{10,9},{13,14},{14,13},{17,18},{18,... | collective-permute-start | bytes 196616 | tf_op jit(solution)/shard_map/ppermute | solution.py:640
  11.5 4.4 %collective-permute-start.3 = (f32[128,128]{1,0:T(8,128)S(1)}, f32[128,128]{1,0:T(8,128)S(1)}, u32[]{:S(2)}, u32[]{:S(2)}) collective-permute-start(f32[128,128]{1,0:T(8,128)S(1)} %get-tuple-element.72), channel_id=1, source_target_pairs={{0,1},{2,3},{1,0},{3,2},{4,5},{6,7},{5,4},{7,6},{8,9},{10,11},{9,8... | collective-permute-start | bytes 196616 | tf_op jit(solution)/shard_map/ppermute | solution.py:640
  15.9 0.0 copy-done
  15.9 0.8 %shard_map.159 = (f32[2,192,128]{2,1,0:T(8,128)S(1)}, f32[2,192,128]{2,1,0:T(8,128)S(1)}, f32[128,256]{1,0:T(8,128)S(1)}) custom-call(bf16[192,576]{1,0:T(8,128)(2,1)S(1)} %get-tuple-element.43.table, f32[2,192,128]{2,1,0:T(8,128)S(1)} %get-tuple-element.48.lone_e1, f32[2,192,128]{2,1,0:T(8,128)S(1)} %get-tuple-element.64.answer_e, ...), custom_call_target="tpu_custom_call" | custom-call | flops 113246208 | bytes 3383296 | tf_op jit(solution)/shard_map/pallas_call | solution.py:614
  16.7 0.0 collective-permute-done.2.across_in
  16.7 0.1 collective-permute-done.3.inside_in
  16.8 1.1 %shard_map.160 = (f32[2,192,128]{2,1,0:T(8,128)S(1)}, f32[2,192,128]{2,1,0:T(8,128)S(1)}, f32[128,128]{1,0:T(8,128)S(1)}) custom-call(bf16[192,576]{1,0:T(8,128)(2,1)S(1)} %get-tuple-element.43.table, bf16[64,576]{1,0:T(8,128)(2,1)S(1)} %get-tuple-element.44.ends, bf16[192,192]{1,0:T(8,128)(2,1)S(1)} %get-tuple-element.45.edges, ...), custom_call_target="tpu_custom_call" | custom-call | flops 113246208 | bytes 2932736 | tf_op jit(solution)/shard_map/pallas_call | solution.py:614
  17.8 12.8 %all_to_all.11 = f32[8,16,128]{2,1,0:T(8,128)S(1)} all-to-all(f32[8,16,128]{2,1,0:T(8,128)S(1)} %bitcast.15), channel_id=1, replica_groups=mesh['exc'=8,'space'=4] {'exc'}, dimensions={0} | all-to-all | bytes 131072 | tf_op jit(solution)/shard_map/all_to_all | solution.py:718
  30.6 0.9 %shard_map.161 = (f32[192,256]{1,0:T(8,128)}, f32[192,256]{1,0:T(8,128)}, f32[16,64]{1,0:T(8,128)}, f32[16,64]{1,0:T(8,128)}) custom-call(f32[128,128]{1,0:T(8,128)S(1)} %bitcast.14, f32[2,192,128]{2,1,0:T(8,128)S(1)} %get-tuple-element.76.e, f32[2,192,128]{2,1,0:T(8,128)S(1)} %get-tuple-element.77.h), custom_call_target="tpu_custom_call" | custom-call | bytes 860160 | tf_op jit(solution)/shard_map/pallas_call | solution.py:614
Async XLA Ops:
  3.1 5.7 %collective-permute-start = (f32[200,128]{1,0:T(8,128)S(1)}, f32[200,128]{1,0:T(8,128)S(1)}, u32[]{:S(2)}, u32[]{:S(2)}) collective-permute-start(f32[200,128]{1,0:T(8,128)S(1)} %get-tuple-element.59), channel_id=1, source_target_pairs={{1,2},{2,1},{5,6},{6,5},{9,10},{10,9},{13,14},{14,13},{17,18},{18,... | collective-permute-start | bytes 307208 | tf_op jit(solution)/shard_map/ppermute | solution.py:640
  3.8 5.3 %collective-permute-start.1 = (f32[200,128]{1,0:T(8,128)S(1)}, f32[200,128]{1,0:T(8,128)S(1)}, u32[]{:S(2)}, u32[]{:S(2)}) collective-permute-start(f32[200,128]{1,0:T(8,128)S(1)} %get-tuple-element.60), channel_id=1, source_target_pairs={{0,1},{2,3},{1,0},{3,2},{4,5},{6,7},{5,4},{7,6},{8,9},{10,11},{9,8... | collective-permute-start | bytes 307208 | tf_op jit(solution)/shard_map/ppermute | solution.py:640
  9.1 6.8 %copy-start = (bf16[1,5,192,256]{3,2,1,0:T(8,128)(2,1)S(1)}, bf16[1,5,192,256]{3,2,1,0:T(8,128)(2,1)}, u32[]{:S(2)}) copy-start(bf16[1,5,192,256]{3,2,1,0:T(8,128)(2,1)} %param.16) | copy-start | bytes 1474564
  10.8 5.8 %collective-permute-start.2 = (f32[128,128]{1,0:T(8,128)S(1)}, f32[128,128]{1,0:T(8,128)S(1)}, u32[]{:S(2)}, u32[]{:S(2)}) collective-permute-start(f32[128,128]{1,0:T(8,128)S(1)} %get-tuple-element.71), channel_id=1, source_target_pairs={{1,2},{2,1},{5,6},{6,5},{9,10},{10,9},{13,14},{14,13},{17,18},{18,... | collective-permute-start | bytes 196616 | tf_op jit(solution)/shard_map/ppermute | solution.py:640
  11.5 5.3 %collective-permute-start.3 = (f32[128,128]{1,0:T(8,128)S(1)}, f32[128,128]{1,0:T(8,128)S(1)}, u32[]{:S(2)}, u32[]{:S(2)}) collective-permute-start(f32[128,128]{1,0:T(8,128)S(1)} %get-tuple-element.72), channel_id=1, source_target_pairs={{0,1},{2,3},{1,0},{3,2},{4,5},{6,7},{5,4},{7,6},{8,9},{10,11},{9,8... | collective-permute-start | bytes 196616 | tf_op jit(solution)/shard_map/ppermute | solution.py:640

commit v6 on v5

--- a/solution.py
+++ b/solution.py
@@ -395,7 +395,7 @@
     rest = [fetch(j_in, j), fetch(w_in, w_all), fetch(v_in, v_all), fetch(ends_in, ends)]
     later = [fetch(edges_in, edges), fetch(design_in, design)]
 
-    for copy in scatter:
+    for copy in scatter + fields + rest:
         copy.wait()
     found = neighbor[...]
     place = jnp.where(found < 0, 0, jnp.bitwise_and(found, LAYER - 1))
@@ -405,34 +405,35 @@
             places[6 * i + face] = jnp.broadcast_to(place[face : face + 1, columns], (8, LAYER))
         there = (found[i : i + 1, columns] >= 0).astype(F32)
         valid[i] = jnp.broadcast_to(there, (8, LAYER))
-    targets = lax.broadcasted_iota(jnp.int32, (2 * LAYER, ports.shape[1]), 0)
-    spread_hot = one_hot(targets, jnp.bitwise_and(ports[...], 2 * LAYER - 1))
-    high, low = halves(profile[...])
-    spread = layers_of(dot_t(high, spread_hot) + dot_t(low, spread_hot))
-    for copy in fields + rest:
-        copy.wait()
     electric = [stored(part) for part in layers_of(e[...])]
     magnetic = [stored(part) for part in layers_of(h[...])]
     current = [stored(part) for part in layers_of(j[...])]
     weight = layers_of(w_all[...])
     scale = layers_of(v_all[...])
-    drive = []
     for i in range(2):
-        source[i] = stored(spread[i])
         w[i] = weight[i]
         v[i] = scale[i]
         start_e[i] = electric[i]
         fe[L0 + i] = electric[i]
         fh[L0 + i] = magnetic[i]
-        now = KEEP * current[i] + TIME_STEP * thrice(weight[i]) * electric[i]
-        first_j[i] = now
-        drive.append(now + source[i])
+    drive = []
+
+    def scatter_source():
+        targets = lax.broadcasted_iota(jnp.int32, (2 * LAYER, ports.shape[1]), 0)
+        spread_hot = one_hot(targets, jnp.bitwise_and(ports[...], 2 * LAYER - 1))
+        high, low = halves(profile[...])
+        spread = layers_of(dot_t(high, spread_hot) + dot_t(low, spread_hot))
+        for i in range(2):
+            source[i] = stored(spread[i])
+            now = KEEP * current[i] + TIME_STEP * thrice(weight[i]) * start_e[i]
+            first_j[i] = now
+            drive.append(now + source[i])
 
     def index(layer, face):
         return places[6 * (layer - L0) + face]
 
     electric, magnetic, up, down = lonely(
-        table, ends, x, index, fe, fh, acc, electric, lambda: drive, v
+        table, ends, x, index, fe, fh, acc, electric, lambda: drive, v, scatter_source
     )
     for i in range(2):
         lone_e1[i] = electric[i]
@@ -501,7 +502,7 @@
     places, valid, across_in, inside_in, *rest
 ):
     end_e, next_h, next_e, next_j, answer_e, answer_j, v_near, near_places = rest[:8]
-    across, inside = rest[8:10]
+    inside, across = rest[8:10]
     fe, fh, acc, x, y, sent_a, sent_b = rest[10:]
     sides_of(across_in, inside_in, sent_a, sent_b, FIRST)
     for side, sent in enumerate((sent_a, sent_b)):
@@ -559,7 +560,7 @@
 
 def last_kernel(
     table, ends, edges, start_e, lone_h1, lone_e1, lone_h2, lone_e2, v, w, places, valid,
-    v_near, near_places, across_in, inside_in, levels, early, pixels, *rest
+    v_near, near_places, inside_in, across_in, levels, early, pixels, *rest
 ):
     out_e, out_h, sums = rest[:3]
     fe, fh, acc, y, sent_a, sent_b = rest[3:]
@@ -630,14 +631,19 @@
     return jax.ShapeDtypeStruct(shape, BF16)
 
 
-def exchange(across, inside):
+def exchange(across, inside, inside_first):
     size = lax.axis_size("space")
 
     def pairs(start):
         found = [(i, i + 1) for i in range(start, size - 1, 2)]
         return found + [(j, i) for i, j in found]
 
-    return lax.ppermute(across, "space", pairs(1)), lax.ppermute(inside, "space", pairs(0))
+    if inside_first:
+        inside = lax.ppermute(inside, "space", pairs(0))
+    across = lax.ppermute(across, "space", pairs(1))
+    if not inside_first:
+        inside = lax.ppermute(inside, "space", pairs(0))
+    return across, inside
 
 
 def local(
@@ -682,7 +688,7 @@
         6 * once,
         [pltpu.HBM] * len(given),
     )
-    across, inside = exchange(*sent)
+    across, inside = exchange(*sent, False)
     h2, e2, j2, pixels = call(
         lone_kernel,
         [field] * 3 + [bf16(PIX_DEV, count)],
@@ -690,7 +696,7 @@
         work,
         4 * once,
     )
-    end_e, h3, e3, j3, answer_e, answer_j, v_near, near_places, across, inside = call(
+    end_e, h3, e3, j3, answer_e, answer_j, v_near, near_places, inside, across = call(
         middle_kernel,
         [field] * 6 + [nodal, indices] + [f32(SECOND, LAYER)] * 2,
         [table, ends, edges, start_e, h1, e1, h2, e2, j2, v, w, source]
@@ -698,7 +704,7 @@
         work + edge_work + received,
         10 * once,
     )
-    across, inside = exchange(across, inside)
+    across, inside = exchange(across, inside, True)
     h4, e4, early = call(
         early_kernel,
         [field] * 2 + [f32(2 * NODES, count)],
@@ -711,7 +717,7 @@
         last_kernel,
         [field, field, f32(PIX_DEV, 2 * NODES)],
         [table, ends, edges, end_e, h3, e3, h4, e4, v, w, places, valid, v_near, near_places]
-        + [across, inside, levels, early, pixels],
+        + [inside, across, levels, early, pixels],
         work[:3] + edge_work + [pltpu.VMEM((SECOND, LAYER), F32)] * 2,
         4 * once,
     )

time: 31.7 us -> 31.2 us (0.984)
  the two profiles are of different devices: /device:TPU:0 before, /device:TPU:2 now
where the time goes in v6:
time: 31.2 us; the launch traced here: 30.9 us
  blocking collectives  12.5 us (40%)
  Pallas kernels  7.57 us (24%)
  waiting for transfers between devices  6.12 us (20%)
  starting transfers between devices  3.98 us (13%)
  between operations  0.72 us (2%)
    all_to_all x1, blocking collectives, local(): parts = lax.all_to_all(sums, 'exc', split_axis=0, concat_axis=0, tiled=True)  12.5 us
    pallas_call x6, Pallas kernels, call(): pl.pallas_call(kernel, out_shape=outs, in_specs=[pl.BlockSpec(memory_spac...  7.57 us
    ppermute x2, waiting for transfers between devices, exchange(): across = lax.ppermute(across, 'space', pairs(1))  6.11 us
    ppermute x2, starting transfers between devices, exchange(): across = lax.ppermute(across, 'space', pairs(1))  3.84 us
  transfers between devices with their start and end apart: 4, of which 2 were waited for; matrix products, arithmetic and copies ran while one was open for 0% of the time, Pallas kernels for 5%

profile of v6, /device:TPU:2, one launch (start us, length us, event | category | flops | bytes accessed | tf_op | source)
XLA Modules:
  0.0 30.9 jit_solution(4508484371511652704)
XLA Ops:
  0.6 2.4 %shard_map.156 = (bf16[192,576]{1,0:T(8,128)(2,1)S(1)}, bf16[64,576]{1,0:T(8,128)(2,1)S(1)}, bf16[192,192]{1,0:T(8,128)(2,1)S(1)}, s32[1,256]{1,0:T(1,128)S(1)},...) custom-call(bf16[192,576]{1,0:T(8,128)(2,1)} %constant.6.clone.table, ...), custom_call_target="tpu_custom_call" | custom-call | flops 169869312 | bytes 3310080 | tf_op jit(solution)/shard_map/pallas_call | solution.py:615
  3.1 1.9 %collective-permute-start = (f32[200,128]{1,0:T(8,128)S(1)}, f32[200,128]{1,0:T(8,128)S(1)}, u32[]{:S(2)}, u32[]{:S(2)}) collective-permute-start(f32[200,128]{1,0:T(8,128)S(1)} %get-tuple-element.59), channel_id=1, source_target_pairs={{1,2},{2,1},{5,6},{6,5},{9,10},{10,9},{13,14},{14,13},{17,18},{18,... | collective-permute-start | bytes 307208 | tf_op jit(solution)/shard_map/ppermute | solution.py:643
  5.0 0.1 collective-permute-start.1
  5.1 0.7 %shard_map.157 = (f32[2,192,128]{2,1,0:T(8,128)S(1)}, f32[2,192,128]{2,1,0:T(8,128)S(1)}, f32[2,192,128]{2,1,0:T(8,128)S(1)}, bf16[128,256]{1,0:T(8,128)(2,1)S(1)}) custom-call(bf16[192,576]{1,0:T(8,128)(2,1)S(1)} %get-tuple-element.43.table, f32[2,192,128]{2,1,0:T(8,128)S(1)} %get-tuple-element.47.lone_h1, f32[2,192,128]{2,1,0:T(8,128)S(1)} %get-tuple-element.48.lone_e1, ...), custom_call_target="tpu_custom_call" | custom-call | flops 113246208 | bytes 1909760 | tf_op jit(solution)/shard_map/pallas_call | solution.py:615
  5.8 3.3 %collective-permute-done.across_in = f32[200,128]{1,0:T(8,128)S(1)} collective-permute-done((f32[200,128]{1,0:T(8,128)S(1)}, f32[200,128]{1,0:T(8,128)S(1)}, u32[]{:S(2)}, u32[]{:S(2)}) %collective-permute-start) | collective-permute-done | bytes 102432 | tf_op jit(solution)/shard_map/ppermute | solution.py:643
  9.0 0.0 collective-permute-done.1.inside_in
  9.0 0.0 copy-start
  9.0 1.8 %shard_map.158 = (f32[2,192,128]{2,1,0:T(8,128)S(1)}, f32[2,192,128]{2,1,0:T(8,128)S(1)}, f32[2,192,128]{2,1,0:T(8,128)S(1)}, f32[2,192,128]{2,1,0:T(8,128)S(1)}...) custom-call(bf16[192,576]{1,0:T(8,128)(2,1)S(1)} %get-tuple-element., ...), custom_call_target="tpu_custom_call" | custom-call | flops 283115520 | bytes 3563520 | tf_op jit(solution)/shard_map/pallas_call | solution.py:615
  10.8 0.1 collective-permute-start.2
  10.9 1.9 %collective-permute-start.3 = (f32[128,128]{1,0:T(8,128)S(1)}, f32[128,128]{1,0:T(8,128)S(1)}, u32[]{:S(2)}, u32[]{:S(2)}) collective-permute-start(f32[128,128]{1,0:T(8,128)S(1)} %get-tuple-element.72), channel_id=1, source_target_pairs={{1,2},{2,1},{5,6},{6,5},{9,10},{10,9},{13,14},{14,13},{17,18},{18,... | collective-permute-start | bytes 196616 | tf_op jit(solution)/shard_map/ppermute | solution.py:643
  12.8 0.0 copy-done
  12.8 0.8 %shard_map.159 = (f32[2,192,128]{2,1,0:T(8,128)S(1)}, f32[2,192,128]{2,1,0:T(8,128)S(1)}, f32[128,256]{1,0:T(8,128)S(1)}) custom-call(bf16[192,576]{1,0:T(8,128)(2,1)S(1)} %get-tuple-element.43.table, f32[2,192,128]{2,1,0:T(8,128)S(1)} %get-tuple-element.48.lone_e1, f32[2,192,128]{2,1,0:T(8,128)S(1)} %get-tuple-element.64.answer_e, ...), custom_call_target="tpu_custom_call" | custom-call | flops 113246208 | bytes 3383296 | tf_op jit(solution)/shard_map/pallas_call | solution.py:615
  13.6 0.0 collective-permute-done.2.inside_in
  13.6 2.8 %collective-permute-done.3.across_in = f32[128,128]{1,0:T(8,128)S(1)} collective-permute-done((f32[128,128]{1,0:T(8,128)S(1)}, f32[128,128]{1,0:T(8,128)S(1)}, u32[]{:S(2)}, u32[]{:S(2)}) %collective-permute-start.3) | collective-permute-done | bytes 65568 | tf_op jit(solution)/shard_map/ppermute | solution.py:643
  16.5 1.1 %shard_map.160 = (f32[2,192,128]{2,1,0:T(8,128)S(1)}, f32[2,192,128]{2,1,0:T(8,128)S(1)}, f32[128,128]{1,0:T(8,128)S(1)}) custom-call(bf16[192,576]{1,0:T(8,128)(2,1)S(1)} %get-tuple-element.43.table, bf16[64,576]{1,0:T(8,128)(2,1)S(1)} %get-tuple-element.44.ends, bf16[192,192]{1,0:T(8,128)(2,1)S(1)} %get-tuple-element.45.edges, ...), custom_call_target="tpu_custom_call" | custom-call | flops 113246208 | bytes 2932736 | tf_op jit(solution)/shard_map/pallas_call | solution.py:615
  17.5 12.5 %all_to_all.11 = f32[8,16,128]{2,1,0:T(8,128)S(1)} all-to-all(f32[8,16,128]{2,1,0:T(8,128)S(1)} %bitcast.15), channel_id=1, replica_groups=mesh['exc'=8,'space'=4] {'exc'}, dimensions={0} | all-to-all | bytes 131072 | tf_op jit(solution)/shard_map/all_to_all | solution.py:724
  30.1 0.9 %shard_map.161 = (f32[192,256]{1,0:T(8,128)}, f32[192,256]{1,0:T(8,128)}, f32[16,64]{1,0:T(8,128)}, f32[16,64]{1,0:T(8,128)}) custom-call(f32[128,128]{1,0:T(8,128)S(1)} %bitcast.14, f32[2,192,128]{2,1,0:T(8,128)S(1)} %get-tuple-element.76.e, f32[2,192,128]{2,1,0:T(8,128)S(1)} %get-tuple-element.77.h), custom_call_target="tpu_custom_call" | custom-call | bytes 860160 | tf_op jit(solution)/shard_map/pallas_call | solution.py:615
Async XLA Ops:
  3.1 6.0 %collective-permute-start = (f32[200,128]{1,0:T(8,128)S(1)}, f32[200,128]{1,0:T(8,128)S(1)}, u32[]{:S(2)}, u32[]{:S(2)}) collective-permute-start(f32[200,128]{1,0:T(8,128)S(1)} %get-tuple-element.59), channel_id=1, source_target_pairs={{1,2},{2,1},{5,6},{6,5},{9,10},{10,9},{13,14},{14,13},{17,18},{18,... | collective-permute-start | bytes 307208 | tf_op jit(solution)/shard_map/ppermute | solution.py:643
  5.0 4.1 %collective-permute-start.1 = (f32[200,128]{1,0:T(8,128)S(1)}, f32[200,128]{1,0:T(8,128)S(1)}, u32[]{:S(2)}, u32[]{:S(2)}) collective-permute-start(f32[200,128]{1,0:T(8,128)S(1)} %get-tuple-element.60), channel_id=1, source_target_pairs={{0,1},{2,3},{1,0},{3,2},{4,5},{6,7},{5,4},{7,6},{8,9},{10,11},{9,8... | collective-permute-start | bytes 307208 | tf_op jit(solution)/shard_map/ppermute | solution.py:645
  9.0 3.8 %copy-start = (bf16[1,5,192,256]{3,2,1,0:T(8,128)(2,1)S(1)}, bf16[1,5,192,256]{3,2,1,0:T(8,128)(2,1)}, u32[]{:S(2)}) copy-start(bf16[1,5,192,256]{3,2,1,0:T(8,128)(2,1)} %param.16) | copy-start | bytes 1474564
  10.8 2.8 %collective-permute-start.2 = (f32[128,128]{1,0:T(8,128)S(1)}, f32[128,128]{1,0:T(8,128)S(1)}, u32[]{:S(2)}, u32[]{:S(2)}) collective-permute-start(f32[128,128]{1,0:T(8,128)S(1)} %get-tuple-element.71), channel_id=1, source_target_pairs={{0,1},{2,3},{1,0},{3,2},{4,5},{6,7},{5,4},{7,6},{8,9},{10,11},{9,8... | collective-permute-start | bytes 196616 | tf_op jit(solution)/shard_map/ppermute | solution.py:642
  10.9 5.6 %collective-permute-start.3 = (f32[128,128]{1,0:T(8,128)S(1)}, f32[128,128]{1,0:T(8,128)S(1)}, u32[]{:S(2)}, u32[]{:S(2)}) collective-permute-start(f32[128,128]{1,0:T(8,128)S(1)} %get-tuple-element.72), channel_id=1, source_target_pairs={{1,2},{2,1},{5,6},{6,5},{9,10},{10,9},{13,14},{14,13},{17,18},{18,... | collective-permute-start | bytes 196616 | tf_op jit(solution)/shard_map/ppermute | solution.py:643

commit v7 on v6

v7 whole, which is shorter than its diff:
```python
import functools

import jax
import jax.numpy as jnp
import numpy as np
from jax import lax
from jax.experimental import pallas as pl
from jax.experimental.pallas import tpu as pltpu
from jax.sharding import PartitionSpec as P

NODES = 64
ROWS = 3 * NODES
LAYER = 128
PIX_DEV = 128

TIME_STEP = 0.025
DAMPING = 0.5
KEEP = 1.0 - TIME_STEP * DAMPING

TANGENT = 32
E_START = 0
H_FIRST = 32
E_FIRST = 64
H_SECOND = 96
SECOND = 128
V_NEAR = 128
N_NEAR = V_NEAR + NODES
FIRST = N_NEAR + 8

A1, L0, L1, B1 = range(4)

BASE = (NODES, 0, 2 * NODES)

BF16 = jnp.bfloat16
F32 = jnp.float32


def parity(c, face, other):
    d = face // 2
    sign = 1.0 if face % 2 else -1.0
    return 6.0 * sign * (c - d) * (d - other) * (other - c) / 2.0


def off_diagonal():
    points = np.array([-1.0, -1.0 / np.sqrt(5.0), 1.0 / np.sqrt(5.0), 1.0])
    barycentric = np.array(
        [1.0 / np.prod([points[j] - points[k] for k in range(4) if k != j]) for j in range(4)]
    )
    deriv = np.zeros((4, 4))
    for row in range(4):
        for column in range(4):
            if row != column:
                deriv[row, column] = (
                    barycentric[column] / barycentric[row] / (points[row] - points[column])
                )
    return (2.0 * deriv).tolist()


SLOPES = off_diagonal()


def slope(parts, row, scale):
    terms = [(scale * SLOPES[row][i]) * parts[i] for i in range(4) if i != row]
    return terms[0] + terms[1] + terms[2]


def halves(x):
    high = x.astype(BF16)
    return high, (x - high.astype(F32)).astype(BF16)


def dot_t(a, b):
    return lax.dot_general(a, b, (((1,), (1,)), ((), ())), preferred_element_type=F32)


def thrice(x):
    return jnp.concatenate([x, x, x], axis=0)


def folded(x):
    return x[0:NODES] + x[NODES : 2 * NODES] + x[2 * NODES : ROWS]


def stored(x):
    return jnp.concatenate([x[NODES : 2 * NODES], x[0:NODES], x[2 * NODES : ROWS]], axis=0)


def one_hot(rows, targets):
    return (rows == targets).astype(F32).astype(BF16)


def picked(x, index):
    rows = x.shape[0]
    if rows < 8:
        index = index[0:rows]
    elif rows > 8:
        index = jnp.concatenate([index] * (rows // 8), axis=0)
    along = lax.GatherDimensionNumbers(
        offset_dims=(),
        collapsed_slice_dims=(1,),
        start_index_map=(1,),
        operand_batching_dims=(0,),
        start_indices_batching_dims=(0,),
    )
    mode = lax.GatherScatterMode.PROMISE_IN_BOUNDS
    return lax.gather(x, index[..., None], along, (1, 1), mode=mode)


def at_end(face):
    return 3 if face % 2 else 0


def x_traces(field, layer, face):
    at = 16 * at_end(face)
    return [field[layer, BASE[c] + at : BASE[c] + at + 16, :] for c in (1, 2)]


def lift_x(target, layer, face, scale, y, z):
    at = 16 * at_end(face)
    rows = slice(BASE[1] + at, BASE[1] + at + 16)
    target[layer, rows, :] += (-scale * parity(1, face, 2)) * z
    rows = slice(BASE[2] + at, BASE[2] + at + 16)
    target[layer, rows, :] += (-scale * parity(2, face, 1)) * y


def add_x(target, field, layer, scale, outer, base=None):
    for c, other, sign in ((1, 2, 1.0), (2, 1, -1.0)):
        parts = [field[layer, BASE[other] + 16 * i : BASE[other] + 16 * i + 16, :] for i in range(4)]
        for i in range(4):
            change = slope(parts, i, scale * sign)
            face = {0: 0, 3: 1}.get(i)
            traces = None if face is None else outer(face)
            if traces is not None:
                change += (-scale * parity(c, face, other)) * traces[other - 1]
            rows = slice(BASE[c] + 16 * i, BASE[c] + 16 * i + 16)
            before = target[layer, rows, :] if base is None else base[rows]
            target[layer, rows, :] = before + change
    if base is not None:
        rows = slice(BASE[0], BASE[0] + NODES)
        target[layer, rows, :] = base[rows]


def add_yz(target, field, layer, index, scale):
    for c, other, sign in ((0, 1, 1.0), (1, 0, -1.0)):
        parts = [field[layer, pl.ds(BASE[other] + k, 16, stride=4), :] for k in range(4)]
        for k in range(4):
            change = slope(parts, k, scale * sign)
            if k in (0, 3):
                face = 4 if k == 0 else 5
                got = picked(parts[3 - k], index(layer, face))
                change += (-scale * parity(c, face, other)) * got
            target[layer, pl.ds(BASE[c] + k, 16, stride=4), :] += change
    sign = jnp.where(lax.broadcasted_iota(jnp.int32, (8, LAYER), 0) < 4, -1.0, 1.0)
    for k in range(4):
        parts = [field[layer, pl.ds(BASE[0] + 4 * j + k, 8, stride=16), :] for j in range(4)]
        for j in range(4):
            change = slope(parts, j, scale)
            if j in (0, 3):
                face = 2 if j == 0 else 3
                got = picked(parts[3 - j], index(layer, face))
                change += (scale * parity(0, face, 2)) * got
            rows = pl.ds(BASE[0] + 4 * j + k, 8, stride=16)
            target[layer, rows, :] += sign * pltpu.roll(change, 4, 0)


def add_end(target, field, layer, i, index, scale, to_x):
    c, other, sign = (0, 1, 1.0) if to_x else (1, 0, -1.0)
    at = BASE[other] + 16 * i
    parts = [field[layer, pl.ds(at + k, 4, stride=4), :] for k in range(4)]
    for k in range(4):
        change = slope(parts, k, scale * sign)
        if k in (0, 3):
            face = 4 if k == 0 else 5
            got = picked(parts[3 - k], index(layer, face))
            change += (-scale * parity(c, face, other)) * got
        target[layer, pl.ds(BASE[c] + 16 * i + k, 4, stride=4), :] += change
    c, other, sign = (0, 2, -1.0) if to_x else (2, 0, 1.0)
    at = BASE[other] + 16 * i
    parts = [field[layer, at + 4 * j : at + 4 * j + 4, :] for j in range(4)]
    for j in range(4):
        change = slope(parts, j, scale * sign)
        if j in (0, 3):
            face = 2 if j == 0 else 3
            got = picked(parts[3 - j], index(layer, face))
            change += (-scale * parity(c, face, other)) * got
        at = BASE[c] + 16 * i + 4 * j
        target[layer, at : at + 4, :] += change


def add_into_end(target, field, layer, i, index, scale):
    for c, other, sign in ((1, 2, 1.0), (2, 1, -1.0)):
        parts = [field[layer, BASE[other] + 16 * n : BASE[other] + 16 * n + 16, :] for n in range(4)]
        rows = slice(BASE[c] + 16 * i, BASE[c] + 16 * i + 16)
        target[layer, rows, :] += slope(parts, i, scale * sign)
    add_end(target, field, layer, i, index, scale, False)


def add_from_end(target, field, layer, i, index, scale):
    for c, other, sign in ((1, 2, 1.0), (2, 1, -1.0)):
        part = field[layer, BASE[other] + 16 * i : BASE[other] + 16 * i + 16, :]
        for n in range(4):
            if n != i:
                rows = slice(BASE[c] + 16 * n, BASE[c] + 16 * n + 16)
                target[layer, rows, :] += (scale * sign * SLOPES[n][i]) * part
    add_end(target, field, layer, i, index, scale, True)


def layers_of(x):
    return [x[:, at : at + LAYER] for at in range(0, x.shape[1], LAYER)]


def between(field, index, layer):
    def outer(face):
        if (layer, face) not in ((L0, 1), (L1, 0)):
            return None
        traces = x_traces(field, L0 + L1 - layer, face ^ 1)
        return [picked(t, index(layer, face)) for t in traces]

    return outer


def lone_h(index, fe, fh):
    for layer in (L0, L1):
        add_x(fh, fe, layer, TIME_STEP, between(fe, index, layer))
        add_yz(fh, fe, layer, index, TIME_STEP)


def lone_e(index, fe, fh, acc, drive, v):
    for i, layer in enumerate((L0, L1)):
        add_x(acc, fh, layer, 1.0, between(fh, index, layer), drive[i])
        add_yz(acc, fh, layer, index, 1.0)
        fe[layer] -= TIME_STEP * thrice(v[i]) * acc[layer]


def lonely(index, fe, fh, acc, drive, v, out_h, out_e):
    def ends_of(field):
        return x_traces(field, L1, 1), x_traces(field, L0, 0)

    found = [ends_of(fe)]
    lone_h(index, fe, fh)
    found.append(ends_of(fh))
    for i in range(2):
        out_h[i] = fh[L0 + i]
    lone_e(index, fe, fh, acc, drive, v)
    found.append(ends_of(fe))
    for i in range(2):
        out_e[i] = fe[L0 + i]
    for face, layer in enumerate((L0, L1)):
        add_into_end(fh, fe, layer, at_end(face), index, TIME_STEP)
    found.append(ends_of(fh))
    return [jnp.concatenate(sum(traces, []), axis=0) for traces in zip(*found)]


def respond(index, valid, fe, fh, acc, lone, v, w, v_near, sent_a, sent_b):
    start_e, lone_h1, lone_e1 = lone
    own, wide = (L0, L1), (A1, L0, L1, B1)
    sides = ((A1, 1, L0, sent_a), (B1, 0, L1, sent_b))
    blank = jnp.zeros((ROWS, LAYER), F32)

    def inward(target, field, scale, start, answered=True):
        for side, (near, face, layer, sent) in enumerate(sides):
            traces = [sent[start + 16 * t : start + 16 * t + 16, :] for t in range(2)]
            if answered:
                traces = [a + b for a, b in zip(traces, x_traces(field, near, face))]
            mask = jnp.concatenate([valid[side]] * 2, axis=0)
            got = [picked(t, index(layer, face ^ 1)) * mask for t in traces]
            lift_x(target, layer, face ^ 1, scale, *got)

    def outward(target, field, alone, scale, answered=True):
        for near, face, layer, _ in sides:
            traces = x_traces(alone, layer - L0, face ^ 1)
            if answered:
                traces = [a + b for a, b in zip(traces, x_traces(field, layer, face ^ 1))]
            got = [picked(t, index(near, face)) for t in traces]
            lift_x(target, near, face, scale, *got)

    for layer in wide:
        fh[layer] = blank
        acc[layer] = blank
    inward(fh, fe, TIME_STEP, E_START, False)
    outward(fh, fe, start_e, TIME_STEP, False)

    inward(acc, fh, 1.0, H_FIRST)
    outward(acc, fh, lone_h1, 1.0)
    first_e = []
    for layer, scale in zip(wide, [v_near[0], v[0], v[1], v_near[1]]):
        add_from_end(acc, fh, layer, 3 if layer in (A1, L1) else 0, index, 1.0)
        first_e.append(-TIME_STEP * thrice(scale) * acc[layer])
        fe[layer] = first_e[-1]

    inward(fh, fe, TIME_STEP, E_FIRST)
    outward(fh, fe, lone_e1, TIME_STEP)
    for near, face, _, _ in sides:
        add_into_end(fh, fe, near, at_end(face), index, TIME_STEP)
    lone_h(index, fe, fh)

    current = [TIME_STEP * thrice(w[i]) * first_e[1 + i] for i in range(2)]
    second_e = []
    for i, layer in enumerate(own):
        add_x(acc, fh, layer, 1.0, between(fh, index, layer), current[i])
        add_yz(acc, fh, layer, index, 1.0)
    inward(acc, fh, 1.0, H_SECOND)
    for i, layer in enumerate(own):
        second_e.append(first_e[1 + i] - TIME_STEP * thrice(v[i]) * acc[layer])
    return first_e[1:3], [fh[layer] for layer in own], second_e, current


def odd_rank():
    return lax.rem(lax.axis_index("space"), 2) == 1


def send(across, inside, at, up, down):
    odd = odd_rank()
    rows = slice(at, at + up.shape[0])
    across[rows, :] = jnp.where(odd, up, down)
    inside[rows, :] = jnp.where(odd, down, up)


def sides_of(across, inside, a, b, rows):
    odd = odd_rank()
    from_across, from_inside = across[0:rows, :], inside[0:rows, :]
    a[...] = jnp.where(odd, from_inside, from_across)
    b[...] = jnp.where(odd, from_across, from_inside)


def first_kernel(
    e_in, h_in, j_in, v_in, w_in, near_in, ports_in, profile_in, design_in, *rest
):
    design, start_e, lone_h1, lone_e1, first_j, v, w, source, places, valid = rest[:10]
    across, inside, fe, fh, acc, neighbor, ports, profile, e, h, j, v_all, w_all, sems = rest[10:]
    started = []

    def fetch(origin, target):
        started.append(pltpu.make_async_copy(origin, target, sems.at[len(started)]))
        started[-1].start()

    fetch(near_in, neighbor)
    fetch(ports_in, ports)
    fetch(profile_in, profile)
    for origin, target in ((e_in, e), (h_in, h), (j_in, j), (w_in, w_all), (v_in, v_all)):
        fetch(origin, target)
    fetch(design_in, design)
    for copy in started:
        copy.wait()
    found = neighbor[...]
    place = jnp.where(found < 0, 0, jnp.bitwise_and(found, LAYER - 1))
    for i in range(2):
        columns = slice(i * LAYER, (i + 1) * LAYER)
        for face in range(6):
            places[6 * i + face] = jnp.broadcast_to(place[face : face + 1, columns], (8, LAYER))
        there = (found[i : i + 1, columns] >= 0).astype(F32)
        valid[i] = jnp.broadcast_to(there, (8, LAYER))
    electric = [stored(part) for part in layers_of(e[...])]
    magnetic = [stored(part) for part in layers_of(h[...])]
    current = [stored(part) for part in layers_of(j[...])]
    weight = layers_of(w_all[...])
    scale = layers_of(v_all[...])
    for i in range(2):
        w[i] = weight[i]
        v[i] = scale[i]
        start_e[i] = electric[i]
        fe[L0 + i] = electric[i]
        fh[L0 + i] = magnetic[i]
    targets = lax.broadcasted_iota(jnp.int32, (2 * LAYER, ports.shape[1]), 0)
    spread_hot = one_hot(targets, jnp.bitwise_and(ports[...], 2 * LAYER - 1))
    high, low = halves(profile[...])
    spread = layers_of(dot_t(high, spread_hot) + dot_t(low, spread_hot))
    drive = []
    for i in range(2):
        source[i] = stored(spread[i])
        now = KEEP * current[i] + TIME_STEP * thrice(weight[i]) * electric[i]
        first_j[i] = now
        drive.append(now + source[i])

    up, down = lonely(own_index(places), fe, fh, acc, drive, v, lone_h1, lone_e1)
    send(across, inside, 0, up, down)
    send(across, inside, V_NEAR, v[1], v[0])
    blank = jnp.zeros((2, LAYER), F32)
    place = place.astype(F32)
    send(
        across,
        inside,
        N_NEAR,
        jnp.concatenate([place[:, LAYER : 2 * LAYER], blank], axis=0),
        jnp.concatenate([place[:, 0:LAYER], blank], axis=0),
    )


def own_index(places):
    def index(layer, face):
        return places[6 * (layer - L0) + face]

    return index


def second_lone_step(lone_h1, lone_e1, first_j, v, w, source, places, work):
    fe, fh, acc = work
    index = own_index(places)
    for i in range(2):
        fe[L0 + i] = lone_e1[i]
        fh[L0 + i] = lone_h1[i]
    current = [KEEP * first_j[i] + TIME_STEP * thrice(w[i]) * lone_e1[i] for i in range(2)]
    lone_h(index, fe, fh)
    lone_e(index, fe, fh, acc, [current[i] + source[i] for i in range(2)], v)
    return current


def lone_kernel(lone_h1, lone_e1, first_j, v, w, source, places, design, *rest):
    lone_h2, lone_e2, lone_j2, pixels, fe, fh, acc = rest
    pixel = jnp.bitwise_and(design[...], PIX_DEV - 1)
    pixels[...] = one_hot(lax.broadcasted_iota(jnp.int32, pixels.shape, 0), pixel)
    current = second_lone_step(
        lone_h1, lone_e1, first_j, v, w, source, places, (fe, fh, acc)
    )
    for i in range(2):
        lone_h2[i] = fh[L0 + i]
        lone_e2[i] = fe[L0 + i]
        lone_j2[i] = current[i]


def index_of(places, near_places):
    def index(layer, face):
        if layer in (L0, L1):
            return places[6 * (layer - L0) + face]
        return near_places[6 * (layer == B1) + face]

    return index


def middle_kernel(
    start_e, lone_h1, lone_e1, lone_h2, lone_e2, lone_j2, v, w, source, places,
    valid, across_in, inside_in, *rest
):
    end_e, next_h, next_e, next_j, answer_e, answer_j, v_near, near_places = rest[:8]
    inside, across = rest[8:10]
    fe, fh, acc, sent_a, sent_b = rest[10:]
    sides_of(across_in, inside_in, sent_a, sent_b, FIRST)
    for side, sent in enumerate((sent_a, sent_b)):
        v_near[side] = sent[V_NEAR : V_NEAR + NODES, :]
        place = sent[N_NEAR : N_NEAR + 8, :].astype(jnp.int32)
        for face in range(6):
            near_places[6 * side + face] = jnp.broadcast_to(place[face : face + 1], (8, LAYER))
    index = index_of(places, near_places)
    first_e, magnetic, second_e, current = respond(
        index, valid, fe, fh, acc, (start_e, lone_h1, lone_e1), v, w, v_near, sent_a, sent_b
    )
    drive = []
    for i in range(2):
        answer_e[i] = first_e[i]
        answer_j[i] = current[i]
        electric = lone_e2[i] + second_e[i]
        end_e[i] = electric
        fe[L0 + i] = electric
        fh[L0 + i] = lone_h2[i] + magnetic[i]
        before = lone_j2[i] + current[i]
        now = KEEP * before + TIME_STEP * thrice(w[i]) * electric
        next_j[i] = now
        drive.append(now + source[i])
    up, down = lonely(index, fe, fh, acc, drive, v, next_h, next_e)
    send(across, inside, 0, up, down)


def early_kernel(
    lone_e1, answer_e, lone_j1, lone_j2, answer_j, end_e, next_h, next_e, next_j, v, w,
    source, places, levels, *rest
):
    last_h, last_e, out, fe, fh, acc = rest
    current = second_lone_step(next_h, next_e, next_j, v, w, source, places, (fe, fh, acc))
    for i in range(2):
        electric = fe[L0 + i]
        last_h[i] = fh[L0 + i]
        last_e[i] = electric
        columns = slice(i * LAYER, (i + 1) * LAYER)
        level = [stored(levels[k, :, columns].astype(F32)) for k in range(5)]
        eps = (lone_e1[i] + answer_e[i]) * (level[1] - level[0])
        eps += end_e[i] * (level[2] - level[1]) + next_e[i] * (level[3] - level[2])
        eps += electric * (level[4] - level[3])
        drude = lone_j1[i] * level[0] + (lone_j2[i] + answer_j[i]) * level[1]
        drude += next_j[i] * level[2] + current[i] * level[3]
        out[0:NODES, columns] = folded(eps)
        out[NODES : 2 * NODES, columns] = folded(drude)


def last_kernel(
    start_e, lone_h1, lone_e1, lone_h2, lone_e2, v, w, places, valid, v_near, near_places,
    inside_in, across_in, levels, early, pixels, *rest
):
    out_e, out_h, sums = rest[:3]
    fe, fh, acc, sent_a, sent_b = rest[3:]
    sides_of(across_in, inside_in, sent_a, sent_b, SECOND)
    first_e, magnetic, second_e, current = respond(
        index_of(places, near_places), valid, fe, fh, acc, (start_e, lone_h1, lone_e1),
        v, w, v_near, sent_a, sent_b,
    )
    parts = []
    for i in range(2):
        out_e[i] = lone_e2[i] + second_e[i]
        out_h[i] = lone_h2[i] + magnetic[i]
        columns = slice(i * LAYER, (i + 1) * LAYER)
        start, middle, end = (stored(levels[k, :, columns].astype(F32)) for k in range(2, 5))
        eps = folded(first_e[i] * (middle - start) + second_e[i] * (end - middle))
        drude = folded(current[i] * middle)
        parts.append(jnp.concatenate([eps, drude], axis=0) + early[:, columns])
    both = jnp.concatenate(parts, axis=1)
    high, low = halves(both)
    sums[...] = dot_t(pixels[...], high) + dot_t(pixels[...], low)


def total_kernel(owners, parts, e, h, out_e, out_h, eps, drude, sums, sems):
    copies = []

    def write(origin, target):
        copies.append(pltpu.make_async_copy(origin, target, sems.at[len(copies)]))
        copies[-1].start()

    for field, target in ((e, out_e), (h, out_h)):
        for i in range(2):
            for c in range(3):
                there = target.at[pl.ds(c * NODES, NODES), pl.ds(i * LAYER, LAYER)]
                write(field.at[i, pl.ds(BASE[c], NODES), :], there)
    share = parts.shape[0] // owners
    total = parts[0:share]
    for owner in range(1, owners):
        total = total + parts[owner * share : (owner + 1) * share]
    total = total * (1.0 / owners)
    sums[0] = total[:, 0:NODES]
    sums[1] = total[:, NODES : 2 * NODES]
    write(sums.at[0], eps)
    write(sums.at[1], drude)
    for copy in copies:
        copy.wait()


def call(kernel, outs, args, scratch=(), spaces=None, out_spaces=None):
    moved = sum(4 * int(np.prod(o.shape)) for o in outs) + sum(
        a.dtype.itemsize * int(np.prod(a.shape)) for a in args
    )
    return pl.pallas_call(
        kernel,
        out_shape=outs,
        in_specs=[pl.BlockSpec(memory_space=s) for s in spaces or [pltpu.VMEM] * len(args)],
        out_specs=[pl.BlockSpec(memory_space=s) for s in out_spaces or [pltpu.VMEM] * len(outs)],
        scratch_shapes=list(scratch),
        compiler_params=pltpu.CompilerParams(vmem_limit_bytes=24 * 1024 * 1024),
        cost_estimate=pl.CostEstimate(flops=moved, bytes_accessed=moved, transcendentals=0),
    )(*args)


def f32(*shape):
    return jax.ShapeDtypeStruct(shape, F32)


def bf16(*shape):
    return jax.ShapeDtypeStruct(shape, BF16)


def exchange(across, inside, inside_first):
    size = lax.axis_size("space")

    def pairs(start):
        found = [(i, i + 1) for i in range(start, size - 1, 2)]
        return found + [(j, i) for i, j in found]

    if inside_first:
        inside = lax.ppermute(inside, "space", pairs(0))
    across = lax.ppermute(across, "space", pairs(1))
    if not inside_first:
        inside = lax.ppermute(inside, "space", pairs(0))
    return across, inside


def local(
    adj_e,
    adj_h,
    adj_j,
    fwd_e,
    inv_eps,
    drude_weight,
    neighbor,
    design_map,
    port_elems,
    port_profile,
):
    count = adj_e.shape[2]
    owners = lax.axis_size("exc")
    levels = fwd_e[0]
    field, nodal = f32(2, ROWS, LAYER), f32(2, NODES, LAYER)
    indices = jax.ShapeDtypeStruct((12, 8, LAYER), jnp.int32)
    work = [pltpu.VMEM((4, ROWS, LAYER), F32)] * 3
    given = [adj_e[0], adj_h[0], adj_j[0], inv_eps, drude_weight]
    given += [neighbor, port_elems, port_profile[0], design_map.reshape(1, count)]
    received = [pltpu.VMEM((FIRST, LAYER), F32)] * 2
    design, start_e, h1, e1, j1, v, w, source, places, valid, *sent = call(
        first_kernel,
        [jax.ShapeDtypeStruct((1, count), jnp.int32)]
        + [field] * 4
        + [nodal, nodal, field, indices, f32(2, 8, LAYER)]
        + [f32(FIRST, LAYER)] * 2,
        [pltpu.with_memory_space_constraint(a, pltpu.HBM) for a in given],
        work
        + [pltpu.VMEM(a.shape, a.dtype) for a in [neighbor, port_elems, port_profile[0]]]
        + [pltpu.VMEM((ROWS, count), F32)] * 3
        + [pltpu.VMEM((NODES, count), F32)] * 2
        + [pltpu.SemaphoreType.DMA((9,))],
        spaces=[pltpu.HBM] * len(given),
    )
    across, inside = exchange(*sent, False)
    h2, e2, j2, pixels = call(
        lone_kernel,
        [field] * 3 + [bf16(PIX_DEV, count)],
        [h1, e1, j1, v, w, source, places, design],
        work,
    )
    end_e, h3, e3, j3, answer_e, answer_j, v_near, near_places, inside, across = call(
        middle_kernel,
        [field] * 6 + [nodal, indices] + [f32(SECOND, LAYER)] * 2,
        [start_e, h1, e1, h2, e2, j2, v, w, source, places, valid, across, inside],
        work + received,
    )
    across, inside = exchange(across, inside, True)
    h4, e4, early = call(
        early_kernel,
        [field] * 2 + [f32(2 * NODES, count)],
        [e1, answer_e, j1, j2, answer_j, end_e, h3, e3, j3, v, w, source, places, levels],
        work,
    )
    e4, h4, sums = call(
        last_kernel,
        [field, field, f32(PIX_DEV, 2 * NODES)],
        [end_e, h3, e3, h4, e4, v, w, places, valid, v_near, near_places]
        + [inside, across, levels, early, pixels],
        work + [pltpu.VMEM((SECOND, LAYER), F32)] * 2,
    )
    parts = lax.all_to_all(sums, "exc", split_axis=0, concat_axis=0, tiled=True)
    share = PIX_DEV // owners
    out_e, out_h, eps, drude = call(
        functools.partial(total_kernel, owners),
        [f32(ROWS, count)] * 2 + [f32(share, NODES)] * 2,
        [parts, e4, h4],
        [pltpu.VMEM((2, share, NODES), F32), pltpu.SemaphoreType.DMA((14,))],
        out_spaces=[pltpu.HBM] * 4,
    )
    return out_e[None], out_h[None], eps.T, drude.T


def solution(mesh):
    return jax.shard_map(
        local,
        mesh=mesh,
        in_specs=(
            P("exc", None, "space"),
            P("exc", None, "space"),
            P("exc", None, "space"),
            P("exc", None, None, "space"),
            P(None, "space"),
            P(None, "space"),
            P(None, "space"),
            P("space"),
            P("exc", "space"),
            P("exc", None, "space"),
        ),
        out_specs=(
            P("exc", None, "space"),
            P("exc", None, "space"),
            P(None, ("space", "exc")),
            P(None, ("space", "exc")),
        ),
        check_vma=False,
    )
```

time: 31.2 us -> 30.3 us (0.971)
  Pallas kernels: 7.57 us -> 6.44 us
    pallas_call x6, Pallas kernels: 7.57 us -> 6.44 us  [call(): pl.pallas_call(kernel, out_shape=outs, in_specs=[pl.BlockSpec(memory_spac...]
  transfers between devices with their start and end apart: 4 -> 4, of which waited for: 2 -> 2; matrix products, arithmetic and copies ran while one was open for 0% -> 0% of each run, Pallas kernels for 5% -> 4%
where the time goes in v7:
time: 30.3 us; the launch traced here: 30 us
  blocking collectives  12.5 us (41%)
  Pallas kernels  6.44 us (21%)
  waiting for transfers between devices  6.37 us (21%)
  starting transfers between devices  3.98 us (13%)
  between operations  0.72 us (2%)
    all_to_all x1, blocking collectives, local(): parts = lax.all_to_all(sums, 'exc', split_axis=0, concat_axis=0, tiled=True)  12.5 us
    pallas_call x6, Pallas kernels, call(): pl.pallas_call(kernel, out_shape=outs, in_specs=[pl.BlockSpec(memory_spac...  6.44 us
    ppermute x2, waiting for transfers between devices, exchange(): across = lax.ppermute(across, 'space', pairs(1))  6.36 us
    ppermute x2, starting transfers between devices, exchange(): across = lax.ppermute(across, 'space', pairs(1))  3.84 us
  transfers between devices with their start and end apart: 4, of which 2 were waited for; matrix products, arithmetic and copies ran while one was open for 0% of the time, Pallas kernels for 4%

profile of v7, /device:TPU:2, one launch (start us, length us, event | category | flops | bytes accessed | tf_op | source)
XLA Modules:
  0.0 30.0 jit_solution(7655566682776694208)
XLA Ops:
  0.6 2.0 %shard_map.129 = (s32[1,256]{1,0:T(1,128)S(1)}, f32[2,192,128]{2,1,0:T(8,128)S(1)}, f32[2,192,128]{2,1,0:T(8,128)S(1)}, f32[2,192,128]{2,1,0:T(8,128)S(1)}, f32[...) custom-call(f32[192,256]{1,0:T(8,128)} %bitcast.16, ...), custom_call_target="tpu_custom_call" | custom-call | flops 2204160 | bytes 2204160 | tf_op jit(solution)/shard_map/pallas_call | solution.py:538
  2.6 1.9 %collective-permute-start = (f32[200,128]{1,0:T(8,128)S(1)}, f32[200,128]{1,0:T(8,128)S(1)}, u32[]{:S(2)}, u32[]{:S(2)}) collective-permute-start(f32[200,128]{1,0:T(8,128)S(1)} %get-tuple-element.53), channel_id=1, source_target_pairs={{1,2},{2,1},{5,6},{6,5},{9,10},{10,9},{13,14},{14,13},{17,18},{18,... | collective-permute-start | bytes 307208 | tf_op jit(solution)/shard_map/ppermute | solution.py:566
  4.5 0.1 collective-permute-start.1
  4.6 0.5 %shard_map.130 = (f32[2,192,128]{2,1,0:T(8,128)S(1)}, f32[2,192,128]{2,1,0:T(8,128)S(1)}, f32[2,192,128]{2,1,0:T(8,128)S(1)}, bf16[128,256]{1,0:T(8,128)(2,1)S(1)}) custom-call(f32[2,192,128]{2,1,0:T(8,128)S(1)} %get-tuple-element.41.lone_h1, f32[2,192,128]{2,1,0:T(8,128)S(1)} %get-tuple-element.42.lone_e1, ...), custom_call_target="tpu_custom_call" | custom-call | flops 1688576 | bytes 1688576 | tf_op jit(solution)/shard_map/pallas_call | solution.py:538
  5.1 3.4 %collective-permute-done.across_in = f32[200,128]{1,0:T(8,128)S(1)} collective-permute-done((f32[200,128]{1,0:T(8,128)S(1)}, f32[200,128]{1,0:T(8,128)S(1)}, u32[]{:S(2)}, u32[]{:S(2)}) %collective-permute-start) | collective-permute-done | bytes 102432 | tf_op jit(solution)/shard_map/ppermute | solution.py:566
  8.6 0.0 collective-permute-done.1.inside_in
  8.6 0.0 copy-start
  8.6 1.4 %shard_map.131 = (f32[2,192,128]{2,1,0:T(8,128)S(1)}, f32[2,192,128]{2,1,0:T(8,128)S(1)}, f32[2,192,128]{2,1,0:T(8,128)S(1)}, f32[2,192,128]{2,1,0:T(8,128)S(1)}...) custom-call(f32[2,192,128]{2,1,0:T(8,128)S(1)} %get-tuple-element.40, ...), custom_call_target="tpu_custom_call" | custom-call | flops 3194880 | bytes 3194880 | tf_op jit(solution)/shard_map/pallas_call | solution.py:538
  10.0 0.1 collective-permute-start.2
  10.0 1.9 %collective-permute-start.3 = (f32[128,128]{1,0:T(8,128)S(1)}, f32[128,128]{1,0:T(8,128)S(1)}, u32[]{:S(2)}, u32[]{:S(2)}) collective-permute-start(f32[128,128]{1,0:T(8,128)S(1)} %get-tuple-element.66), channel_id=1, source_target_pairs={{1,2},{2,1},{5,6},{6,5},{9,10},{10,9},{13,14},{14,13},{17,18},{18,... | collective-permute-start | bytes 196616 | tf_op jit(solution)/shard_map/ppermute | solution.py:566
  12.0 0.0 copy-done
  12.0 0.7 %shard_map.132 = (f32[2,192,128]{2,1,0:T(8,128)S(1)}, f32[2,192,128]{2,1,0:T(8,128)S(1)}, f32[128,256]{1,0:T(8,128)S(1)}) custom-call(f32[2,192,128]{2,1,0:T(8,128)S(1)} %get-tuple-element.42.lone_e1, f32[2,192,128]{2,1,0:T(8,128)S(1)} %get-tuple-element.58.answer_e, f32[2,192,128]{2,1,0:T(8,128)S(1)} %get-tuple-element.43.first_j.lone_j1, ...), custom_call_target="tpu_custom_call" | custom-call | flops 3162112 | bytes 3162112 | tf_op jit(solution)/shard_map/pallas_call | solution.py:538
  12.7 0.0 collective-permute-done.2.inside_in
  12.7 2.9 %collective-permute-done.3.across_in = f32[128,128]{1,0:T(8,128)S(1)} collective-permute-done((f32[128,128]{1,0:T(8,128)S(1)}, f32[128,128]{1,0:T(8,128)S(1)}, u32[]{:S(2)}, u32[]{:S(2)}) %collective-permute-start.3) | collective-permute-done | bytes 65568 | tf_op jit(solution)/shard_map/ppermute | solution.py:566
  15.6 1.0 %shard_map.133 = (f32[2,192,128]{2,1,0:T(8,128)S(1)}, f32[2,192,128]{2,1,0:T(8,128)S(1)}, f32[128,128]{1,0:T(8,128)S(1)}) custom-call(f32[2,192,128]{2,1,0:T(8,128)S(1)} %get-tuple-element.55.end_e.start_e, f32[2,192,128]{2,1,0:T(8,128)S(1)} %get-tuple-element.56.next_h.lone_h1, f32[2,192,128]{2,1,0:T(8,128)S(1)} %get-tuple-element.57.next_e.lone_e1, ...), custom_call_target="tpu_custom_call" | custom-call | flops 2564096 | bytes 2564096 | tf_op jit(solution)/shard_map/pallas_call | solution.py:538
  16.6 12.5 %all_to_all.11 = f32[8,16,128]{2,1,0:T(8,128)S(1)} all-to-all(f32[8,16,128]{2,1,0:T(8,128)S(1)} %bitcast.15), channel_id=1, replica_groups=mesh['exc'=8,'space'=4] {'exc'}, dimensions={0} | all-to-all | bytes 131072 | tf_op jit(solution)/shard_map/all_to_all | solution.py:634
  29.2 0.9 %shard_map.134 = (f32[192,256]{1,0:T(8,128)}, f32[192,256]{1,0:T(8,128)}, f32[16,64]{1,0:T(8,128)}, f32[16,64]{1,0:T(8,128)}) custom-call(f32[128,128]{1,0:T(8,128)S(1)} %bitcast.14, f32[2,192,128]{2,1,0:T(8,128)S(1)} %get-tuple-element.70.e, f32[2,192,128]{2,1,0:T(8,128)S(1)} %get-tuple-element.71.h), custom_call_target="tpu_custom_call" | custom-call | flops 860160 | bytes 860160 | tf_op jit(solution)/shard_map/pallas_call | solution.py:538
Async XLA Ops:
  2.6 6.0 %collective-permute-start = (f32[200,128]{1,0:T(8,128)S(1)}, f32[200,128]{1,0:T(8,128)S(1)}, u32[]{:S(2)}, u32[]{:S(2)}) collective-permute-start(f32[200,128]{1,0:T(8,128)S(1)} %get-tuple-element.53), channel_id=1, source_target_pairs={{1,2},{2,1},{5,6},{6,5},{9,10},{10,9},{13,14},{14,13},{17,18},{18,... | collective-permute-start | bytes 307208 | tf_op jit(solution)/shard_map/ppermute | solution.py:566
  4.5 4.1 %collective-permute-start.1 = (f32[200,128]{1,0:T(8,128)S(1)}, f32[200,128]{1,0:T(8,128)S(1)}, u32[]{:S(2)}, u32[]{:S(2)}) collective-permute-start(f32[200,128]{1,0:T(8,128)S(1)} %get-tuple-element.54), channel_id=1, source_target_pairs={{0,1},{2,3},{1,0},{3,2},{4,5},{6,7},{5,4},{7,6},{8,9},{10,11},{9,8... | collective-permute-start | bytes 307208 | tf_op jit(solution)/shard_map/ppermute | solution.py:568
  8.6 3.4 %copy-start = (bf16[1,5,192,256]{3,2,1,0:T(8,128)(2,1)S(1)}, bf16[1,5,192,256]{3,2,1,0:T(8,128)(2,1)}, u32[]{:S(2)}) copy-start(bf16[1,5,192,256]{3,2,1,0:T(8,128)(2,1)} %param.13) | copy-start | bytes 1474564
  10.0 2.7 %collective-permute-start.2 = (f32[128,128]{1,0:T(8,128)S(1)}, f32[128,128]{1,0:T(8,128)S(1)}, u32[]{:S(2)}, u32[]{:S(2)}) collective-permute-start(f32[128,128]{1,0:T(8,128)S(1)} %get-tuple-element.65), channel_id=1, source_target_pairs={{0,1},{2,3},{1,0},{3,2},{4,5},{6,7},{5,4},{7,6},{8,9},{10,11},{9,8... | collective-permute-start | bytes 196616 | tf_op jit(solution)/shard_map/ppermute | solution.py:565
  10.0 5.6 %collective-permute-start.3 = (f32[128,128]{1,0:T(8,128)S(1)}, f32[128,128]{1,0:T(8,128)S(1)}, u32[]{:S(2)}, u32[]{:S(2)}) collective-permute-start(f32[128,128]{1,0:T(8,128)S(1)} %get-tuple-element.66), channel_id=1, source_target_pairs={{1,2},{2,1},{5,6},{6,5},{9,10},{10,9},{13,14},{14,13},{17,18},{18,... | collective-permute-start | bytes 196616 | tf_op jit(solution)/shard_map/ppermute | solution.py:566

commit v8 on v7

--- a/solution.py
+++ b/solution.py
@@ -24,7 +24,7 @@
 H_SECOND = 96
 SECOND = 128
 V_NEAR = 128
-N_NEAR = V_NEAR + NODES
+N_NEAR = V_NEAR + 32
 FIRST = N_NEAR + 8
 
 A1, L0, L1, B1 = range(4)
@@ -123,7 +123,7 @@
     target[layer, rows, :] += (-scale * parity(2, face, 1)) * y
 
 
-def add_x(target, field, layer, scale, outer, base=None):
+def add_x(target, field, layer, scale, outer, base=None, ends=None):
     for c, other, sign in ((1, 2, 1.0), (2, 1, -1.0)):
         parts = [field[layer, BASE[other] + 16 * i : BASE[other] + 16 * i + 16, :] for i in range(4)]
         for i in range(4):
@@ -133,14 +133,17 @@
             if traces is not None:
                 change += (-scale * parity(c, face, other)) * traces[other - 1]
             rows = slice(BASE[c] + 16 * i, BASE[c] + 16 * i + 16)
-            before = target[layer, rows, :] if base is None else base[rows]
-            target[layer, rows, :] = before + change
+            if ends is None:
+                change += target[layer, rows, :] if base is None else base[rows]
+            elif ends[0] == i:
+                change += ends[c]
+            target[layer, rows, :] = change
     if base is not None:
         rows = slice(BASE[0], BASE[0] + NODES)
         target[layer, rows, :] = base[rows]
 
 
-def add_yz(target, field, layer, index, scale):
+def add_yz(target, field, layer, index, scale, fresh=False):
     for c, other, sign in ((0, 1, 1.0), (1, 0, -1.0)):
         parts = [field[layer, pl.ds(BASE[other] + k, 16, stride=4), :] for k in range(4)]
         for k in range(4):
@@ -149,7 +152,11 @@
                 face = 4 if k == 0 else 5
                 got = picked(parts[3 - k], index(layer, face))
                 change += (-scale * parity(c, face, other)) * got
-            target[layer, pl.ds(BASE[c] + k, 16, stride=4), :] += change
+            rows = pl.ds(BASE[c] + k, 16, stride=4)
+            if fresh and c == 0:
+                target[layer, rows, :] = change
+            else:
+                target[layer, rows, :] += change
     sign = jnp.where(lax.broadcasted_iota(jnp.int32, (8, LAYER), 0) < 4, -1.0, 1.0)
     for k in range(4):
         parts = [field[layer, pl.ds(BASE[0] + 4 * j + k, 8, stride=16), :] for j in range(4)]
@@ -195,14 +202,11 @@
     add_end(target, field, layer, i, index, scale, False)
 
 
-def add_from_end(target, field, layer, i, index, scale):
-    for c, other, sign in ((1, 2, 1.0), (2, 1, -1.0)):
-        part = field[layer, BASE[other] + 16 * i : BASE[other] + 16 * i + 16, :]
-        for n in range(4):
-            if n != i:
-                rows = slice(BASE[c] + 16 * n, BASE[c] + 16 * n + 16)
-                target[layer, rows, :] += (scale * sign * SLOPES[n][i]) * part
-    add_end(target, field, layer, i, index, scale, True)
+def passed_back(v, i):
+    terms = [
+        (SLOPES[i][n] * SLOPES[n][i]) * v[16 * n : 16 * n + 16] for n in range(4) if n != i
+    ]
+    return terms[0] + terms[1] + terms[2]
 
 
 def layers_of(x):
@@ -251,58 +255,94 @@
     return [jnp.concatenate(sum(traces, []), axis=0) for traces in zip(*found)]
 
 
-def respond(index, valid, fe, fh, acc, lone, v, w, v_near, sent_a, sent_b):
+def respond(index, valid, fe, fh, acc, lone, v, w, near_v, sent_a, sent_b):
     start_e, lone_h1, lone_e1 = lone
-    own, wide = (L0, L1), (A1, L0, L1, B1)
-    sides = ((A1, 1, L0, sent_a), (B1, 0, L1, sent_b))
-    blank = jnp.zeros((ROWS, LAYER), F32)
-
-    def inward(target, field, scale, start, answered=True):
-        for side, (near, face, layer, sent) in enumerate(sides):
-            traces = [sent[start + 16 * t : start + 16 * t + 16, :] for t in range(2)]
-            if answered:
-                traces = [a + b for a, b in zip(traces, x_traces(field, near, face))]
-            mask = jnp.concatenate([valid[side]] * 2, axis=0)
-            got = [picked(t, index(layer, face ^ 1)) * mask for t in traces]
-            lift_x(target, layer, face ^ 1, scale, *got)
-
-    def outward(target, field, alone, scale, answered=True):
-        for near, face, layer, _ in sides:
-            traces = x_traces(alone, layer - L0, face ^ 1)
-            if answered:
-                traces = [a + b for a, b in zip(traces, x_traces(field, layer, face ^ 1))]
-            got = [picked(t, index(near, face)) for t in traces]
-            lift_x(target, near, face, scale, *got)
-
-    for layer in wide:
-        fh[layer] = blank
-        acc[layer] = blank
-    inward(fh, fe, TIME_STEP, E_START, False)
-    outward(fh, fe, start_e, TIME_STEP, False)
-
-    inward(acc, fh, 1.0, H_FIRST)
-    outward(acc, fh, lone_h1, 1.0)
-    first_e = []
-    for layer, scale in zip(wide, [v_near[0], v[0], v[1], v_near[1]]):
-        add_from_end(acc, fh, layer, 3 if layer in (A1, L1) else 0, index, 1.0)
-        first_e.append(-TIME_STEP * thrice(scale) * acc[layer])
-        fe[layer] = first_e[-1]
-
-    inward(fh, fe, TIME_STEP, E_FIRST)
-    outward(fh, fe, lone_e1, TIME_STEP)
-    for near, face, _, _ in sides:
-        add_into_end(fh, fe, near, at_end(face), index, TIME_STEP)
-    lone_h(index, fe, fh)
-
-    current = [TIME_STEP * thrice(w[i]) * first_e[1 + i] for i in range(2)]
-    second_e = []
+    own = (L0, L1)
+    sides = ((A1, 1, L0, 0), (B1, 0, L1, 1))
+    sent = (sent_a, sent_b)
+    empty = jnp.zeros((16, LAYER), F32)
+
+    def rows_at(c, i):
+        return slice(BASE[c] + 16 * i, BASE[c] + 16 * i + 16)
+
+    def lifted(face, scale, y, z):
+        return (-scale * parity(1, face, 2)) * z, (-scale * parity(2, face, 1)) * y
+
+    def inward(side, start, scale, answers=None):
+        near, _, layer, face = sides[side]
+        traces = [sent[side][start + 16 * t : start + 16 * t + 16, :] for t in range(2)]
+        if answers is not None:
+            traces = [a + b for a, b in zip(traces, answers)]
+        mask = jnp.concatenate([valid[side]] * 2, axis=0)
+        return lifted(face, scale, *[picked(t, index(layer, face)) * mask for t in traces])
+
+    def outward(side, alone, scale, answers=None):
+        near, face, layer, own_face = sides[side]
+        traces = x_traces(alone, layer - L0, own_face)
+        if answers is not None:
+            traces = [a + b for a, b in zip(traces, answers)]
+        return lifted(face, scale, *[picked(t, index(near, face)) for t in traces])
+
+    def put(target, layer, i, pair):
+        target[layer, rows_at(1, i), :] = pair[0]
+        target[layer, rows_at(2, i), :] = pair[1]
+
+    def add(target, layer, i, pair):
+        target[layer, rows_at(1, i), :] += pair[0]
+        target[layer, rows_at(2, i), :] += pair[1]
+
+    near_h, own_h = [], []
+    for side, (near, face, layer, own_face) in enumerate(sides):
+        near_h.append(outward(side, start_e, TIME_STEP))
+        own_h.append(inward(side, E_START, TIME_STEP))
+        put(fh, near, at_end(face), near_h[side])
+        put(fh, layer, at_end(own_face), own_h[side])
+
+    for side, (near, face, layer, own_face) in enumerate(sides):
+        i = at_end(face)
+        pair = outward(side, lone_h1, 1.0, own_h[side])
+        acc[near, rows_at(0, i), :] = empty
+        add_end(acc, fh, near, i, index, 1.0, True)
+        scale = -TIME_STEP * near_v[side, 0:16, :]
+        put(fe, near, i, [scale * part for part in pair])
+        fe[near, rows_at(0, i), :] = scale * acc[near, rows_at(0, i), :]
+
+        i = at_end(own_face)
+        pair = inward(side, H_FIRST, 1.0, near_h[side])
+        acc[layer, rows_at(0, i), :] = empty
+        add_end(acc, fh, layer, i, index, 1.0, True)
+        for n in range(4):
+            scale = -TIME_STEP * v[side, 16 * n : 16 * n + 16, :]
+            if n == i:
+                put(fe, layer, n, [scale * part for part in pair])
+                fe[layer, rows_at(0, n), :] = scale * acc[layer, rows_at(0, n), :]
+            else:
+                y, z = own_h[side]
+                put(fe, layer, n, [scale * (SLOPES[n][i] * z), scale * (-SLOPES[n][i] * y)])
+                fe[layer, rows_at(0, n), :] = empty
+
+    for side, (near, face, layer, own_face) in enumerate(sides):
+        i = at_end(face)
+        pair = outward(side, lone_e1, TIME_STEP, x_traces(fe, layer, own_face))
+        back = 1.0 + TIME_STEP * TIME_STEP * near_v[side, 16:32, :]
+        put(fh, near, i, [a + back * b for a, b in zip(pair, near_h[side])])
+        add_end(fh, fe, near, i, index, TIME_STEP, False)
+        ends = (at_end(own_face), *own_h[side])
+        add_x(fh, fe, layer, TIME_STEP, between(fe, index, layer), None, ends)
+        add_yz(fh, fe, layer, index, TIME_STEP, True)
+        i = at_end(own_face)
+        add(fh, layer, i, inward(side, E_FIRST, TIME_STEP, x_traces(fe, near, face)))
+
+    current, second_e = [], []
     for i, layer in enumerate(own):
+        current.append(TIME_STEP * thrice(w[i]) * fe[layer])
         add_x(acc, fh, layer, 1.0, between(fh, index, layer), current[i])
         add_yz(acc, fh, layer, index, 1.0)
-    inward(acc, fh, 1.0, H_SECOND)
-    for i, layer in enumerate(own):
-        second_e.append(first_e[1 + i] - TIME_STEP * thrice(v[i]) * acc[layer])
-    return first_e[1:3], [fh[layer] for layer in own], second_e, current
+    for side, (near, face, layer, own_face) in enumerate(sides):
+        i = at_end(own_face)
+        add(acc, layer, i, inward(side, H_SECOND, 1.0, x_traces(fh, near, face)))
+        second_e.append(fe[layer] - TIME_STEP * thrice(v[side]) * acc[layer])
+    return second_e, current
 
 
 def odd_rank():
@@ -374,7 +414,8 @@
 
     up, down = lonely(own_index(places), fe, fh, acc, drive, v, lone_h1, lone_e1)
     send(across, inside, 0, up, down)
-    send(across, inside, V_NEAR, v[1], v[0])
+    send(across, inside, V_NEAR, scale[1][48:NODES], scale[0][0:16])
+    send(across, inside, V_NEAR + 16, passed_back(scale[1], 3), passed_back(scale[0], 0))
     blank = jnp.zeros((2, LAYER), F32)
     place = place.astype(F32)
     send(
@@ -431,27 +472,27 @@
     start_e, lone_h1, lone_e1, lone_h2, lone_e2, lone_j2, v, w, source, places,
     valid, across_in, inside_in, *rest
 ):
-    end_e, next_h, next_e, next_j, answer_e, answer_j, v_near, near_places = rest[:8]
+    end_e, next_h, next_e, next_j, answer_e, answer_j, near_v, near_places = rest[:8]
     inside, across = rest[8:10]
     fe, fh, acc, sent_a, sent_b = rest[10:]
     sides_of(across_in, inside_in, sent_a, sent_b, FIRST)
     for side, sent in enumerate((sent_a, sent_b)):
-        v_near[side] = sent[V_NEAR : V_NEAR + NODES, :]
+        near_v[side] = sent[V_NEAR : V_NEAR + 32, :]
         place = sent[N_NEAR : N_NEAR + 8, :].astype(jnp.int32)
         for face in range(6):
             near_places[6 * side + face] = jnp.broadcast_to(place[face : face + 1], (8, LAYER))
     index = index_of(places, near_places)
-    first_e, magnetic, second_e, current = respond(
-        index, valid, fe, fh, acc, (start_e, lone_h1, lone_e1), v, w, v_near, sent_a, sent_b
+    second_e, current = respond(
+        index, valid, fe, fh, acc, (start_e, lone_h1, lone_e1), v, w, near_v, sent_a, sent_b
     )
     drive = []
     for i in range(2):
-        answer_e[i] = first_e[i]
+        answer_e[i] = fe[L0 + i]
         answer_j[i] = current[i]
         electric = lone_e2[i] + second_e[i]
         end_e[i] = electric
         fe[L0 + i] = electric
-        fh[L0 + i] = lone_h2[i] + magnetic[i]
+        fh[L0 + i] += lone_h2[i]
         before = lone_j2[i] + current[i]
         now = KEEP * before + TIME_STEP * thrice(w[i]) * electric
         next_j[i] = now
@@ -464,7 +505,7 @@
     lone_e1, answer_e, lone_j1, lone_j2, answer_j, end_e, next_h, next_e, next_j, v, w,
     source, places, levels, *rest
 ):
-    last_h, last_e, out, fe, fh, acc = rest
+    last_h, last_e, out, changes, fe, fh, acc = rest
     current = second_lone_step(next_h, next_e, next_j, v, w, source, places, (fe, fh, acc))
     for i in range(2):
         electric = fe[L0 + i]
@@ -479,27 +520,29 @@
         drude += next_j[i] * level[2] + current[i] * level[3]
         out[0:NODES, columns] = folded(eps)
         out[NODES : 2 * NODES, columns] = folded(drude)
+        changes[0, i] = level[3] - level[2]
+        changes[1, i] = level[4] - level[3]
+        changes[2, i] = level[3]
 
 
 def last_kernel(
-    start_e, lone_h1, lone_e1, lone_h2, lone_e2, v, w, places, valid, v_near, near_places,
-    inside_in, across_in, levels, early, pixels, *rest
+    start_e, lone_h1, lone_e1, lone_h2, lone_e2, v, w, places, valid, near_v, near_places,
+    inside_in, across_in, changes, early, pixels, *rest
 ):
     out_e, out_h, sums = rest[:3]
     fe, fh, acc, sent_a, sent_b = rest[3:]
     sides_of(across_in, inside_in, sent_a, sent_b, SECOND)
-    first_e, magnetic, second_e, current = respond(
+    second_e, current = respond(
         index_of(places, near_places), valid, fe, fh, acc, (start_e, lone_h1, lone_e1),
-        v, w, v_near, sent_a, sent_b,
+        v, w, near_v, sent_a, sent_b,
     )
     parts = []
     for i in range(2):
         out_e[i] = lone_e2[i] + second_e[i]
-        out_h[i] = lone_h2[i] + magnetic[i]
+        out_h[i] = lone_h2[i] + fh[L0 + i]
+        eps = folded(fe[L0 + i] * changes[0, i] + second_e[i] * changes[1, i])
+        drude = folded(current[i] * changes[2, i])
         columns = slice(i * LAYER, (i + 1) * LAYER)
-        start, middle, end = (stored(levels[k, :, columns].astype(F32)) for k in range(2, 5))
-        eps = folded(first_e[i] * (middle - start) + second_e[i] * (end - middle))
-        drude = folded(current[i] * middle)
         parts.append(jnp.concatenate([eps, drude], axis=0) + early[:, columns])
     both = jnp.concatenate(parts, axis=1)
     high, low = halves(both)
@@ -611,24 +654,24 @@
         [h1, e1, j1, v, w, source, places, design],
         work,
     )
-    end_e, h3, e3, j3, answer_e, answer_j, v_near, near_places, inside, across = call(
+    end_e, h3, e3, j3, answer_e, answer_j, near_v, near_places, inside, across = call(
         middle_kernel,
-        [field] * 6 + [nodal, indices] + [f32(SECOND, LAYER)] * 2,
+        [field] * 6 + [f32(2, 32, LAYER), indices] + [f32(SECOND, LAYER)] * 2,
         [start_e, h1, e1, h2, e2, j2, v, w, source, places, valid, across, inside],
         work + received,
     )
     across, inside = exchange(across, inside, True)
-    h4, e4, early = call(
+    h4, e4, early, changes = call(
         early_kernel,
-        [field] * 2 + [f32(2 * NODES, count)],
+        [field] * 2 + [f32(2 * NODES, count), f32(3, 2, ROWS, LAYER)],
         [e1, answer_e, j1, j2, answer_j, end_e, h3, e3, j3, v, w, source, places, levels],
         work,
     )
     e4, h4, sums = call(
         last_kernel,
         [field, field, f32(PIX_DEV, 2 * NODES)],
-        [end_e, h3, e3, h4, e4, v, w, places, valid, v_near, near_places]
-        + [inside, across, levels, early, pixels],
+        [end_e, h3, e3, h4, e4, v, w, places, valid, near_v, near_places]
+        + [inside, across, changes, early, pixels],
         work + [pltpu.VMEM((SECOND, LAYER), F32)] * 2,
     )
     parts = lax.all_to_all(sums, "exc", split_axis=0, concat_axis=0, tiled=True)

time: 30.3 us -> 30 us (0.990)
  no operation moved by 1% of the time
where the time goes in v8:
time: 30 us; the launch traced here: 29.8 us
  blocking collectives  12.5 us (42%)
  Pallas kernels  6.36 us (21%)
  waiting for transfers between devices  6.2 us (21%)
  starting transfers between devices  3.98 us (13%)
  between operations  0.72 us (2%)
    all_to_all x1, blocking collectives, local(): parts = lax.all_to_all(sums, 'exc', split_axis=0, concat_axis=0, tiled=True)  12.5 us
    pallas_call x6, Pallas kernels, call(): pl.pallas_call(kernel, out_shape=outs, in_specs=[pl.BlockSpec(memory_spac...  6.36 us
    ppermute x2, waiting for transfers between devices, exchange(): across = lax.ppermute(across, 'space', pairs(1))  6.19 us
    ppermute x2, starting transfers between devices, exchange(): across = lax.ppermute(across, 'space', pairs(1))  3.84 us
  transfers between devices with their start and end apart: 4, of which 2 were waited for; matrix products, arithmetic and copies ran while one was open for 0% of the time, Pallas kernels for 4%

profile of v8, /device:TPU:2, one launch (start us, length us, event | category | flops | bytes accessed | tf_op | source)
XLA Modules:
  0.0 29.8 jit_solution(7889310085395707805)
XLA Ops:
  0.6 2.0 %shard_map.129 = (s32[1,256]{1,0:T(1,128)S(1)}, f32[2,192,128]{2,1,0:T(8,128)S(1)}, f32[2,192,128]{2,1,0:T(8,128)S(1)}, f32[2,192,128]{2,1,0:T(8,128)S(1)}, f32[...) custom-call(f32[192,256]{1,0:T(8,128)} %bitcast.15, ...), custom_call_target="tpu_custom_call" | custom-call | flops 2171392 | bytes 2171392 | tf_op jit(solution)/shard_map/pallas_call | solution.py:581
  2.6 1.9 %collective-permute-start = (f32[168,128]{1,0:T(8,128)S(1)}, f32[168,128]{1,0:T(8,128)S(1)}, u32[]{:S(2)}, u32[]{:S(2)}) collective-permute-start(f32[168,128]{1,0:T(8,128)S(1)} %get-tuple-element.54), channel_id=1, source_target_pairs={{1,2},{2,1},{5,6},{6,5},{9,10},{10,9},{13,14},{14,13},{17,18},{18,... | collective-permute-start | bytes 258056 | tf_op jit(solution)/shard_map/ppermute | solution.py:609
  4.5 0.1 collective-permute-start.1
  4.6 0.5 %shard_map.130 = (f32[2,192,128]{2,1,0:T(8,128)S(1)}, f32[2,192,128]{2,1,0:T(8,128)S(1)}, f32[2,192,128]{2,1,0:T(8,128)S(1)}, bf16[128,256]{1,0:T(8,128)(2,1)S(1)}) custom-call(f32[2,192,128]{2,1,0:T(8,128)S(1)} %get-tuple-element.42.lone_h1, f32[2,192,128]{2,1,0:T(8,128)S(1)} %get-tuple-element.43.lone_e1, ...), custom_call_target="tpu_custom_call" | custom-call | flops 1688576 | bytes 1688576 | tf_op jit(solution)/shard_map/pallas_call | solution.py:581
  5.1 3.3 %collective-permute-done.across_in = f32[168,128]{1,0:T(8,128)S(1)} collective-permute-done((f32[168,128]{1,0:T(8,128)S(1)}, f32[168,128]{1,0:T(8,128)S(1)}, u32[]{:S(2)}, u32[]{:S(2)}) %collective-permute-start) | collective-permute-done | bytes 86048 | tf_op jit(solution)/shard_map/ppermute | solution.py:609
  8.4 0.0 collective-permute-done.1.inside_in
  8.4 0.0 copy-start
  8.4 1.4 %shard_map.131 = (f32[2,192,128]{2,1,0:T(8,128)S(1)}, f32[2,192,128]{2,1,0:T(8,128)S(1)}, f32[2,192,128]{2,1,0:T(8,128)S(1)}, f32[2,192,128]{2,1,0:T(8,128)S(1)}...) custom-call(f32[2,192,128]{2,1,0:T(8,128)S(1)} %get-tuple-element.41, ...), custom_call_target="tpu_custom_call" | custom-call | flops 3129344 | bytes 3129344 | tf_op jit(solution)/shard_map/pallas_call | solution.py:581
  9.8 0.1 collective-permute-start.2
  9.8 1.9 %collective-permute-start.3 = (f32[128,128]{1,0:T(8,128)S(1)}, f32[128,128]{1,0:T(8,128)S(1)}, u32[]{:S(2)}, u32[]{:S(2)}) collective-permute-start(f32[128,128]{1,0:T(8,128)S(1)} %get-tuple-element.67), channel_id=1, source_target_pairs={{1,2},{2,1},{5,6},{6,5},{9,10},{10,9},{13,14},{14,13},{17,18},{18,... | collective-permute-start | bytes 196616 | tf_op jit(solution)/shard_map/ppermute | solution.py:609
  11.8 0.0 copy-done
  11.8 0.7 %shard_map.132 = (f32[2,192,128]{2,1,0:T(8,128)S(1)}, f32[2,192,128]{2,1,0:T(8,128)S(1)}, f32[128,256]{1,0:T(8,128)S(1)}, f32[3,2,192,128]{3,2,1,0:T(8,128)S(1)}) custom-call(f32[2,192,128]{2,1,0:T(8,128)S(1)} %get-tuple-element.43.lone_e1, f32[2,192,128]{2,1,0:T(8,128)S(1)} %get-tuple-element.59.answer_e, ...), custom_call_target="tpu_custom_call" | custom-call | flops 3751936 | bytes 3751936 | tf_op jit(solution)/shard_map/pallas_call | solution.py:581
  12.5 0.0 collective-permute-done.2.inside_in
  12.5 2.9 %collective-permute-done.3.across_in = f32[128,128]{1,0:T(8,128)S(1)} collective-permute-done((f32[128,128]{1,0:T(8,128)S(1)}, f32[128,128]{1,0:T(8,128)S(1)}, u32[]{:S(2)}, u32[]{:S(2)}) %collective-permute-start.3) | collective-permute-done | bytes 65568 | tf_op jit(solution)/shard_map/ppermute | solution.py:609
  15.4 1.0 %shard_map.133 = (f32[2,192,128]{2,1,0:T(8,128)S(1)}, f32[2,192,128]{2,1,0:T(8,128)S(1)}, f32[128,128]{1,0:T(8,128)S(1)}) custom-call(f32[2,192,128]{2,1,0:T(8,128)S(1)} %get-tuple-element.56.end_e.start_e, f32[2,192,128]{2,1,0:T(8,128)S(1)} %get-tuple-element.57.next_h.lone_h1, f32[2,192,128]{2,1,0:T(8,128)S(1)} %get-tuple-element.58.next_e.lone_e1, ...), custom_call_target="tpu_custom_call" | custom-call | flops 2629632 | bytes 2629632 | tf_op jit(solution)/shard_map/pallas_call | solution.py:581
  16.4 12.5 %all_to_all.11 = f32[8,16,128]{2,1,0:T(8,128)S(1)} all-to-all(f32[8,16,128]{2,1,0:T(8,128)S(1)} %bitcast.14), channel_id=1, replica_groups=mesh['exc'=8,'space'=4] {'exc'}, dimensions={0} | all-to-all | bytes 131072 | tf_op jit(solution)/shard_map/all_to_all | solution.py:677
  28.9 0.9 %shard_map.134 = (f32[192,256]{1,0:T(8,128)}, f32[192,256]{1,0:T(8,128)}, f32[16,64]{1,0:T(8,128)}, f32[16,64]{1,0:T(8,128)}) custom-call(f32[128,128]{1,0:T(8,128)S(1)} %bitcast.13, f32[2,192,128]{2,1,0:T(8,128)S(1)} %get-tuple-element.72.e, f32[2,192,128]{2,1,0:T(8,128)S(1)} %get-tuple-element.73.h), custom_call_target="tpu_custom_call" | custom-call | flops 860160 | bytes 860160 | tf_op jit(solution)/shard_map/pallas_call | solution.py:581
Async XLA Ops:
  2.6 5.8 %collective-permute-start = (f32[168,128]{1,0:T(8,128)S(1)}, f32[168,128]{1,0:T(8,128)S(1)}, u32[]{:S(2)}, u32[]{:S(2)}) collective-permute-start(f32[168,128]{1,0:T(8,128)S(1)} %get-tuple-element.54), channel_id=1, source_target_pairs={{1,2},{2,1},{5,6},{6,5},{9,10},{10,9},{13,14},{14,13},{17,18},{18,... | collective-permute-start | bytes 258056 | tf_op jit(solution)/shard_map/ppermute | solution.py:609
  4.5 3.9 %collective-permute-start.1 = (f32[168,128]{1,0:T(8,128)S(1)}, f32[168,128]{1,0:T(8,128)S(1)}, u32[]{:S(2)}, u32[]{:S(2)}) collective-permute-start(f32[168,128]{1,0:T(8,128)S(1)} %get-tuple-element.55), channel_id=1, source_target_pairs={{0,1},{2,3},{1,0},{3,2},{4,5},{6,7},{5,4},{7,6},{8,9},{10,11},{9,8... | collective-permute-start | bytes 258056 | tf_op jit(solution)/shard_map/ppermute | solution.py:611
  8.4 3.4 %copy-start = (bf16[1,5,192,256]{3,2,1,0:T(8,128)(2,1)S(1)}, bf16[1,5,192,256]{3,2,1,0:T(8,128)(2,1)}, u32[]{:S(2)}) copy-start(bf16[1,5,192,256]{3,2,1,0:T(8,128)(2,1)} %param.13) | copy-start | bytes 1474564
  9.8 2.7 %collective-permute-start.2 = (f32[128,128]{1,0:T(8,128)S(1)}, f32[128,128]{1,0:T(8,128)S(1)}, u32[]{:S(2)}, u32[]{:S(2)}) collective-permute-start(f32[128,128]{1,0:T(8,128)S(1)} %get-tuple-element.66), channel_id=1, source_target_pairs={{0,1},{2,3},{1,0},{3,2},{4,5},{6,7},{5,4},{7,6},{8,9},{10,11},{9,8... | collective-permute-start | bytes 196616 | tf_op jit(solution)/shard_map/ppermute | solution.py:608
  9.8 5.6 %collective-permute-start.3 = (f32[128,128]{1,0:T(8,128)S(1)}, f32[128,128]{1,0:T(8,128)S(1)}, u32[]{:S(2)}, u32[]{:S(2)}) collective-permute-start(f32[128,128]{1,0:T(8,128)S(1)} %get-tuple-element.67), channel_id=1, source_target_pairs={{1,2},{2,1},{5,6},{6,5},{9,10},{10,9},{13,14},{14,13},{17,18},{18,... | collective-permute-start | bytes 196616 | tf_op jit(solution)/shard_map/ppermute | solution.py:609

commit v9 on v8

v9 whole, which is shorter than its diff:
```python
import functools

import jax
import jax.numpy as jnp
import numpy as np
from jax import lax
from jax.experimental import pallas as pl
from jax.experimental.pallas import tpu as pltpu
from jax.sharding import PartitionSpec as P

NODES = 64
ROWS = 3 * NODES
LAYER = 128
PIX_DEV = 128

TIME_STEP = 0.025
DAMPING = 0.5
KEEP = 1.0 - TIME_STEP * DAMPING

TANGENT = 32
E_START = 0
H_FIRST = 32
E_FIRST = 64
H_SECOND = 96
SECOND = 128
V_NEAR = 128
N_NEAR = V_NEAR + 32
FIRST = N_NEAR + 8

A1, L0, L1, B1 = range(4)

E_BASE = (NODES, 0, 2 * NODES)
H_BASE = (2 * NODES, 0, NODES)

BF16 = jnp.bfloat16
F32 = jnp.float32


def parity(c, face, other):
    d = face // 2
    sign = 1.0 if face % 2 else -1.0
    return 6.0 * sign * (c - d) * (d - other) * (other - c) / 2.0


def off_diagonal():
    points = np.array([-1.0, -1.0 / np.sqrt(5.0), 1.0 / np.sqrt(5.0), 1.0])
    barycentric = np.array(
        [1.0 / np.prod([points[j] - points[k] for k in range(4) if k != j]) for j in range(4)]
    )
    deriv = np.zeros((4, 4))
    for row in range(4):
        for column in range(4):
            if row != column:
                deriv[row, column] = (
                    barycentric[column] / barycentric[row] / (points[row] - points[column])
                )
    return (2.0 * deriv).tolist()


SLOPES = off_diagonal()


def slope(parts, row, scale):
    terms = [(scale * SLOPES[row][i]) * parts[i] for i in range(4) if i != row]
    return terms[0] + terms[1] + terms[2]


def halves(x):
    high = x.astype(BF16)
    return high, (x - high.astype(F32)).astype(BF16)


def dot_t(a, b):
    return lax.dot_general(a, b, (((1,), (1,)), ((), ())), preferred_element_type=F32)


def thrice(x):
    return jnp.concatenate([x, x, x], axis=0)


def folded(x):
    return x[0:NODES] + x[NODES : 2 * NODES] + x[2 * NODES : ROWS]


def stored(x, order=(1, 0, 2)):
    return jnp.concatenate([x[c * NODES : (c + 1) * NODES] for c in order], axis=0)


def one_hot(rows, targets):
    return (rows == targets).astype(F32).astype(BF16)


def picked(x, index):
    rows = x.shape[0]
    if rows < 8:
        index = index[0:rows]
    elif rows > 8:
        index = jnp.concatenate([index] * (rows // 8), axis=0)
    along = lax.GatherDimensionNumbers(
        offset_dims=(),
        collapsed_slice_dims=(1,),
        start_index_map=(1,),
        operand_batching_dims=(0,),
        start_indices_batching_dims=(0,),
    )
    mode = lax.GatherScatterMode.PROMISE_IN_BOUNDS
    return lax.gather(x, index[..., None], along, (1, 1), mode=mode)


def at_end(face):
    return 3 if face % 2 else 0


class Fields:
    def __init__(self, ref, base):
        self.ref, self.base = ref, base

    def rows(self, c, i, count=16):
        at = self.base[c] + 16 * i
        return slice(at, at + count)


def x_traces(field, layer, face):
    return [field.ref[layer, field.rows(c, at_end(face)), :] for c in (1, 2)]


def add_x(target, field, layer, scale, outer, base=None, ends=None):
    for c, other, sign in ((1, 2, 1.0), (2, 1, -1.0)):
        parts = [field.ref[layer, field.rows(other, i), :] for i in range(4)]
        for i in range(4):
            change = slope(parts, i, scale * sign)
            face = {0: 0, 3: 1}.get(i)
            traces = None if face is None else outer(face)
            if traces is not None:
                change += (-scale * parity(c, face, other)) * traces[other - 1]
            rows = target.rows(c, i)
            if ends is None:
                change += target.ref[layer, rows, :] if base is None else base[rows]
            elif ends[0] == i:
                change += ends[c]
            target.ref[layer, rows, :] = change
    if base is not None:
        rows = target.rows(0, 0, NODES)
        target.ref[layer, rows, :] = base[rows]


def add_yz(target, field, layer, index, scale, fresh=False):
    for c, other, sign in ((0, 1, 1.0), (1, 0, -1.0)):
        parts = [field.ref[layer, pl.ds(field.base[other] + k, 16, stride=4), :] for k in range(4)]
        for k in range(4):
            change = slope(parts, k, scale * sign)
            if k in (0, 3):
                face = 4 if k == 0 else 5
                got = picked(parts[3 - k], index(layer, face))
                change += (-scale * parity(c, face, other)) * got
            rows = pl.ds(target.base[c] + k, 16, stride=4)
            if fresh and c == 0:
                target.ref[layer, rows, :] = change
            else:
                target.ref[layer, rows, :] += change
    first = lax.broadcasted_iota(jnp.int32, (8, LAYER), 0) < 4
    sign = jnp.where(first, 1.0, -1.0) if field.base == E_BASE else jnp.where(first, -1.0, 1.0)
    for k in range(4):
        rows = [pl.ds(NODES + 4 * j + k, 8, stride=16) for j in range(4)]
        parts = [field.ref[layer, row, :] for row in rows]
        for j in range(4):
            change = slope(parts, j, scale)
            if j in (0, 3):
                face = 2 if j == 0 else 3
                got = picked(parts[3 - j], index(layer, face))
                change += (scale * parity(0, face, 2)) * got
            target.ref[layer, rows[j], :] += sign * change


def add_end(target, field, layer, i, index, scale, to_x):
    c, other, sign = (0, 1, 1.0) if to_x else (1, 0, -1.0)
    at = field.base[other] + 16 * i
    parts = [field.ref[layer, pl.ds(at + k, 4, stride=4), :] for k in range(4)]
    for k in range(4):
        change = slope(parts, k, scale * sign)
        if k in (0, 3):
            face = 4 if k == 0 else 5
            got = picked(parts[3 - k], index(layer, face))
            change += (-scale * parity(c, face, other)) * got
        target.ref[layer, pl.ds(target.base[c] + 16 * i + k, 4, stride=4), :] += change
    c, other, sign = (0, 2, -1.0) if to_x else (2, 0, 1.0)
    at = field.base[other] + 16 * i
    parts = [field.ref[layer, at + 4 * j : at + 4 * j + 4, :] for j in range(4)]
    for j in range(4):
        change = slope(parts, j, scale * sign)
        if j in (0, 3):
            face = 2 if j == 0 else 3
            got = picked(parts[3 - j], index(layer, face))
            change += (-scale * parity(c, face, other)) * got
        at = target.base[c] + 16 * i + 4 * j
        target.ref[layer, at : at + 4, :] += change


def add_into_end(target, field, layer, i, index, scale):
    for c, other, sign in ((1, 2, 1.0), (2, 1, -1.0)):
        parts = [field.ref[layer, field.rows(other, n), :] for n in range(4)]
        target.ref[layer, target.rows(c, i), :] += slope(parts, i, scale * sign)
    add_end(target, field, layer, i, index, scale, False)


def passed_back(v, i):
    terms = [
        (SLOPES[i][n] * SLOPES[n][i]) * v[16 * n : 16 * n + 16] for n in range(4) if n != i
    ]
    return terms[0] + terms[1] + terms[2]


def layers_of(x):
    return [x[:, at : at + LAYER] for at in range(0, x.shape[1], LAYER)]


def between(field, index, layer):
    def outer(face):
        if (layer, face) not in ((L0, 1), (L1, 0)):
            return None
        traces = x_traces(field, L0 + L1 - layer, face ^ 1)
        return [picked(t, index(layer, face)) for t in traces]

    return outer


def lone_h(index, fe, fh):
    for layer in (L0, L1):
        add_x(fh, fe, layer, TIME_STEP, between(fe, index, layer))
        add_yz(fh, fe, layer, index, TIME_STEP)


def lone_e(index, fe, fh, acc, drive, v):
    for i, layer in enumerate((L0, L1)):
        add_x(acc, fh, layer, 1.0, between(fh, index, layer), drive[i])
        add_yz(acc, fh, layer, index, 1.0)
        fe.ref[layer] -= TIME_STEP * thrice(v[i]) * acc.ref[layer]


def lonely(index, fe, fh, acc, drive, v, out_h, out_e):
    def ends_of(field):
        return x_traces(field, L1, 1), x_traces(field, L0, 0)

    found = [ends_of(fe)]
    lone_h(index, fe, fh)
    found.append(ends_of(fh))
    for i in range(2):
        out_h[i] = fh.ref[L0 + i]
    lone_e(index, fe, fh, acc, drive, v)
    found.append(ends_of(fe))
    for i in range(2):
        out_e[i] = fe.ref[L0 + i]
    for face, layer in enumerate((L0, L1)):
        add_into_end(fh, fe, layer, at_end(face), index, TIME_STEP)
    found.append(ends_of(fh))
    return [jnp.concatenate(sum(traces, []), axis=0) for traces in zip(*found)]


def respond(index, valid, fe, fh, acc, own_sent, v, w, near_v, sent_a, sent_b):
    own = (L0, L1)
    sides = ((A1, 1, L0, 0), (B1, 0, L1, 1))
    sent = (sent_a, sent_b)
    empty = jnp.zeros((16, LAYER), F32)

    def lifted(face, scale, y, z):
        return (-scale * parity(1, face, 2)) * z, (-scale * parity(2, face, 1)) * y

    def inward(side, start, scale, answers=None):
        near, _, layer, face = sides[side]
        traces = [sent[side][start + 16 * t : start + 16 * t + 16, :] for t in range(2)]
        if answers is not None:
            traces = [a + b for a, b in zip(traces, answers)]
        mask = jnp.concatenate([valid[side]] * 2, axis=0)
        return lifted(face, scale, *[picked(t, index(layer, face)) * mask for t in traces])

    def outward(side, start, scale, answers=None):
        near, face, layer, own_face = sides[side]
        traces = [own_sent[side, start + 16 * t : start + 16 * t + 16, :] for t in range(2)]
        if answers is not None:
            traces = [a + b for a, b in zip(traces, answers)]
        return lifted(face, scale, *[picked(t, index(near, face)) for t in traces])

    def put(target, layer, i, pair):
        target.ref[layer, target.rows(1, i), :] = pair[0]
        target.ref[layer, target.rows(2, i), :] = pair[1]

    def add(target, layer, i, pair):
        target.ref[layer, target.rows(1, i), :] += pair[0]
        target.ref[layer, target.rows(2, i), :] += pair[1]

    near_h, own_h = [], []
    for side, (near, face, layer, own_face) in enumerate(sides):
        near_h.append(outward(side, E_START, TIME_STEP))
        own_h.append(inward(side, E_START, TIME_STEP))
        put(fh, near, at_end(face), near_h[side])
        put(fh, layer, at_end(own_face), own_h[side])

    for side, (near, face, layer, own_face) in enumerate(sides):
        i = at_end(face)
        pair = outward(side, H_FIRST, 1.0, own_h[side])
        acc.ref[near, acc.rows(0, i), :] = empty
        add_end(acc, fh, near, i, index, 1.0, True)
        scale = -TIME_STEP * near_v[side, 0:16, :]
        put(fe, near, i, [scale * part for part in pair])
        fe.ref[near, fe.rows(0, i), :] = scale * acc.ref[near, acc.rows(0, i), :]

        i = at_end(own_face)
        pair = inward(side, H_FIRST, 1.0, near_h[side])
        acc.ref[layer, acc.rows(0, i), :] = empty
        add_end(acc, fh, layer, i, index, 1.0, True)
        for n in range(4):
            scale = -TIME_STEP * v[side][16 * n : 16 * n + 16]
            if n == i:
                put(fe, layer, n, [scale * part for part in pair])
                fe.ref[layer, fe.rows(0, n), :] = scale * acc.ref[layer, acc.rows(0, n), :]
            else:
                y, z = own_h[side]
                put(fe, layer, n, [scale * (SLOPES[n][i] * z), scale * (-SLOPES[n][i] * y)])
                fe.ref[layer, fe.rows(0, n), :] = empty

    for side, (near, face, layer, own_face) in enumerate(sides):
        i = at_end(face)
        pair = outward(side, E_FIRST, TIME_STEP, x_traces(fe, layer, own_face))
        back = 1.0 + TIME_STEP * TIME_STEP * near_v[side, 16:32, :]
        put(fh, near, i, [a + back * b for a, b in zip(pair, near_h[side])])
        add_end(fh, fe, near, i, index, TIME_STEP, False)
        ends = (at_end(own_face), *own_h[side])
        add_x(fh, fe, layer, TIME_STEP, between(fe, index, layer), None, ends)
        add_yz(fh, fe, layer, index, TIME_STEP, True)
        i = at_end(own_face)
        add(fh, layer, i, inward(side, E_FIRST, TIME_STEP, x_traces(fe, near, face)))

    current, second_e = [], []
    for i, layer in enumerate(own):
        current.append(TIME_STEP * thrice(w[i]) * fe.ref[layer])
        add_x(acc, fh, layer, 1.0, between(fh, index, layer), current[i])
        add_yz(acc, fh, layer, index, 1.0)
    for side, (near, face, layer, own_face) in enumerate(sides):
        i = at_end(own_face)
        add(acc, layer, i, inward(side, H_SECOND, 1.0, x_traces(fh, near, face)))
        second_e.append(fe.ref[layer] - TIME_STEP * thrice(v[side]) * acc.ref[layer])
    return second_e, current


def odd_rank():
    return lax.rem(lax.axis_index("space"), 2) == 1


def send(across, inside, at, up, down):
    odd = odd_rank()
    rows = slice(at, at + up.shape[0])
    across[rows, :] = jnp.where(odd, up, down)
    inside[rows, :] = jnp.where(odd, down, up)


def sides_of(across, inside, a, b, rows):
    odd = odd_rank()
    from_across, from_inside = across[0:rows, :], inside[0:rows, :]
    a[...] = jnp.where(odd, from_inside, from_across)
    b[...] = jnp.where(odd, from_across, from_inside)


def wrapped(fe, fh, acc):
    return Fields(fe, E_BASE), Fields(fh, H_BASE), Fields(acc, E_BASE)


def first_kernel(
    e_in, h_in, j_in, v_in, w_in, near_in, ports_in, profile_in, design_in, *rest
):
    design, v, w, lone_h1, lone_e1, first_j, source, places, valid, own_sent = rest[:10]
    across, inside, fe, fh, acc, neighbor, ports, profile, e, h, j, sems = rest[10:]
    fe, fh, acc = wrapped(fe, fh, acc)
    copies = []
    for origin, target in (
        (near_in, neighbor), (ports_in, ports), (profile_in, profile), (e_in, e), (h_in, h),
        (j_in, j), (w_in, w), (v_in, v), (design_in, design),
    ):
        copies.append(pltpu.make_async_copy(origin, target, sems.at[len(copies)]))
        copies[-1].start()
    for copy in copies:
        copy.wait()

    found = neighbor[...]
    place = jnp.where(found < 0, 0, jnp.bitwise_and(found, LAYER - 1))
    for i in range(2):
        columns = slice(i * LAYER, (i + 1) * LAYER)
        for face in range(6):
            places[6 * i + face] = jnp.broadcast_to(place[face : face + 1, columns], (8, LAYER))
        there = (found[i : i + 1, columns] >= 0).astype(F32)
        valid[i] = jnp.broadcast_to(there, (8, LAYER))
    electric = [stored(part) for part in layers_of(e[...])]
    magnetic = [stored(part, (1, 2, 0)) for part in layers_of(h[...])]
    current = [stored(part) for part in layers_of(j[...])]
    weight = layers_of(w[...])
    scale = layers_of(v[...])
    targets = lax.broadcasted_iota(jnp.int32, (2 * LAYER, ports.shape[1]), 0)
    spread_hot = one_hot(targets, jnp.bitwise_and(ports[...], 2 * LAYER - 1))
    high, low = halves(profile[...])
    spread = layers_of(dot_t(high, spread_hot) + dot_t(low, spread_hot))
    drive = []
    for i in range(2):
        fe.ref[L0 + i] = electric[i]
        fh.ref[L0 + i] = magnetic[i]
        source[i] = stored(spread[i])
        now = KEEP * current[i] + TIME_STEP * thrice(weight[i]) * electric[i]
        first_j[i] = now
        drive.append(now + source[i])

    up, down = lonely(own_index(places), fe, fh, acc, drive, scale, lone_h1, lone_e1)
    own_sent[0] = down
    own_sent[1] = up
    send(across, inside, 0, up, down)
    send(across, inside, V_NEAR, scale[1][48:NODES], scale[0][0:16])
    send(across, inside, V_NEAR + 16, passed_back(scale[1], 3), passed_back(scale[0], 0))
    blank = jnp.zeros((2, LAYER), F32)
    place = place.astype(F32)
    send(
        across,
        inside,
        N_NEAR,
        jnp.concatenate([place[:, LAYER : 2 * LAYER], blank], axis=0),
        jnp.concatenate([place[:, 0:LAYER], blank], axis=0),
    )


def own_index(places):
    def index(layer, face):
        return places[6 * (layer - L0) + face]

    return index


def index_of(places, near_places):
    def index(layer, face):
        if layer in (L0, L1):
            return places[6 * (layer - L0) + face]
        return near_places[6 * (layer == B1) + face]

    return index


def second_lone_step(lone_h1, lone_e1, first_j, v, w, source, places, work):
    fe, fh, acc = work
    index = own_index(places)
    current = []
    for i in range(2):
        electric = lone_e1[i]
        fe.ref[L0 + i] = electric
        fh.ref[L0 + i] = lone_h1[i]
        current.append(KEEP * first_j[i] + TIME_STEP * thrice(w[i]) * electric)
    lone_h(index, fe, fh)
    lone_e(index, fe, fh, acc, [current[i] + source[i] for i in range(2)], v)
    return current


def lone_kernel(lone_h1, lone_e1, first_j, v, w, source, places, design, *rest):
    lone_h2, lone_e2, lone_j2, pixels, *work = rest
    fe, fh, acc = wrapped(*work)
    pixel = jnp.bitwise_and(design[...], PIX_DEV - 1)
    pixels[...] = one_hot(lax.broadcasted_iota(jnp.int32, pixels.shape, 0), pixel)
    scale, weight = layers_of(v[...]), layers_of(w[...])
    current = second_lone_step(
        lone_h1, lone_e1, first_j, scale, weight, source, places, (fe, fh, acc)
    )
    for i in range(2):
        lone_h2[i] = fh.ref[L0 + i]
        lone_e2[i] = fe.ref[L0 + i]
        lone_j2[i] = current[i]


def middle_kernel(
    own_sent, lone_h2, lone_e2, lone_j2, v, w, source, places, valid, across_in, inside_in,
    *rest
):
    end_e, next_h, next_e, answer_e, own_next, near_v, near_places, across, inside = rest[:9]
    fe, fh, acc = wrapped(*rest[9:12])
    sent_a, sent_b = rest[12:]
    sides_of(across_in, inside_in, sent_a, sent_b, FIRST)
    for side, sent in enumerate((sent_a, sent_b)):
        near_v[side] = sent[V_NEAR : V_NEAR + 32, :]
        place = sent[N_NEAR : N_NEAR + 8, :].astype(jnp.int32)
        for face in range(6):
            near_places[6 * side + face] = jnp.broadcast_to(place[face : face + 1], (8, LAYER))
    index = index_of(places, near_places)
    scale, weight = layers_of(v[...]), layers_of(w[...])
    second_e, current = respond(
        index, valid, fe, fh, acc, own_sent, scale, weight, near_v, sent_a, sent_b
    )
    drive = []
    for i in range(2):
        answer_e[i] = fe.ref[L0 + i]
        electric = lone_e2[i] + second_e[i]
        end_e[i] = electric
        fe.ref[L0 + i] = electric
        fh.ref[L0 + i] += lone_h2[i]
        before = lone_j2[i] + current[i]
        now = KEEP * before + TIME_STEP * thrice(weight[i]) * electric
        drive.append(now + source[i])
    up, down = lonely(index, fe, fh, acc, drive, scale, next_h, next_e)
    own_next[0] = down
    own_next[1] = up
    send(across, inside, 0, up, down)


def early_kernel(
    lone_e1, answer_e, lone_j1, lone_j2, end_e, next_h, next_e, v, w, source, places, levels,
    *rest
):
    last_h, last_e, out, changes, *work = rest
    fe, fh, acc = wrapped(*work)
    scale, weight = layers_of(v[...]), layers_of(w[...])
    second_j, third_j = [], []
    for i in range(2):
        rise = TIME_STEP * thrice(weight[i])
        second_j.append(lone_j2[i] + rise * answer_e[i])
        third_j.append(KEEP * second_j[i] + rise * end_e[i])
    current = second_lone_step(
        next_h, next_e, third_j, scale, weight, source, places, (fe, fh, acc)
    )
    for i in range(2):
        electric = fe.ref[L0 + i]
        last_h[i] = fh.ref[L0 + i]
        last_e[i] = electric
        columns = slice(i * LAYER, (i + 1) * LAYER)
        level = [stored(levels[k, :, columns].astype(F32)) for k in range(5)]
        eps = (lone_e1[i] + answer_e[i]) * (level[1] - level[0])
        eps += end_e[i] * (level[2] - level[1]) + next_e[i] * (level[3] - level[2])
        eps += electric * (level[4] - level[3])
        drude = lone_j1[i] * level[0] + second_j[i] * level[1]
        drude += third_j[i] * level[2] + current[i] * level[3]
        out[0:NODES, columns] = folded(eps)
        out[NODES : 2 * NODES, columns] = folded(drude)
        changes[0, i] = level[3] - level[2]
        changes[1, i] = level[4] - level[3]
        changes[2, i] = level[3]


def last_kernel(
    own_sent, lone_h2, lone_e2, v, w, places, valid, near_v, near_places, inside_in, across_in,
    changes, early, pixels, *rest
):
    out_e, out_h, sums = rest[:3]
    fe, fh, acc = wrapped(*rest[3:6])
    sent_a, sent_b = rest[6:]
    sides_of(across_in, inside_in, sent_a, sent_b, SECOND)
    second_e, current = respond(
        index_of(places, near_places), valid, fe, fh, acc, own_sent,
        layers_of(v[...]), layers_of(w[...]), near_v, sent_a, sent_b,
    )
    parts = []
    for i in range(2):
        out_e[i] = lone_e2[i] + second_e[i]
        out_h[i] = lone_h2[i] + fh.ref[L0 + i]
        eps = folded(fe.ref[L0 + i] * changes[0, i] + second_e[i] * changes[1, i])
        drude = folded(current[i] * changes[2, i])
        columns = slice(i * LAYER, (i + 1) * LAYER)
        parts.append(jnp.concatenate([eps, drude], axis=0) + early[:, columns])
    both = jnp.concatenate(parts, axis=1)
    high, low = halves(both)
    sums[...] = dot_t(pixels[...], high) + dot_t(pixels[...], low)


def total_kernel(owners, parts, e, h, out_e, out_h, eps, drude, sums, sems):
    copies = []

    def write(origin, target):
        copies.append(pltpu.make_async_copy(origin, target, sems.at[len(copies)]))
        copies[-1].start()

    for field, base, target in ((e, E_BASE, out_e), (h, H_BASE, out_h)):
        for i in range(2):
            for c in range(3):
                there = target.at[pl.ds(c * NODES, NODES), pl.ds(i * LAYER, LAYER)]
                write(field.at[i, pl.ds(base[c], NODES), :], there)
    share = parts.shape[0] // owners
    total = parts[0:share]
    for owner in range(1, owners):
        total = total + parts[owner * share : (owner + 1) * share]
    total = total * (1.0 / owners)
    sums[0] = total[:, 0:NODES]
    sums[1] = total[:, NODES : 2 * NODES]
    write(sums.at[0], eps)
    write(sums.at[1], drude)
    for copy in copies:
        copy.wait()


def call(kernel, outs, args, scratch=(), spaces=None, out_spaces=None):
    moved = sum(4 * int(np.prod(o.shape)) for o in outs) + sum(
        a.dtype.itemsize * int(np.prod(a.shape)) for a in args
    )
    return pl.pallas_call(
        kernel,
        out_shape=outs,
        in_specs=[pl.BlockSpec(memory_space=s) for s in spaces or [pltpu.VMEM] * len(args)],
        out_specs=[pl.BlockSpec(memory_space=s) for s in out_spaces or [pltpu.VMEM] * len(outs)],
        scratch_shapes=list(scratch),
        compiler_params=pltpu.CompilerParams(vmem_limit_bytes=24 * 1024 * 1024),
        cost_estimate=pl.CostEstimate(flops=moved, bytes_accessed=moved, transcendentals=0),
    )(*args)


def f32(*shape):
    return jax.ShapeDtypeStruct(shape, F32)


def bf16(*shape):
    return jax.ShapeDtypeStruct(shape, BF16)


def exchange(across, inside, inside_first):
    size = lax.axis_size("space")

    def pairs(start):
        found = [(i, i + 1) for i in range(start, size - 1, 2)]
        return found + [(j, i) for i, j in found]

    if inside_first:
        inside = lax.ppermute(inside, "space", pairs(0))
    across = lax.ppermute(across, "space", pairs(1))
    if not inside_first:
        inside = lax.ppermute(inside, "space", pairs(0))
    return across, inside


def local(
    adj_e,
    adj_h,
    adj_j,
    fwd_e,
    inv_eps,
    drude_weight,
    neighbor,
    design_map,
    port_elems,
    port_profile,
):
    count = adj_e.shape[2]
    owners = lax.axis_size("exc")
    levels = fwd_e[0]
    field, nodal, sent = f32(2, ROWS, LAYER), f32(NODES, count), f32(2, SECOND, LAYER)
    indices = jax.ShapeDtypeStruct((12, 8, LAYER), jnp.int32)
    work = [pltpu.VMEM((4, ROWS, LAYER), F32)] * 3
    given = [adj_e[0], adj_h[0], adj_j[0], inv_eps, drude_weight]
    given += [neighbor, port_elems, port_profile[0], design_map.reshape(1, count)]
    design, v, w, h1, e1, j1, source, places, valid, own_sent, across, inside = call(
        first_kernel,
        [jax.ShapeDtypeStruct((1, count), jnp.int32), nodal, nodal]
        + [field] * 4
        + [indices, f32(2, 8, LAYER), sent]
        + [f32(FIRST, LAYER)] * 2,
        [pltpu.with_memory_space_constraint(a, pltpu.HBM) for a in given],
        work
        + [pltpu.VMEM(a.shape, a.dtype) for a in [neighbor, port_elems, port_profile[0]]]
        + [pltpu.VMEM((ROWS, count), F32)] * 3
        + [pltpu.SemaphoreType.DMA((9,))],
        spaces=[pltpu.HBM] * len(given),
    )
    across, inside = exchange(across, inside, False)
    h2, e2, j2, pixels = call(
        lone_kernel,
        [field] * 3 + [bf16(PIX_DEV, count)],
        [h1, e1, j1, v, w, source, places, design],
        work,
    )
    end_e, h3, e3, answer_e, own_sent, near_v, near_places, across, inside = call(
        middle_kernel,
        [field] * 4 + [sent, f32(2, 32, LAYER), indices] + [f32(SECOND, LAYER)] * 2,
        [own_sent, h2, e2, j2, v, w, source, places, valid, across, inside],
        work + [pltpu.VMEM((FIRST, LAYER), F32)] * 2,
    )
    across, inside = exchange(across, inside, True)
    h4, e4, early, changes = call(
        early_kernel,
        [field] * 2 + [f32(2 * NODES, count), f32(3, 2, ROWS, LAYER)],
        [e1, answer_e, j1, j2, end_e, h3, e3, v, w, source, places, levels],
        work,
    )
    e4, h4, sums = call(
        last_kernel,
        [field, field, f32(PIX_DEV, 2 * NODES)],
        [own_sent, h4, e4, v, w, places, valid, near_v, near_places]
        + [inside, across, changes, early, pixels],
        work + [pltpu.VMEM((SECOND, LAYER), F32)] * 2,
    )
    parts = lax.all_to_all(sums, "exc", split_axis=0, concat_axis=0, tiled=True)
    share = PIX_DEV // owners
    out_e, out_h, eps, drude = call(
        functools.partial(total_kernel, owners),
        [f32(ROWS, count)] * 2 + [f32(share, NODES)] * 2,
        [parts, e4, h4],
        [pltpu.VMEM((2, share, NODES), F32), pltpu.SemaphoreType.DMA((14,))],
        out_spaces=[pltpu.HBM] * 4,
    )
    return out_e[None], out_h[None], eps.T, drude.T


def solution(mesh):
    return jax.shard_map(
        local,
        mesh=mesh,
        in_specs=(
            P("exc", None, "space"),
            P("exc", None, "space"),
            P("exc", None, "space"),
            P("exc", None, None, "space"),
            P(None, "space"),
            P(None, "space"),
            P(None, "space"),
            P("space"),
            P("exc", "space"),
            P("exc", None, "space"),
        ),
        out_specs=(
            P("exc", None, "space"),
            P("exc", None, "space"),
            P(None, ("space", "exc")),
            P(None, ("space", "exc")),
        ),
        check_vma=False,
    )
```

time: 30 us -> 30.1 us (level)
  no operation moved by 1% of the time
where the time goes in v9:
time: 30.1 us; the launch traced here: 29.9 us
  blocking collectives  12.5 us (42%)
  Pallas kernels  6.51 us (22%)
  waiting for transfers between devices  6.11 us (20%)
  starting transfers between devices  3.98 us (13%)
  between operations  0.72 us (2%)
    all_to_all x1, blocking collectives, local(): parts = lax.all_to_all(sums, 'exc', split_axis=0, concat_axis=0, tiled=True)  12.5 us
    pallas_call x6, Pallas kernels, call(): pl.pallas_call(kernel, out_shape=outs, in_specs=[pl.BlockSpec(memory_spac...  6.51 us
    ppermute x2, waiting for transfers between devices, exchange(): across = lax.ppermute(across, 'space', pairs(1))  6.11 us
    ppermute x2, starting transfers between devices, exchange(): across = lax.ppermute(across, 'space', pairs(1))  3.84 us
  transfers between devices with their start and end apart: 4, of which 2 were waited for; matrix products, arithmetic and copies ran while one was open for 0% of the time, Pallas kernels for 4%

profile of v9, /device:TPU:2, one launch (start us, length us, event | category | flops | bytes accessed | tf_op | source)
XLA Modules:
  0.0 29.9 jit_solution(17151464368492583311)
XLA Ops:
  0.6 2.0 %shard_map.129 = (s32[1,256]{1,0:T(1,128)S(1)}, f32[64,256]{1,0:T(8,128)S(1)}, f32[64,256]{1,0:T(8,128)S(1)}, f32[2,192,128]{2,1,0:T(8,128)S(1)}, f32[2,192,128]...) custom-call(f32[192,256]{1,0:T(8,128)} %bitcast.15, ...), custom_call_target="tpu_custom_call" | custom-call | flops 2105856 | bytes 2105856 | tf_op jit(solution)/shard_map/pallas_call | solution.py:592
  2.6 1.9 %collective-permute-start = (f32[168,128]{1,0:T(8,128)S(1)}, f32[168,128]{1,0:T(8,128)S(1)}, u32[]{:S(2)}, u32[]{:S(2)}) collective-permute-start(f32[168,128]{1,0:T(8,128)S(1)} %get-tuple-element.53), channel_id=1, source_target_pairs={{1,2},{2,1},{5,6},{6,5},{9,10},{10,9},{13,14},{14,13},{17,18},{18,... | collective-permute-start | bytes 258056 | tf_op jit(solution)/shard_map/ppermute | solution.py:620
  4.5 0.1 collective-permute-start.1
  4.6 0.5 %shard_map.130 = (f32[2,192,128]{2,1,0:T(8,128)S(1)}, f32[2,192,128]{2,1,0:T(8,128)S(1)}, f32[2,192,128]{2,1,0:T(8,128)S(1)}, bf16[128,256]{1,0:T(8,128)(2,1)S(1)}) custom-call(f32[2,192,128]{2,1,0:T(8,128)S(1)} %get-tuple-element.41.lone_h1, f32[2,192,128]{2,1,0:T(8,128)S(1)} %get-tuple-element.42.lone_e1, ...), custom_call_target="tpu_custom_call" | custom-call | flops 1688576 | bytes 1688576 | tf_op jit(solution)/shard_map/pallas_call | solution.py:592
  5.1 3.3 %collective-permute-done.across_in = f32[168,128]{1,0:T(8,128)S(1)} collective-permute-done((f32[168,128]{1,0:T(8,128)S(1)}, f32[168,128]{1,0:T(8,128)S(1)}, u32[]{:S(2)}, u32[]{:S(2)}) %collective-permute-start) | collective-permute-done | bytes 86048 | tf_op jit(solution)/shard_map/ppermute | solution.py:620
  8.4 0.0 collective-permute-done.1.inside_in
  8.4 0.0 copy-start
  8.4 1.4 %shard_map.131 = (f32[2,192,128]{2,1,0:T(8,128)S(1)}, f32[2,192,128]{2,1,0:T(8,128)S(1)}, f32[2,192,128]{2,1,0:T(8,128)S(1)}, f32[2,192,128]{2,1,0:T(8,128)S(1)}...) custom-call(f32[2,128,128]{2,1,0:T(8,128)S(1)} %get-tuple-element.40, ...), custom_call_target="tpu_custom_call" | custom-call | flops 2408448 | bytes 2408448 | tf_op jit(solution)/shard_map/pallas_call | solution.py:592
  9.8 0.1 collective-permute-start.2
  9.9 1.9 %collective-permute-start.3 = (f32[128,128]{1,0:T(8,128)S(1)}, f32[128,128]{1,0:T(8,128)S(1)}, u32[]{:S(2)}, u32[]{:S(2)}) collective-permute-start(f32[128,128]{1,0:T(8,128)S(1)} %get-tuple-element.65), channel_id=1, source_target_pairs={{1,2},{2,1},{5,6},{6,5},{9,10},{10,9},{13,14},{14,13},{17,18},{18,... | collective-permute-start | bytes 196616 | tf_op jit(solution)/shard_map/ppermute | solution.py:620
  11.8 0.0 copy-done
  11.8 0.8 %shard_map.132 = (f32[2,192,128]{2,1,0:T(8,128)S(1)}, f32[2,192,128]{2,1,0:T(8,128)S(1)}, f32[128,256]{1,0:T(8,128)S(1)}, f32[3,2,192,128]{3,2,1,0:T(8,128)S(1)}) custom-call(f32[2,192,128]{2,1,0:T(8,128)S(1)} %get-tuple-element.42.lone_e1, f32[2,192,128]{2,1,0:T(8,128)S(1)} %get-tuple-element.56.answer_e, ...), custom_call_target="tpu_custom_call" | custom-call | flops 3358720 | bytes 3358720 | tf_op jit(solution)/shard_map/pallas_call | solution.py:592
  12.6 0.0 collective-permute-done.2.inside_in
  12.6 2.8 %collective-permute-done.3.across_in = f32[128,128]{1,0:T(8,128)S(1)} collective-permute-done((f32[128,128]{1,0:T(8,128)S(1)}, f32[128,128]{1,0:T(8,128)S(1)}, u32[]{:S(2)}, u32[]{:S(2)}) %collective-permute-start.3) | collective-permute-done | bytes 65568 | tf_op jit(solution)/shard_map/ppermute | solution.py:620
  15.5 1.0 %shard_map.133 = (f32[2,192,128]{2,1,0:T(8,128)S(1)}, f32[2,192,128]{2,1,0:T(8,128)S(1)}, f32[128,128]{1,0:T(8,128)S(1)}) custom-call(f32[2,128,128]{2,1,0:T(8,128)S(1)} %get-tuple-element.55.own_sent, f32[2,192,128]{2,1,0:T(8,128)S(1)} %get-tuple-element.60.lone_h2, f32[2,192,128]{2,1,0:T(8,128)S(1)} %get-tuple-element.61.lone_e2, ...), custom_call_target="tpu_custom_call" | custom-call | flops 2170880 | bytes 2170880 | tf_op jit(solution)/shard_map/pallas_call | solution.py:592
  16.5 12.5 %all_to_all.11 = f32[8,16,128]{2,1,0:T(8,128)S(1)} all-to-all(f32[8,16,128]{2,1,0:T(8,128)S(1)} %bitcast.14), channel_id=1, replica_groups=mesh['exc'=8,'space'=4] {'exc'}, dimensions={0} | all-to-all | bytes 131072 | tf_op jit(solution)/shard_map/all_to_all | solution.py:686
  29.0 0.9 %shard_map.134 = (f32[192,256]{1,0:T(8,128)}, f32[192,256]{1,0:T(8,128)}, f32[16,64]{1,0:T(8,128)}, f32[16,64]{1,0:T(8,128)}) custom-call(f32[128,128]{1,0:T(8,128)S(1)} %bitcast.13, f32[2,192,128]{2,1,0:T(8,128)S(1)} %get-tuple-element.70.e, f32[2,192,128]{2,1,0:T(8,128)S(1)} %get-tuple-element.71.h), custom_call_target="tpu_custom_call" | custom-call | flops 860160 | bytes 860160 | tf_op jit(solution)/shard_map/pallas_call | solution.py:592
Async XLA Ops:
  2.6 5.8 %collective-permute-start = (f32[168,128]{1,0:T(8,128)S(1)}, f32[168,128]{1,0:T(8,128)S(1)}, u32[]{:S(2)}, u32[]{:S(2)}) collective-permute-start(f32[168,128]{1,0:T(8,128)S(1)} %get-tuple-element.53), channel_id=1, source_target_pairs={{1,2},{2,1},{5,6},{6,5},{9,10},{10,9},{13,14},{14,13},{17,18},{18,... | collective-permute-start | bytes 258056 | tf_op jit(solution)/shard_map/ppermute | solution.py:620
  4.5 3.9 %collective-permute-start.1 = (f32[168,128]{1,0:T(8,128)S(1)}, f32[168,128]{1,0:T(8,128)S(1)}, u32[]{:S(2)}, u32[]{:S(2)}) collective-permute-start(f32[168,128]{1,0:T(8,128)S(1)} %get-tuple-element.54), channel_id=1, source_target_pairs={{0,1},{2,3},{1,0},{3,2},{4,5},{6,7},{5,4},{7,6},{8,9},{10,11},{9,8... | collective-permute-start | bytes 258056 | tf_op jit(solution)/shard_map/ppermute | solution.py:622
  8.4 3.4 %copy-start = (bf16[1,5,192,256]{3,2,1,0:T(8,128)(2,1)S(1)}, bf16[1,5,192,256]{3,2,1,0:T(8,128)(2,1)}, u32[]{:S(2)}) copy-start(bf16[1,5,192,256]{3,2,1,0:T(8,128)(2,1)} %param.13) | copy-start | bytes 1474564
  9.8 2.8 %collective-permute-start.2 = (f32[128,128]{1,0:T(8,128)S(1)}, f32[128,128]{1,0:T(8,128)S(1)}, u32[]{:S(2)}, u32[]{:S(2)}) collective-permute-start(f32[128,128]{1,0:T(8,128)S(1)} %get-tuple-element.64), channel_id=1, source_target_pairs={{0,1},{2,3},{1,0},{3,2},{4,5},{6,7},{5,4},{7,6},{8,9},{10,11},{9,8... | collective-permute-start | bytes 196616 | tf_op jit(solution)/shard_map/ppermute | solution.py:619
  9.9 5.6 %collective-permute-start.3 = (f32[128,128]{1,0:T(8,128)S(1)}, f32[128,128]{1,0:T(8,128)S(1)}, u32[]{:S(2)}, u32[]{:S(2)}) collective-permute-start(f32[128,128]{1,0:T(8,128)S(1)} %get-tuple-element.65), channel_id=1, source_target_pairs={{1,2},{2,1},{5,6},{6,5},{9,10},{10,9},{13,14},{14,13},{17,18},{18,... | collective-permute-start | bytes 196616 | tf_op jit(solution)/shard_map/ppermute | solution.py:620

commit v10 on v8

--- a/solution.py
+++ b/solution.py
@@ -16,6 +16,8 @@
 TIME_STEP = 0.025
 DAMPING = 0.5
 KEEP = 1.0 - TIME_STEP * DAMPING
+
+PER_STEP = 1.0 / TIME_STEP
 
 TANGENT = 32
 E_START = 0
@@ -60,8 +62,17 @@
 
 
 def slope(parts, row, scale):
-    terms = [(scale * SLOPES[row][i]) * parts[i] for i in range(4) if i != row]
-    return terms[0] + terms[1] + terms[2]
+    total = None
+    for i in (1, 2, 0, 3):
+        factor = scale * SLOPES[row][i]
+        if i == row:
+            continue
+        if abs(abs(factor) - 1.0) > 1e-9:
+            term = factor * parts[i]
+            total = term if total is None else total + term
+        else:
+            total = total + parts[i] if factor > 0 else total - parts[i]
+    return total
 
 
 def halves(x):
@@ -225,18 +236,18 @@
 
 def lone_h(index, fe, fh):
     for layer in (L0, L1):
-        add_x(fh, fe, layer, TIME_STEP, between(fe, index, layer))
-        add_yz(fh, fe, layer, index, TIME_STEP)
+        add_x(fh, fe, layer, 1.0, between(fe, index, layer))
+        add_yz(fh, fe, layer, index, 1.0)
 
 
 def lone_e(index, fe, fh, acc, drive, v):
     for i, layer in enumerate((L0, L1)):
         add_x(acc, fh, layer, 1.0, between(fh, index, layer), drive[i])
         add_yz(acc, fh, layer, index, 1.0)
-        fe[layer] -= TIME_STEP * thrice(v[i]) * acc[layer]
-
-
-def lonely(index, fe, fh, acc, drive, v, out_h, out_e):
+        fe[layer] -= thrice(v[i]) * acc[layer]
+
+
+def lonely(index, fe, fh, acc, drive_of, v, out_h, out_e):
     def ends_of(field):
         return x_traces(field, L1, 1), x_traces(field, L0, 0)
 
@@ -245,12 +256,12 @@
     found.append(ends_of(fh))
     for i in range(2):
         out_h[i] = fh[L0 + i]
-    lone_e(index, fe, fh, acc, drive, v)
+    lone_e(index, fe, fh, acc, drive_of(), v)
     found.append(ends_of(fe))
     for i in range(2):
         out_e[i] = fe[L0 + i]
     for face, layer in enumerate((L0, L1)):
-        add_into_end(fh, fe, layer, at_end(face), index, TIME_STEP)
+        add_into_end(fh, fe, layer, at_end(face), index, 1.0)
     found.append(ends_of(fh))
     return [jnp.concatenate(sum(traces, []), axis=0) for traces in zip(*found)]
 
@@ -293,8 +304,8 @@
 
     near_h, own_h = [], []
     for side, (near, face, layer, own_face) in enumerate(sides):
-        near_h.append(outward(side, start_e, TIME_STEP))
-        own_h.append(inward(side, E_START, TIME_STEP))
+        near_h.append(outward(side, start_e, 1.0))
+        own_h.append(inward(side, E_START, 1.0))
         put(fh, near, at_end(face), near_h[side])
         put(fh, layer, at_end(own_face), own_h[side])
 
@@ -303,7 +314,7 @@
         pair = outward(side, lone_h1, 1.0, own_h[side])
         acc[near, rows_at(0, i), :] = empty
         add_end(acc, fh, near, i, index, 1.0, True)
-        scale = -TIME_STEP * near_v[side, 0:16, :]
+        scale = -near_v[side, 0:16, :]
         put(fe, near, i, [scale * part for part in pair])
         fe[near, rows_at(0, i), :] = scale * acc[near, rows_at(0, i), :]
 
@@ -312,7 +323,7 @@
         acc[layer, rows_at(0, i), :] = empty
         add_end(acc, fh, layer, i, index, 1.0, True)
         for n in range(4):
-            scale = -TIME_STEP * v[side, 16 * n : 16 * n + 16, :]
+            scale = -v[side, 16 * n : 16 * n + 16, :]
             if n == i:
                 put(fe, layer, n, [scale * part for part in pair])
                 fe[layer, rows_at(0, n), :] = scale * acc[layer, rows_at(0, n), :]
@@ -323,25 +334,25 @@
 
     for side, (near, face, layer, own_face) in enumerate(sides):
         i = at_end(face)
-        pair = outward(side, lone_e1, TIME_STEP, x_traces(fe, layer, own_face))
-        back = 1.0 + TIME_STEP * TIME_STEP * near_v[side, 16:32, :]
+        pair = outward(side, lone_e1, 1.0, x_traces(fe, layer, own_face))
+        back = 1.0 + near_v[side, 16:32, :]
         put(fh, near, i, [a + back * b for a, b in zip(pair, near_h[side])])
-        add_end(fh, fe, near, i, index, TIME_STEP, False)
+        add_end(fh, fe, near, i, index, 1.0, False)
         ends = (at_end(own_face), *own_h[side])
-        add_x(fh, fe, layer, TIME_STEP, between(fe, index, layer), None, ends)
-        add_yz(fh, fe, layer, index, TIME_STEP, True)
+        add_x(fh, fe, layer, 1.0, between(fe, index, layer), None, ends)
+        add_yz(fh, fe, layer, index, 1.0, True)
         i = at_end(own_face)
-        add(fh, layer, i, inward(side, E_FIRST, TIME_STEP, x_traces(fe, near, face)))
+        add(fh, layer, i, inward(side, E_FIRST, 1.0, x_traces(fe, near, face)))
 
     current, second_e = [], []
     for i, layer in enumerate(own):
-        current.append(TIME_STEP * thrice(w[i]) * fe[layer])
+        current.append(thrice(w[i]) * fe[layer])
         add_x(acc, fh, layer, 1.0, between(fh, index, layer), current[i])
         add_yz(acc, fh, layer, index, 1.0)
     for side, (near, face, layer, own_face) in enumerate(sides):
         i = at_end(own_face)
         add(acc, layer, i, inward(side, H_SECOND, 1.0, x_traces(fh, near, face)))
-        second_e.append(fe[layer] - TIME_STEP * thrice(v[side]) * acc[layer])
+        second_e.append(fe[layer] - thrice(v[side]) * acc[layer])
     return second_e, current
 
 
@@ -370,18 +381,24 @@
     across, inside, fe, fh, acc, neighbor, ports, profile, e, h, j, v_all, w_all, sems = rest[10:]
     started = []
 
-    def fetch(origin, target):
-        started.append(pltpu.make_async_copy(origin, target, sems.at[len(started)]))
-        started[-1].start()
-
-    fetch(near_in, neighbor)
-    fetch(ports_in, ports)
-    fetch(profile_in, profile)
-    for origin, target in ((e_in, e), (h_in, h), (j_in, j), (w_in, w_all), (v_in, v_all)):
-        fetch(origin, target)
-    fetch(design_in, design)
-    for copy in started:
-        copy.wait()
+    def fetch(*pairs):
+        copies = []
+        for origin, target in pairs:
+            copies.append(pltpu.make_async_copy(origin, target, sems.at[len(started)]))
+            copies[-1].start()
+            started.append(None)
+        return copies
+
+    def wait(copies):
+        for copy in copies:
+            copy.wait()
+
+    scatter = fetch((near_in, neighbor), (ports_in, ports), (profile_in, profile))
+    fields = fetch((e_in, e), (h_in, h))
+    weights = fetch((j_in, j), (w_in, w_all), (v_in, v_all))
+    later = fetch((design_in, design))
+
+    wait(scatter)
     found = neighbor[...]
     place = jnp.where(found < 0, 0, jnp.bitwise_and(found, LAYER - 1))
     for i in range(2):
@@ -390,29 +407,39 @@
             places[6 * i + face] = jnp.broadcast_to(place[face : face + 1, columns], (8, LAYER))
         there = (found[i : i + 1, columns] >= 0).astype(F32)
         valid[i] = jnp.broadcast_to(there, (8, LAYER))
+    targets = lax.broadcasted_iota(jnp.int32, (2 * LAYER, ports.shape[1]), 0)
+    spread_hot = one_hot(targets, jnp.bitwise_and(ports[...], 2 * LAYER - 1))
+    high, low = halves(PER_STEP * profile[...])
+    spread = layers_of(dot_t(high, spread_hot) + dot_t(low, spread_hot))
+    for i in range(2):
+        source[i] = stored(spread[i])
+
+    wait(fields)
     electric = [stored(part) for part in layers_of(e[...])]
     magnetic = [stored(part) for part in layers_of(h[...])]
-    current = [stored(part) for part in layers_of(j[...])]
-    weight = layers_of(w_all[...])
-    scale = layers_of(v_all[...])
-    for i in range(2):
-        w[i] = weight[i]
-        v[i] = scale[i]
+    for i in range(2):
         start_e[i] = electric[i]
         fe[L0 + i] = electric[i]
-        fh[L0 + i] = magnetic[i]
-    targets = lax.broadcasted_iota(jnp.int32, (2 * LAYER, ports.shape[1]), 0)
-    spread_hot = one_hot(targets, jnp.bitwise_and(ports[...], 2 * LAYER - 1))
-    high, low = halves(profile[...])
-    spread = layers_of(dot_t(high, spread_hot) + dot_t(low, spread_hot))
-    drive = []
-    for i in range(2):
-        source[i] = stored(spread[i])
-        now = KEEP * current[i] + TIME_STEP * thrice(weight[i]) * electric[i]
-        first_j[i] = now
-        drive.append(now + source[i])
-
-    up, down = lonely(own_index(places), fe, fh, acc, drive, v, lone_h1, lone_e1)
+        fh[L0 + i] = PER_STEP * magnetic[i]
+
+    scale = []
+
+    def drive_of():
+        wait(weights)
+        current = [stored(part) for part in layers_of(j[...])]
+        weight = layers_of(w_all[...])
+        drive = []
+        for i, part in enumerate(layers_of(v_all[...])):
+            scale.append((TIME_STEP * TIME_STEP) * part)
+            v[i] = scale[i]
+            w[i] = weight[i]
+            now = (KEEP * PER_STEP) * current[i] + thrice(weight[i]) * start_e[i]
+            first_j[i] = now
+            drive.append(now + source[i])
+        return drive
+
+    up, down = lonely(own_index(places), fe, fh, acc, drive_of, v, lone_h1, lone_e1)
+    wait(later)
     send(across, inside, 0, up, down)
     send(across, inside, V_NEAR, scale[1][48:NODES], scale[0][0:16])
     send(across, inside, V_NEAR + 16, passed_back(scale[1], 3), passed_back(scale[0], 0))
@@ -440,7 +467,7 @@
     for i in range(2):
         fe[L0 + i] = lone_e1[i]
         fh[L0 + i] = lone_h1[i]
-    current = [KEEP * first_j[i] + TIME_STEP * thrice(w[i]) * lone_e1[i] for i in range(2)]
+    current = [KEEP * first_j[i] + thrice(w[i]) * lone_e1[i] for i in range(2)]
     lone_h(index, fe, fh)
     lone_e(index, fe, fh, acc, [current[i] + source[i] for i in range(2)], v)
     return current
@@ -494,10 +521,10 @@
         fe[L0 + i] = electric
         fh[L0 + i] += lone_h2[i]
         before = lone_j2[i] + current[i]
-        now = KEEP * before + TIME_STEP * thrice(w[i]) * electric
+        now = KEEP * before + thrice(w[i]) * electric
         next_j[i] = now
         drive.append(now + source[i])
-    up, down = lonely(index, fe, fh, acc, drive, v, next_h, next_e)
+    up, down = lonely(index, fe, fh, acc, lambda: drive, v, next_h, next_e)
     send(across, inside, 0, up, down)
 
 
@@ -519,7 +546,7 @@
         drude = lone_j1[i] * level[0] + (lone_j2[i] + answer_j[i]) * level[1]
         drude += next_j[i] * level[2] + current[i] * level[3]
         out[0:NODES, columns] = folded(eps)
-        out[NODES : 2 * NODES, columns] = folded(drude)
+        out[NODES : 2 * NODES, columns] = TIME_STEP * folded(drude)
         changes[0, i] = level[3] - level[2]
         changes[1, i] = level[4] - level[3]
         changes[2, i] = level[3]
@@ -539,9 +566,9 @@
     parts = []
     for i in range(2):
         out_e[i] = lone_e2[i] + second_e[i]
-        out_h[i] = lone_h2[i] + fh[L0 + i]
+        out_h[i] = TIME_STEP * (lone_h2[i] + fh[L0 + i])
         eps = folded(fe[L0 + i] * changes[0, i] + second_e[i] * changes[1, i])
-        drude = folded(current[i] * changes[2, i])
+        drude = TIME_STEP * folded(current[i] * changes[2, i])
         columns = slice(i * LAYER, (i + 1) * LAYER)
         parts.append(jnp.concatenate([eps, drude], axis=0) + early[:, columns])
     both = jnp.concatenate(parts, axis=1)

time: 30 us -> 29.9 us (level)
  no operation moved by 1% of the time
where the time goes in v10:
time: 29.9 us; the launch traced here: 29.7 us
  blocking collectives  12.5 us (42%)
  waiting for transfers between devices  6.24 us (21%)
  Pallas kernels  6.2 us (21%)
  starting transfers between devices  3.98 us (13%)
  between operations  0.71 us (2%)
    all_to_all x1, blocking collectives, local(): parts = lax.all_to_all(sums, 'exc', split_axis=0, concat_axis=0, tiled=True)  12.5 us
    ppermute x2, waiting for transfers between devices, exchange(): across = lax.ppermute(across, 'space', pairs(1))  6.23 us
    pallas_call x6, Pallas kernels, call(): pl.pallas_call(kernel, out_shape=outs, in_specs=[pl.BlockSpec(memory_spac...  6.2 us
    ppermute x2, starting transfers between devices, exchange(): across = lax.ppermute(across, 'space', pairs(1))  3.84 us
  transfers between devices with their start and end apart: 4, of which 2 were waited for; matrix products, arithmetic and copies ran while one was open for 0% of the time, Pallas kernels for 4%

profile of v10, /device:TPU:2, one launch (start us, length us, event | category | flops | bytes accessed | tf_op | source)
XLA Modules:
  0.0 29.7 jit_solution(9024439959628680135)
XLA Ops:
  0.6 1.9 %shard_map.129 = (s32[1,256]{1,0:T(1,128)S(1)}, f32[2,192,128]{2,1,0:T(8,128)S(1)}, f32[2,192,128]{2,1,0:T(8,128)S(1)}, f32[2,192,128]{2,1,0:T(8,128)S(1)}, f32[...) custom-call(f32[192,256]{1,0:T(8,128)} %bitcast.15, ...), custom_call_target="tpu_custom_call" | custom-call | flops 2171392 | bytes 2171392 | tf_op jit(solution)/shard_map/pallas_call | solution.py:608
  2.5 1.9 %collective-permute-start = (f32[168,128]{1,0:T(8,128)S(1)}, f32[168,128]{1,0:T(8,128)S(1)}, u32[]{:S(2)}, u32[]{:S(2)}) collective-permute-start(f32[168,128]{1,0:T(8,128)S(1)} %get-tuple-element.54), channel_id=1, source_target_pairs={{1,2},{2,1},{5,6},{6,5},{9,10},{10,9},{13,14},{14,13},{17,18},{18,... | collective-permute-start | bytes 258056 | tf_op jit(solution)/shard_map/ppermute | solution.py:636
  4.4 0.1 collective-permute-start.1
  4.5 0.5 %shard_map.130 = (f32[2,192,128]{2,1,0:T(8,128)S(1)}, f32[2,192,128]{2,1,0:T(8,128)S(1)}, f32[2,192,128]{2,1,0:T(8,128)S(1)}, bf16[128,256]{1,0:T(8,128)(2,1)S(1)}) custom-call(f32[2,192,128]{2,1,0:T(8,128)S(1)} %get-tuple-element.42.lone_h1, f32[2,192,128]{2,1,0:T(8,128)S(1)} %get-tuple-element.43.lone_e1, ...), custom_call_target="tpu_custom_call" | custom-call | flops 1688576 | bytes 1688576 | tf_op jit(solution)/shard_map/pallas_call | solution.py:608
  5.0 3.3 %collective-permute-done.across_in = f32[168,128]{1,0:T(8,128)S(1)} collective-permute-done((f32[168,128]{1,0:T(8,128)S(1)}, f32[168,128]{1,0:T(8,128)S(1)}, u32[]{:S(2)}, u32[]{:S(2)}) %collective-permute-start) | collective-permute-done | bytes 86048 | tf_op jit(solution)/shard_map/ppermute | solution.py:636
  8.3 0.0 collective-permute-done.1.inside_in
  8.3 0.0 copy-start
  8.3 1.3 %shard_map.131 = (f32[2,192,128]{2,1,0:T(8,128)S(1)}, f32[2,192,128]{2,1,0:T(8,128)S(1)}, f32[2,192,128]{2,1,0:T(8,128)S(1)}, f32[2,192,128]{2,1,0:T(8,128)S(1)}...) custom-call(f32[2,192,128]{2,1,0:T(8,128)S(1)} %get-tuple-element.41, ...), custom_call_target="tpu_custom_call" | custom-call | flops 3129344 | bytes 3129344 | tf_op jit(solution)/shard_map/pallas_call | solution.py:608
  9.6 0.1 collective-permute-start.2
  9.7 1.9 %collective-permute-start.3 = (f32[128,128]{1,0:T(8,128)S(1)}, f32[128,128]{1,0:T(8,128)S(1)}, u32[]{:S(2)}, u32[]{:S(2)}) collective-permute-start(f32[128,128]{1,0:T(8,128)S(1)} %get-tuple-element.67), channel_id=1, source_target_pairs={{1,2},{2,1},{5,6},{6,5},{9,10},{10,9},{13,14},{14,13},{17,18},{18,... | collective-permute-start | bytes 196616 | tf_op jit(solution)/shard_map/ppermute | solution.py:636
  11.6 0.0 copy-done
  11.7 0.7 %shard_map.132 = (f32[2,192,128]{2,1,0:T(8,128)S(1)}, f32[2,192,128]{2,1,0:T(8,128)S(1)}, f32[128,256]{1,0:T(8,128)S(1)}, f32[3,2,192,128]{3,2,1,0:T(8,128)S(1)}) custom-call(f32[2,192,128]{2,1,0:T(8,128)S(1)} %get-tuple-element.43.lone_e1, f32[2,192,128]{2,1,0:T(8,128)S(1)} %get-tuple-element.59.answer_e, ...), custom_call_target="tpu_custom_call" | custom-call | flops 3751936 | bytes 3751936 | tf_op jit(solution)/shard_map/pallas_call | solution.py:608
  12.4 0.0 collective-permute-done.2.inside_in
  12.4 2.9 %collective-permute-done.3.across_in = f32[128,128]{1,0:T(8,128)S(1)} collective-permute-done((f32[128,128]{1,0:T(8,128)S(1)}, f32[128,128]{1,0:T(8,128)S(1)}, u32[]{:S(2)}, u32[]{:S(2)}) %collective-permute-start.3) | collective-permute-done | bytes 65568 | tf_op jit(solution)/shard_map/ppermute | solution.py:636
  15.3 1.0 %shard_map.133 = (f32[2,192,128]{2,1,0:T(8,128)S(1)}, f32[2,192,128]{2,1,0:T(8,128)S(1)}, f32[128,128]{1,0:T(8,128)S(1)}) custom-call(f32[2,192,128]{2,1,0:T(8,128)S(1)} %get-tuple-element.56.end_e.start_e, f32[2,192,128]{2,1,0:T(8,128)S(1)} %get-tuple-element.57.next_h.lone_h1, f32[2,192,128]{2,1,0:T(8,128)S(1)} %get-tuple-element.58.next_e.lone_e1, ...), custom_call_target="tpu_custom_call" | custom-call | flops 2629632 | bytes 2629632 | tf_op jit(solution)/shard_map/pallas_call | solution.py:608
  16.3 12.5 %all_to_all.11 = f32[8,16,128]{2,1,0:T(8,128)S(1)} all-to-all(f32[8,16,128]{2,1,0:T(8,128)S(1)} %bitcast.14), channel_id=1, replica_groups=mesh['exc'=8,'space'=4] {'exc'}, dimensions={0} | all-to-all | bytes 131072 | tf_op jit(solution)/shard_map/all_to_all | solution.py:704
  28.8 0.9 %shard_map.134 = (f32[192,256]{1,0:T(8,128)}, f32[192,256]{1,0:T(8,128)}, f32[16,64]{1,0:T(8,128)}, f32[16,64]{1,0:T(8,128)}) custom-call(f32[128,128]{1,0:T(8,128)S(1)} %bitcast.13, f32[2,192,128]{2,1,0:T(8,128)S(1)} %get-tuple-element.72.e, f32[2,192,128]{2,1,0:T(8,128)S(1)} %get-tuple-element.73.h), custom_call_target="tpu_custom_call" | custom-call | flops 860160 | bytes 860160 | tf_op jit(solution)/shard_map/pallas_call | solution.py:608
Async XLA Ops:
  2.5 5.8 %collective-permute-start = (f32[168,128]{1,0:T(8,128)S(1)}, f32[168,128]{1,0:T(8,128)S(1)}, u32[]{:S(2)}, u32[]{:S(2)}) collective-permute-start(f32[168,128]{1,0:T(8,128)S(1)} %get-tuple-element.54), channel_id=1, source_target_pairs={{1,2},{2,1},{5,6},{6,5},{9,10},{10,9},{13,14},{14,13},{17,18},{18,... | collective-permute-start | bytes 258056 | tf_op jit(solution)/shard_map/ppermute | solution.py:636
  4.4 3.9 %collective-permute-start.1 = (f32[168,128]{1,0:T(8,128)S(1)}, f32[168,128]{1,0:T(8,128)S(1)}, u32[]{:S(2)}, u32[]{:S(2)}) collective-permute-start(f32[168,128]{1,0:T(8,128)S(1)} %get-tuple-element.55), channel_id=1, source_target_pairs={{0,1},{2,3},{1,0},{3,2},{4,5},{6,7},{5,4},{7,6},{8,9},{10,11},{9,8... | collective-permute-start | bytes 258056 | tf_op jit(solution)/shard_map/ppermute | solution.py:638
  8.3 3.3 %copy-start = (bf16[1,5,192,256]{3,2,1,0:T(8,128)(2,1)S(1)}, bf16[1,5,192,256]{3,2,1,0:T(8,128)(2,1)}, u32[]{:S(2)}) copy-start(bf16[1,5,192,256]{3,2,1,0:T(8,128)(2,1)} %param.13) | copy-start | bytes 1474564
  9.6 2.7 %collective-permute-start.2 = (f32[128,128]{1,0:T(8,128)S(1)}, f32[128,128]{1,0:T(8,128)S(1)}, u32[]{:S(2)}, u32[]{:S(2)}) collective-permute-start(f32[128,128]{1,0:T(8,128)S(1)} %get-tuple-element.66), channel_id=1, source_target_pairs={{0,1},{2,3},{1,0},{3,2},{4,5},{6,7},{5,4},{7,6},{8,9},{10,11},{9,8... | collective-permute-start | bytes 196616 | tf_op jit(solution)/shard_map/ppermute | solution.py:635
  9.7 5.6 %collective-permute-start.3 = (f32[128,128]{1,0:T(8,128)S(1)}, f32[128,128]{1,0:T(8,128)S(1)}, u32[]{:S(2)}, u32[]{:S(2)}) collective-permute-start(f32[128,128]{1,0:T(8,128)S(1)} %get-tuple-element.67), channel_id=1, source_target_pairs={{1,2},{2,1},{5,6},{6,5},{9,10},{10,9},{13,14},{14,13},{17,18},{18,... | collective-permute-start | bytes 196616 | tf_op jit(solution)/shard_map/ppermute | solution.py:636

commit v11 on v10

--- a/solution.py
+++ b/solution.py
@@ -168,17 +168,28 @@
                 target[layer, rows, :] = change
             else:
                 target[layer, rows, :] += change
-    sign = jnp.where(lax.broadcasted_iota(jnp.int32, (8, LAYER), 0) < 4, -1.0, 1.0)
-    for k in range(4):
-        parts = [field[layer, pl.ds(BASE[0] + 4 * j + k, 8, stride=16), :] for j in range(4)]
-        for j in range(4):
-            change = slope(parts, j, scale)
-            if j in (0, 3):
-                face = 2 if j == 0 else 3
-                got = picked(parts[3 - j], index(layer, face))
-                change += (scale * parity(0, face, 2)) * got
-            rows = pl.ds(BASE[0] + 4 * j + k, 8, stride=16)
-            target[layer, rows, :] += sign * pltpu.roll(change, 4, 0)
+    first = lax.broadcasted_iota(jnp.int32, (8, LAYER), 0) < 4
+    mixed = jnp.where(first, index(layer, 2), index(layer, 3))
+    for c, other, sign in ((0, 2, -scale), (2, 0, scale)):
+
+        def pair(upper, lower):
+            return jnp.where(first, sign * upper, sign * lower)
+
+        d = SLOPES
+        face_low = jnp.where(first, -scale * parity(c, 2, other), 0.0)
+        face_high = jnp.where(first, 0.0, -scale * parity(c, 3, other))
+        for i in range(4):
+            at = BASE[other] + 16 * i
+            low, high = field[layer, at : at + 8, :], field[layer, at + 8 : at + 16, :]
+            low_turned, high_turned = pltpu.roll(low, 4, 0), pltpu.roll(high, 4, 0)
+            got = picked(jnp.where(first, high_turned, low_turned), mixed)
+            change_low = pair(d[0][1], d[1][0]) * low_turned + pair(d[0][2], d[1][3]) * high
+            change_low += pair(d[0][3], d[1][2]) * high_turned + face_low * got
+            change_high = pair(d[2][0], d[3][1]) * low + pair(d[2][1], d[3][0]) * low_turned
+            change_high += pair(d[2][3], d[3][2]) * high_turned + face_high * got
+            at = BASE[c] + 16 * i
+            target[layer, at : at + 8, :] += change_low
+            target[layer, at + 8 : at + 16, :] += change_high
 
 
 def add_end(target, field, layer, i, index, scale, to_x):
@@ -565,11 +576,15 @@
     )
     parts = []
     for i in range(2):
-        out_e[i] = lone_e2[i] + second_e[i]
-        out_h[i] = TIME_STEP * (lone_h2[i] + fh[L0 + i])
+        columns = slice(i * LAYER, (i + 1) * LAYER)
+        electric = lone_e2[i] + second_e[i]
+        magnetic = TIME_STEP * (lone_h2[i] + fh[L0 + i])
+        for c in range(3):
+            rows, there = slice(BASE[c], BASE[c] + NODES), slice(c * NODES, (c + 1) * NODES)
+            out_e[there, columns] = electric[rows]
+            out_h[there, columns] = magnetic[rows]
         eps = folded(fe[L0 + i] * changes[0, i] + second_e[i] * changes[1, i])
         drude = TIME_STEP * folded(current[i] * changes[2, i])
-        columns = slice(i * LAYER, (i + 1) * LAYER)
         parts.append(jnp.concatenate([eps, drude], axis=0) + early[:, columns])
     both = jnp.concatenate(parts, axis=1)
     high, low = halves(both)
@@ -583,11 +598,8 @@
         copies.append(pltpu.make_async_copy(origin, target, sems.at[len(copies)]))
         copies[-1].start()
 
-    for field, target in ((e, out_e), (h, out_h)):
-        for i in range(2):
-            for c in range(3):
-                there = target.at[pl.ds(c * NODES, NODES), pl.ds(i * LAYER, LAYER)]
-                write(field.at[i, pl.ds(BASE[c], NODES), :], there)
+    write(e, out_e)
+    write(h, out_h)
     share = parts.shape[0] // owners
     total = parts[0:share]
     for owner in range(1, owners):
@@ -696,7 +708,7 @@
     )
     e4, h4, sums = call(
         last_kernel,
-        [field, field, f32(PIX_DEV, 2 * NODES)],
+        [f32(ROWS, count)] * 2 + [f32(PIX_DEV, 2 * NODES)],
         [end_e, h3, e3, h4, e4, v, w, places, valid, near_v, near_places]
         + [inside, across, changes, early, pixels],
         work + [pltpu.VMEM((SECOND, LAYER), F32)] * 2,
@@ -707,7 +719,7 @@
         functools.partial(total_kernel, owners),
         [f32(ROWS, count)] * 2 + [f32(share, NODES)] * 2,
         [parts, e4, h4],
-        [pltpu.VMEM((2, share, NODES), F32), pltpu.SemaphoreType.DMA((14,))],
+        [pltpu.VMEM((2, share, NODES), F32), pltpu.SemaphoreType.DMA((4,))],
         out_spaces=[pltpu.HBM] * 4,
     )
     return out_e[None], out_h[None], eps.T, drude.T

time: 29.9 us -> 29.2 us (0.977)
  Pallas kernels: 6.2 us -> 5.21 us
    pallas_call x6, Pallas kernels: 6.2 us -> 5.21 us  [call(): pl.pallas_call(kernel, out_shape=outs, in_specs=[pl.BlockSpec(memory_spac...]
  transfers between devices with their start and end apart: 4 -> 4, of which waited for: 2 -> 2; matrix products, arithmetic and copies ran while one was open for 0% -> 0% of each run, Pallas kernels for 4% -> 3%
where the time goes in v11:
time: 29.2 us; the launch traced here: 28.9 us
  blocking collectives  12.5 us (43%)
  waiting for transfers between devices  6.51 us (22%)
  Pallas kernels  5.21 us (18%)
  starting transfers between devices  3.98 us (14%)
  between operations  0.71 us (2%)
    all_to_all x1, blocking collectives, local(): parts = lax.all_to_all(sums, 'exc', split_axis=0, concat_axis=0, tiled=True)  12.5 us
    ppermute x2, waiting for transfers between devices, exchange(): across = lax.ppermute(across, 'space', pairs(1))  6.5 us
    pallas_call x6, Pallas kernels, call(): pl.pallas_call(kernel, out_shape=outs, in_specs=[pl.BlockSpec(memory_spac...  5.21 us
    ppermute x2, starting transfers between devices, exchange(): across = lax.ppermute(across, 'space', pairs(1))  3.84 us
  transfers between devices with their start and end apart: 4, of which 2 were waited for; matrix products, arithmetic and copies ran while one was open for 0% of the time, Pallas kernels for 3%

profile of v11, /device:TPU:2, one launch (start us, length us, event | category | flops | bytes accessed | tf_op | source)
XLA Modules:
  0.0 28.9 jit_solution(2203210038235705678)
XLA Ops:
  0.6 1.7 %shard_map.129 = (s32[1,256]{1,0:T(1,128)S(1)}, f32[2,192,128]{2,1,0:T(8,128)S(1)}, f32[2,192,128]{2,1,0:T(8,128)S(1)}, f32[2,192,128]{2,1,0:T(8,128)S(1)}, f32[...) custom-call(f32[192,256]{1,0:T(8,128)} %bitcast.15, ...), custom_call_target="tpu_custom_call" | custom-call | flops 2171392 | bytes 2171392 | tf_op jit(solution)/shard_map/pallas_call | solution.py:620
  2.3 1.9 %collective-permute-start = (f32[168,128]{1,0:T(8,128)S(1)}, f32[168,128]{1,0:T(8,128)S(1)}, u32[]{:S(2)}, u32[]{:S(2)}) collective-permute-start(f32[168,128]{1,0:T(8,128)S(1)} %get-tuple-element.54), channel_id=1, source_target_pairs={{1,2},{2,1},{5,6},{6,5},{9,10},{10,9},{13,14},{14,13},{17,18},{18,... | collective-permute-start | bytes 258056 | tf_op jit(solution)/shard_map/ppermute | solution.py:648
  4.3 0.1 collective-permute-start.1
  4.3 0.4 %shard_map.130 = (f32[2,192,128]{2,1,0:T(8,128)S(1)}, f32[2,192,128]{2,1,0:T(8,128)S(1)}, f32[2,192,128]{2,1,0:T(8,128)S(1)}, bf16[128,256]{1,0:T(8,128)(2,1)S(1)}) custom-call(f32[2,192,128]{2,1,0:T(8,128)S(1)} %get-tuple-element.42.lone_h1, f32[2,192,128]{2,1,0:T(8,128)S(1)} %get-tuple-element.43.lone_e1, ...), custom_call_target="tpu_custom_call" | custom-call | flops 1688576 | bytes 1688576 | tf_op jit(solution)/shard_map/pallas_call | solution.py:620
  4.7 3.4 %collective-permute-done.across_in = f32[168,128]{1,0:T(8,128)S(1)} collective-permute-done((f32[168,128]{1,0:T(8,128)S(1)}, f32[168,128]{1,0:T(8,128)S(1)}, u32[]{:S(2)}, u32[]{:S(2)}) %collective-permute-start) | collective-permute-done | bytes 86048 | tf_op jit(solution)/shard_map/ppermute | solution.py:648
  8.1 0.0 collective-permute-done.1.inside_in
  8.1 0.0 copy-start
  8.1 1.0 %shard_map.131 = (f32[2,192,128]{2,1,0:T(8,128)S(1)}, f32[2,192,128]{2,1,0:T(8,128)S(1)}, f32[2,192,128]{2,1,0:T(8,128)S(1)}, f32[2,192,128]{2,1,0:T(8,128)S(1)}...) custom-call(f32[2,192,128]{2,1,0:T(8,128)S(1)} %get-tuple-element.41, ...), custom_call_target="tpu_custom_call" | custom-call | flops 3129344 | bytes 3129344 | tf_op jit(solution)/shard_map/pallas_call | solution.py:620
  9.2 0.1 collective-permute-start.2
  9.2 1.9 %collective-permute-start.3 = (f32[128,128]{1,0:T(8,128)S(1)}, f32[128,128]{1,0:T(8,128)S(1)}, u32[]{:S(2)}, u32[]{:S(2)}) collective-permute-start(f32[128,128]{1,0:T(8,128)S(1)} %get-tuple-element.67), channel_id=1, source_target_pairs={{1,2},{2,1},{5,6},{6,5},{9,10},{10,9},{13,14},{14,13},{17,18},{18,... | collective-permute-start | bytes 196616 | tf_op jit(solution)/shard_map/ppermute | solution.py:648
  11.2 0.0 copy-done
  11.2 0.6 %shard_map.132 = (f32[2,192,128]{2,1,0:T(8,128)S(1)}, f32[2,192,128]{2,1,0:T(8,128)S(1)}, f32[128,256]{1,0:T(8,128)S(1)}, f32[3,2,192,128]{3,2,1,0:T(8,128)S(1)}) custom-call(f32[2,192,128]{2,1,0:T(8,128)S(1)} %get-tuple-element.43.lone_e1, f32[2,192,128]{2,1,0:T(8,128)S(1)} %get-tuple-element.59.answer_e, ...), custom_call_target="tpu_custom_call" | custom-call | flops 3751936 | bytes 3751936 | tf_op jit(solution)/shard_map/pallas_call | solution.py:620
  11.7 0.0 collective-permute-done.2.inside_in
  11.7 3.1 %collective-permute-done.3.across_in = f32[128,128]{1,0:T(8,128)S(1)} collective-permute-done((f32[128,128]{1,0:T(8,128)S(1)}, f32[128,128]{1,0:T(8,128)S(1)}, u32[]{:S(2)}, u32[]{:S(2)}) %collective-permute-start.3) | collective-permute-done | bytes 65568 | tf_op jit(solution)/shard_map/ppermute | solution.py:648
  14.8 0.8 %shard_map.133 = (f32[192,256]{1,0:T(8,128)S(1)}, f32[192,256]{1,0:T(8,128)S(1)}, f32[128,128]{1,0:T(8,128)S(1)}) custom-call(f32[2,192,128]{2,1,0:T(8,128)S(1)} %get-tuple-element.56.end_e.start_e, f32[2,192,128]{2,1,0:T(8,128)S(1)} %get-tuple-element.57.next_h.lone_h1, f32[2,192,128]{2,1,0:T(8,128)S(1)} %get-tuple-element.58.next_e.lone_e1, ...), custom_call_target="tpu_custom_call" | custom-call | flops 2629632 | bytes 2629632 | tf_op jit(solution)/shard_map/pallas_call | solution.py:620
  15.6 12.5 %all_to_all.11 = f32[8,16,128]{2,1,0:T(8,128)S(1)} all-to-all(f32[8,16,128]{2,1,0:T(8,128)S(1)} %bitcast.14), channel_id=1, replica_groups=mesh['exc'=8,'space'=4] {'exc'}, dimensions={0} | all-to-all | bytes 131072 | tf_op jit(solution)/shard_map/all_to_all | solution.py:716
  28.2 0.8 %shard_map.134 = (f32[192,256]{1,0:T(8,128)}, f32[192,256]{1,0:T(8,128)}, f32[16,64]{1,0:T(8,128)}, f32[16,64]{1,0:T(8,128)}) custom-call(f32[128,128]{1,0:T(8,128)S(1)} %bitcast.13, f32[192,256]{1,0:T(8,128)S(1)} %get-tuple-element.72.e, f32[192,256]{1,0:T(8,128)S(1)} %get-tuple-element.73.h), custom_call_target="tpu_custom_call" | custom-call | flops 860160 | bytes 860160 | tf_op jit(solution)/shard_map/pallas_call | solution.py:620
Async XLA Ops:
  2.3 5.8 %collective-permute-start = (f32[168,128]{1,0:T(8,128)S(1)}, f32[168,128]{1,0:T(8,128)S(1)}, u32[]{:S(2)}, u32[]{:S(2)}) collective-permute-start(f32[168,128]{1,0:T(8,128)S(1)} %get-tuple-element.54), channel_id=1, source_target_pairs={{1,2},{2,1},{5,6},{6,5},{9,10},{10,9},{13,14},{14,13},{17,18},{18,... | collective-permute-start | bytes 258056 | tf_op jit(solution)/shard_map/ppermute | solution.py:648
  4.3 3.9 %collective-permute-start.1 = (f32[168,128]{1,0:T(8,128)S(1)}, f32[168,128]{1,0:T(8,128)S(1)}, u32[]{:S(2)}, u32[]{:S(2)}) collective-permute-start(f32[168,128]{1,0:T(8,128)S(1)} %get-tuple-element.55), channel_id=1, source_target_pairs={{0,1},{2,3},{1,0},{3,2},{4,5},{6,7},{5,4},{7,6},{8,9},{10,11},{9,8... | collective-permute-start | bytes 258056 | tf_op jit(solution)/shard_map/ppermute | solution.py:650
  8.1 3.0 %copy-start = (bf16[1,5,192,256]{3,2,1,0:T(8,128)(2,1)S(1)}, bf16[1,5,192,256]{3,2,1,0:T(8,128)(2,1)}, u32[]{:S(2)}) copy-start(bf16[1,5,192,256]{3,2,1,0:T(8,128)(2,1)} %param.13) | copy-start | bytes 1474564
  9.2 2.6 %collective-permute-start.2 = (f32[128,128]{1,0:T(8,128)S(1)}, f32[128,128]{1,0:T(8,128)S(1)}, u32[]{:S(2)}, u32[]{:S(2)}) collective-permute-start(f32[128,128]{1,0:T(8,128)S(1)} %get-tuple-element.66), channel_id=1, source_target_pairs={{0,1},{2,3},{1,0},{3,2},{4,5},{6,7},{5,4},{7,6},{8,9},{10,11},{9,8... | collective-permute-start | bytes 196616 | tf_op jit(solution)/shard_map/ppermute | solution.py:647
  9.2 5.6 %collective-permute-start.3 = (f32[128,128]{1,0:T(8,128)S(1)}, f32[128,128]{1,0:T(8,128)S(1)}, u32[]{:S(2)}, u32[]{:S(2)}) collective-permute-start(f32[128,128]{1,0:T(8,128)S(1)} %get-tuple-element.67), channel_id=1, source_target_pairs={{1,2},{2,1},{5,6},{6,5},{9,10},{10,9},{13,14},{14,13},{17,18},{18,... | collective-permute-start | bytes 196616 | tf_op jit(solution)/shard_map/ppermute | solution.py:648

commit v12 on v11

--- a/solution.py
+++ b/solution.py
@@ -134,62 +134,61 @@
     target[layer, rows, :] += (-scale * parity(2, face, 1)) * y
 
 
-def add_x(target, field, layer, scale, outer, base=None, ends=None):
-    for c, other, sign in ((1, 2, 1.0), (2, 1, -1.0)):
-        parts = [field[layer, BASE[other] + 16 * i : BASE[other] + 16 * i + 16, :] for i in range(4)]
-        for i in range(4):
-            change = slope(parts, i, scale * sign)
-            face = {0: 0, 3: 1}.get(i)
-            traces = None if face is None else outer(face)
-            if traces is not None:
-                change += (-scale * parity(c, face, other)) * traces[other - 1]
-            rows = slice(BASE[c] + 16 * i, BASE[c] + 16 * i + 16)
-            if ends is None:
-                change += target[layer, rows, :] if base is None else base[rows]
-            elif ends[0] == i:
-                change += ends[c]
-            target[layer, rows, :] = change
-    if base is not None:
-        rows = slice(BASE[0], BASE[0] + NODES)
-        target[layer, rows, :] = base[rows]
-
-
-def add_yz(target, field, layer, index, scale, fresh=False):
+def rates(field, layer, index, outer, planes, use):
     for c, other, sign in ((0, 1, 1.0), (1, 0, -1.0)):
         parts = [field[layer, pl.ds(BASE[other] + k, 16, stride=4), :] for k in range(4)]
         for k in range(4):
-            change = slope(parts, k, scale * sign)
+            change = slope(parts, k, sign)
             if k in (0, 3):
                 face = 4 if k == 0 else 5
                 got = picked(parts[3 - k], index(layer, face))
-                change += (-scale * parity(c, face, other)) * got
-            rows = pl.ds(BASE[c] + k, 16, stride=4)
-            if fresh and c == 0:
-                target[layer, rows, :] = change
-            else:
-                target[layer, rows, :] += change
+                change += -parity(c, face, other) * got
+            planes[layer, pl.ds(NODES * c + k, 16, stride=4), :] = change
+    block = [
+        [field[layer, BASE[c] + 8 * n : BASE[c] + 8 * n + 8, :] for n in range(8)] for c in range(3)
+    ]
+
     first = lax.broadcasted_iota(jnp.int32, (8, LAYER), 0) < 4
     mixed = jnp.where(first, index(layer, 2), index(layer, 3))
-    for c, other, sign in ((0, 2, -scale), (2, 0, scale)):
-
+    d = SLOPES
+
+    def in_y(c, other, sign, i):
         def pair(upper, lower):
             return jnp.where(first, sign * upper, sign * lower)
 
-        d = SLOPES
-        face_low = jnp.where(first, -scale * parity(c, 2, other), 0.0)
-        face_high = jnp.where(first, 0.0, -scale * parity(c, 3, other))
-        for i in range(4):
-            at = BASE[other] + 16 * i
-            low, high = field[layer, at : at + 8, :], field[layer, at + 8 : at + 16, :]
-            low_turned, high_turned = pltpu.roll(low, 4, 0), pltpu.roll(high, 4, 0)
-            got = picked(jnp.where(first, high_turned, low_turned), mixed)
-            change_low = pair(d[0][1], d[1][0]) * low_turned + pair(d[0][2], d[1][3]) * high
-            change_low += pair(d[0][3], d[1][2]) * high_turned + face_low * got
-            change_high = pair(d[2][0], d[3][1]) * low + pair(d[2][1], d[3][0]) * low_turned
-            change_high += pair(d[2][3], d[3][2]) * high_turned + face_high * got
-            at = BASE[c] + 16 * i
-            target[layer, at : at + 8, :] += change_low
-            target[layer, at + 8 : at + 16, :] += change_high
+        low, high = block[other][2 * i], block[other][2 * i + 1]
+        low_turned, high_turned = pltpu.roll(low, 4, 0), pltpu.roll(high, 4, 0)
+        got = picked(jnp.where(first, high_turned, low_turned), mixed)
+        change_low = pair(d[0][1], d[1][0]) * low_turned + pair(d[0][2], d[1][3]) * high
+        change_low += pair(d[0][3], d[1][2]) * high_turned
+        change_low += jnp.where(first, -parity(c, 2, other), 0.0) * got
+        change_high = pair(d[2][0], d[3][1]) * low + pair(d[2][1], d[3][0]) * low_turned
+        change_high += pair(d[2][3], d[3][2]) * high_turned
+        change_high += jnp.where(first, 0.0, -parity(c, 3, other)) * got
+        return change_low, change_high
+
+    def in_x(c, other, sign, i, half):
+        change = slope([block[other][2 * m + half] for m in range(4)], i, sign)
+        face = {0: 0, 3: 1}.get(i)
+        if face is not None and traces[face] is not None:
+            trace = traces[face][other - 1][8 * half : 8 * half + 8]
+            change += -parity(c, face, other) * trace
+        return change
+
+    traces = [outer(0), outer(1)]
+    for i in range(4):
+        x_from_z = in_y(0, 2, -1.0, i)
+        z_from_x = in_y(2, 0, 1.0, i)
+        for half in range(2):
+            n = 2 * i + half
+            use(0, n, x_from_z[half] + planes[layer, 8 * n : 8 * n + 8, :])
+            change = in_x(1, 2, 1.0, i, half)
+            use(1, n, change + planes[layer, NODES + 8 * n : NODES + 8 * n + 8, :])
+            use(2, n, z_from_x[half] + in_x(2, 1, -1.0, i, half))
+
+
+def block_rows(c, n):
+    return slice(BASE[c] + 8 * n, BASE[c] + 8 * n + 8)
 
 
 def add_end(target, field, layer, i, index, scale, to_x):
@@ -245,29 +244,36 @@
     return outer
 
 
-def lone_h(index, fe, fh):
+def lone_h(index, fe, fh, planes):
     for layer in (L0, L1):
-        add_x(fh, fe, layer, 1.0, between(fe, index, layer))
-        add_yz(fh, fe, layer, index, 1.0)
-
-
-def lone_e(index, fe, fh, acc, drive, v):
+
+        def use(c, n, change, layer=layer):
+            fh[layer, block_rows(c, n), :] += change
+
+        rates(fe, layer, index, between(fe, index, layer), planes, use)
+
+
+def lone_e(index, fe, fh, planes, drive, v):
     for i, layer in enumerate((L0, L1)):
-        add_x(acc, fh, layer, 1.0, between(fh, index, layer), drive[i])
-        add_yz(acc, fh, layer, index, 1.0)
-        fe[layer] -= thrice(v[i]) * acc[layer]
-
-
-def lonely(index, fe, fh, acc, drive_of, v, out_h, out_e):
+
+        def use(c, n, change, i=i, layer=layer):
+            rows = block_rows(c, n)
+            fe[layer, rows, :] -= v[i][8 * n : 8 * n + 8] * (drive[i][rows] + change)
+
+        rates(fh, layer, index, between(fh, index, layer), planes, use)
+
+
+def lonely(index, fe, fh, planes, drive_of, v_of, out_h, out_e):
     def ends_of(field):
         return x_traces(field, L1, 1), x_traces(field, L0, 0)
 
     found = [ends_of(fe)]
-    lone_h(index, fe, fh)
+    lone_h(index, fe, fh, planes)
     found.append(ends_of(fh))
     for i in range(2):
         out_h[i] = fh[L0 + i]
-    lone_e(index, fe, fh, acc, drive_of(), v)
+    drive = drive_of()
+    lone_e(index, fe, fh, planes, drive, v_of())
     found.append(ends_of(fe))
     for i in range(2):
         out_e[i] = fe[L0 + i]
@@ -277,7 +283,7 @@
     return [jnp.concatenate(sum(traces, []), axis=0) for traces in zip(*found)]
 
 
-def respond(index, valid, fe, fh, acc, lone, v, w, near_v, sent_a, sent_b):
+def respond(index, valid, fe, fh, acc, planes, lone, v, w, near_v, sent_a, sent_b):
     start_e, lone_h1, lone_e1 = lone
     own = (L0, L1)
     sides = ((A1, 1, L0, 0), (B1, 0, L1, 1))
@@ -290,13 +296,27 @@
     def lifted(face, scale, y, z):
         return (-scale * parity(1, face, 2)) * z, (-scale * parity(2, face, 1)) * y
 
-    def inward(side, start, scale, answers=None):
-        near, _, layer, face = sides[side]
+    def arrived(side, start, answers=None):
+        _, _, layer, face = sides[side]
         traces = [sent[side][start + 16 * t : start + 16 * t + 16, :] for t in range(2)]
         if answers is not None:
             traces = [a + b for a, b in zip(traces, answers)]
         mask = jnp.concatenate([valid[side]] * 2, axis=0)
-        return lifted(face, scale, *[picked(t, index(layer, face)) * mask for t in traces])
+        return [picked(t, index(layer, face)) * mask for t in traces]
+
+    def inward(side, start, scale, answers=None):
+        return lifted(sides[side][3], scale, *arrived(side, start, answers))
+
+    def outer_of(side, field, start):
+        near, near_face, layer, own_face = sides[side]
+        inside = between(field, index, layer)
+
+        def outer(face):
+            if face != own_face:
+                return inside(face)
+            return arrived(side, start, x_traces(field, near, near_face))
+
+        return outer
 
     def outward(side, alone, scale, answers=None):
         near, face, layer, own_face = sides[side]
@@ -308,10 +328,6 @@
     def put(target, layer, i, pair):
         target[layer, rows_at(1, i), :] = pair[0]
         target[layer, rows_at(2, i), :] = pair[1]
-
-    def add(target, layer, i, pair):
-        target[layer, rows_at(1, i), :] += pair[0]
-        target[layer, rows_at(2, i), :] += pair[1]
 
     near_h, own_h = [], []
     for side, (near, face, layer, own_face) in enumerate(sides):
@@ -349,22 +365,25 @@
         back = 1.0 + near_v[side, 16:32, :]
         put(fh, near, i, [a + back * b for a, b in zip(pair, near_h[side])])
         add_end(fh, fe, near, i, index, 1.0, False)
-        ends = (at_end(own_face), *own_h[side])
-        add_x(fh, fe, layer, 1.0, between(fe, index, layer), None, ends)
-        add_yz(fh, fe, layer, index, 1.0, True)
-        i = at_end(own_face)
-        add(fh, layer, i, inward(side, E_FIRST, 1.0, x_traces(fe, near, face)))
-
-    current, second_e = [], []
-    for i, layer in enumerate(own):
-        current.append(thrice(w[i]) * fe[layer])
-        add_x(acc, fh, layer, 1.0, between(fh, index, layer), current[i])
-        add_yz(acc, fh, layer, index, 1.0)
-    for side, (near, face, layer, own_face) in enumerate(sides):
-        i = at_end(own_face)
-        add(acc, layer, i, inward(side, H_SECOND, 1.0, x_traces(fh, near, face)))
-        second_e.append(fe[layer] - thrice(v[side]) * acc[layer])
-    return second_e, current
+
+        def use_h(c, n, change, layer=layer, i=at_end(own_face), own=own_h[side]):
+            if c > 0 and n // 2 == i:
+                change += own[c - 1][8 * (n % 2) : 8 * (n % 2) + 8]
+            fh[layer, block_rows(c, n), :] = change
+
+        rates(fe, layer, index, outer_of(side, fe, E_FIRST), planes, use_h)
+
+    current = []
+    for side, layer in enumerate(own):
+        current.append(thrice(w[side]) * fe[layer])
+
+        def use_e(c, n, change, side=side, layer=layer):
+            rows = block_rows(c, n)
+            change = v[side][8 * n : 8 * n + 8] * (current[side][rows] + change)
+            acc[layer, rows, :] = fe[layer, rows, :] - change
+
+        rates(fh, layer, index, outer_of(side, fh, H_SECOND), planes, use_e)
+    return current
 
 
 def odd_rank():
@@ -389,7 +408,9 @@
     e_in, h_in, j_in, v_in, w_in, near_in, ports_in, profile_in, design_in, *rest
 ):
     design, start_e, lone_h1, lone_e1, first_j, v, w, source, places, valid = rest[:10]
-    across, inside, fe, fh, acc, neighbor, ports, profile, e, h, j, v_all, w_all, sems = rest[10:]
+    across, inside, fe, fh, _, planes, neighbor, ports, profile, e, h, j, v_all, w_all, sems = (
+        rest[10:]
+    )
     started = []
 
     def fetch(*pairs):
@@ -449,7 +470,9 @@
             drive.append(now + source[i])
         return drive
 
-    up, down = lonely(own_index(places), fe, fh, acc, drive_of, v, lone_h1, lone_e1)
+    up, down = lonely(
+        own_index(places), fe, fh, planes, drive_of, lambda: scale, lone_h1, lone_e1
+    )
     wait(later)
     send(across, inside, 0, up, down)
     send(across, inside, V_NEAR, scale[1][48:NODES], scale[0][0:16])
@@ -473,23 +496,24 @@
 
 
 def second_lone_step(lone_h1, lone_e1, first_j, v, w, source, places, work):
-    fe, fh, acc = work
+    fe, fh, _, planes = work
     index = own_index(places)
     for i in range(2):
         fe[L0 + i] = lone_e1[i]
         fh[L0 + i] = lone_h1[i]
     current = [KEEP * first_j[i] + thrice(w[i]) * lone_e1[i] for i in range(2)]
-    lone_h(index, fe, fh)
-    lone_e(index, fe, fh, acc, [current[i] + source[i] for i in range(2)], v)
+    lone_h(index, fe, fh, planes)
+    lone_e(index, fe, fh, planes, [current[i] + source[i] for i in range(2)], v)
     return current
 
 
 def lone_kernel(lone_h1, lone_e1, first_j, v, w, source, places, design, *rest):
-    lone_h2, lone_e2, lone_j2, pixels, fe, fh, acc = rest
+    lone_h2, lone_e2, lone_j2, pixels, *work = rest
+    fe, fh = work[:2]
     pixel = jnp.bitwise_and(design[...], PIX_DEV - 1)
     pixels[...] = one_hot(lax.broadcasted_iota(jnp.int32, pixels.shape, 0), pixel)
     current = second_lone_step(
-        lone_h1, lone_e1, first_j, v, w, source, places, (fe, fh, acc)
+        lone_h1, lone_e1, first_j, v, w, source, places, work
     )
     for i in range(2):
         lone_h2[i] = fh[L0 + i]
@@ -512,7 +536,7 @@
 ):
     end_e, next_h, next_e, next_j, answer_e, answer_j, near_v, near_places = rest[:8]
     inside, across = rest[8:10]
-    fe, fh, acc, sent_a, sent_b = rest[10:]
+    fe, fh, acc, planes, sent_a, sent_b = rest[10:]
     sides_of(across_in, inside_in, sent_a, sent_b, FIRST)
     for side, sent in enumerate((sent_a, sent_b)):
         near_v[side] = sent[V_NEAR : V_NEAR + 32, :]
@@ -520,14 +544,15 @@
         for face in range(6):
             near_places[6 * side + face] = jnp.broadcast_to(place[face : face + 1], (8, LAYER))
     index = index_of(places, near_places)
-    second_e, current = respond(
-        index, valid, fe, fh, acc, (start_e, lone_h1, lone_e1), v, w, near_v, sent_a, sent_b
+    current = respond(
+        index, valid, fe, fh, acc, planes, (start_e, lone_h1, lone_e1), v, w, near_v,
+        sent_a, sent_b,
     )
     drive = []
     for i in range(2):
         answer_e[i] = fe[L0 + i]
         answer_j[i] = current[i]
-        electric = lone_e2[i] + second_e[i]
+        electric = lone_e2[i] + acc[L0 + i]
         end_e[i] = electric
         fe[L0 + i] = electric
         fh[L0 + i] += lone_h2[i]
@@ -535,7 +560,7 @@
         now = KEEP * before + thrice(w[i]) * electric
         next_j[i] = now
         drive.append(now + source[i])
-    up, down = lonely(index, fe, fh, acc, lambda: drive, v, next_h, next_e)
+    up, down = lonely(index, fe, fh, planes, lambda: drive, lambda: v, next_h, next_e)
     send(across, inside, 0, up, down)
 
 
@@ -543,8 +568,9 @@
     lone_e1, answer_e, lone_j1, lone_j2, answer_j, end_e, next_h, next_e, next_j, v, w,
     source, places, levels, *rest
 ):
-    last_h, last_e, out, changes, fe, fh, acc = rest
-    current = second_lone_step(next_h, next_e, next_j, v, w, source, places, (fe, fh, acc))
+    last_h, last_e, out, changes, *work = rest
+    fe, fh = work[:2]
+    current = second_lone_step(next_h, next_e, next_j, v, w, source, places, work)
     for i in range(2):
         electric = fe[L0 + i]
         last_h[i] = fh[L0 + i]
@@ -568,22 +594,23 @@
     inside_in, across_in, changes, early, pixels, *rest
 ):
     out_e, out_h, sums = rest[:3]
-    fe, fh, acc, sent_a, sent_b = rest[3:]
+    fe, fh, acc, planes, sent_a, sent_b = rest[3:]
     sides_of(across_in, inside_in, sent_a, sent_b, SECOND)
-    second_e, current = respond(
-        index_of(places, near_places), valid, fe, fh, acc, (start_e, lone_h1, lone_e1),
+    current = respond(
+        index_of(places, near_places), valid, fe, fh, acc, planes, (start_e, lone_h1, lone_e1),
         v, w, near_v, sent_a, sent_b,
     )
     parts = []
     for i in range(2):
         columns = slice(i * LAYER, (i + 1) * LAYER)
-        electric = lone_e2[i] + second_e[i]
+        second_e = acc[L0 + i]
+        electric = lone_e2[i] + second_e
         magnetic = TIME_STEP * (lone_h2[i] + fh[L0 + i])
         for c in range(3):
             rows, there = slice(BASE[c], BASE[c] + NODES), slice(c * NODES, (c + 1) * NODES)
             out_e[there, columns] = electric[rows]
             out_h[there, columns] = magnetic[rows]
-        eps = folded(fe[L0 + i] * changes[0, i] + second_e[i] * changes[1, i])
+        eps = folded(fe[L0 + i] * changes[0, i] + second_e * changes[1, i])
         drude = TIME_STEP * folded(current[i] * changes[2, i])
         parts.append(jnp.concatenate([eps, drude], axis=0) + early[:, columns])
     both = jnp.concatenate(parts, axis=1)
@@ -668,7 +695,7 @@
     levels = fwd_e[0]
     field, nodal = f32(2, ROWS, LAYER), f32(2, NODES, LAYER)
     indices = jax.ShapeDtypeStruct((12, 8, LAYER), jnp.int32)
-    work = [pltpu.VMEM((4, ROWS, LAYER), F32)] * 3
+    work = [pltpu.VMEM((4, ROWS, LAYER), F32)] * 3 + [pltpu.VMEM((4, 2 * NODES, LAYER), F32)]
     given = [adj_e[0], adj_h[0], adj_j[0], inv_eps, drude_weight]
     given += [neighbor, port_elems, port_profile[0], design_map.reshape(1, count)]
     received = [pltpu.VMEM((FIRST, LAYER), F32)] * 2

time: 29.2 us -> 29.1 us (level)
  no operation moved by 1% of the time
where the time goes in v12:
time: 29.1 us; the launch traced here: 28.8 us
  blocking collectives  12.5 us (43%)
  waiting for transfers between devices  6.54 us (22%)
  Pallas kernels  5.07 us (17%)
  starting transfers between devices  3.98 us (14%)
  between operations  0.72 us (2%)
    all_to_all x1, blocking collectives, local(): parts = lax.all_to_all(sums, 'exc', split_axis=0, concat_axis=0, tiled=True)  12.5 us
    ppermute x2, waiting for transfers between devices, exchange(): across = lax.ppermute(across, 'space', pairs(1))  6.54 us
    pallas_call x6, Pallas kernels, call(): pl.pallas_call(kernel, out_shape=outs, in_specs=[pl.BlockSpec(memory_spac...  5.07 us
    ppermute x2, starting transfers between devices, exchange(): across = lax.ppermute(across, 'space', pairs(1))  3.84 us
  transfers between devices with their start and end apart: 4, of which 2 were waited for; matrix products, arithmetic and copies ran while one was open for 0% of the time, Pallas kernels for 3%

profile of v12, /device:TPU:2, one launch (start us, length us, event | category | flops | bytes accessed | tf_op | source)
XLA Modules:
  0.0 28.8 jit_solution(18359371812423385386)
XLA Ops:
  0.6 1.7 %shard_map.129 = (s32[1,256]{1,0:T(1,128)S(1)}, f32[2,192,128]{2,1,0:T(8,128)S(1)}, f32[2,192,128]{2,1,0:T(8,128)S(1)}, f32[2,192,128]{2,1,0:T(8,128)S(1)}, f32[...) custom-call(f32[192,256]{1,0:T(8,128)} %bitcast.15, ...), custom_call_target="tpu_custom_call" | custom-call | flops 2171392 | bytes 2171392 | tf_op jit(solution)/shard_map/pallas_call | solution.py:647
  2.3 1.9 %collective-permute-start = (f32[168,128]{1,0:T(8,128)S(1)}, f32[168,128]{1,0:T(8,128)S(1)}, u32[]{:S(2)}, u32[]{:S(2)}) collective-permute-start(f32[168,128]{1,0:T(8,128)S(1)} %get-tuple-element.54), channel_id=1, source_target_pairs={{1,2},{2,1},{5,6},{6,5},{9,10},{10,9},{13,14},{14,13},{17,18},{18,... | collective-permute-start | bytes 258056 | tf_op jit(solution)/shard_map/ppermute | solution.py:675
  4.2 0.1 collective-permute-start.1
  4.3 0.4 %shard_map.130 = (f32[2,192,128]{2,1,0:T(8,128)S(1)}, f32[2,192,128]{2,1,0:T(8,128)S(1)}, f32[2,192,128]{2,1,0:T(8,128)S(1)}, bf16[128,256]{1,0:T(8,128)(2,1)S(1)}) custom-call(f32[2,192,128]{2,1,0:T(8,128)S(1)} %get-tuple-element.42.lone_h1, f32[2,192,128]{2,1,0:T(8,128)S(1)} %get-tuple-element.43.lone_e1, ...), custom_call_target="tpu_custom_call" | custom-call | flops 1688576 | bytes 1688576 | tf_op jit(solution)/shard_map/pallas_call | solution.py:647
  4.7 3.4 %collective-permute-done.across_in = f32[168,128]{1,0:T(8,128)S(1)} collective-permute-done((f32[168,128]{1,0:T(8,128)S(1)}, f32[168,128]{1,0:T(8,128)S(1)}, u32[]{:S(2)}, u32[]{:S(2)}) %collective-permute-start) | collective-permute-done | bytes 86048 | tf_op jit(solution)/shard_map/ppermute | solution.py:675
  8.1 0.0 collective-permute-done.1.inside_in
  8.1 0.0 copy-start
  8.1 0.9 %shard_map.131 = (f32[2,192,128]{2,1,0:T(8,128)S(1)}, f32[2,192,128]{2,1,0:T(8,128)S(1)}, f32[2,192,128]{2,1,0:T(8,128)S(1)}, f32[2,192,128]{2,1,0:T(8,128)S(1)}...) custom-call(f32[2,192,128]{2,1,0:T(8,128)S(1)} %get-tuple-element.41, ...), custom_call_target="tpu_custom_call" | custom-call | flops 3129344 | bytes 3129344 | tf_op jit(solution)/shard_map/pallas_call | solution.py:647
  9.1 0.1 collective-permute-start.2
  9.1 1.9 %collective-permute-start.3 = (f32[128,128]{1,0:T(8,128)S(1)}, f32[128,128]{1,0:T(8,128)S(1)}, u32[]{:S(2)}, u32[]{:S(2)}) collective-permute-start(f32[128,128]{1,0:T(8,128)S(1)} %get-tuple-element.67), channel_id=1, source_target_pairs={{1,2},{2,1},{5,6},{6,5},{9,10},{10,9},{13,14},{14,13},{17,18},{18,... | collective-permute-start | bytes 196616 | tf_op jit(solution)/shard_map/ppermute | solution.py:675
  11.1 0.0 copy-done
  11.1 0.5 %shard_map.132 = (f32[2,192,128]{2,1,0:T(8,128)S(1)}, f32[2,192,128]{2,1,0:T(8,128)S(1)}, f32[128,256]{1,0:T(8,128)S(1)}, f32[3,2,192,128]{3,2,1,0:T(8,128)S(1)}) custom-call(f32[2,192,128]{2,1,0:T(8,128)S(1)} %get-tuple-element.43.lone_e1, f32[2,192,128]{2,1,0:T(8,128)S(1)} %get-tuple-element.59.answer_e, ...), custom_call_target="tpu_custom_call" | custom-call | flops 3751936 | bytes 3751936 | tf_op jit(solution)/shard_map/pallas_call | solution.py:647
  11.6 0.0 collective-permute-done.2.inside_in
  11.6 3.1 %collective-permute-done.3.across_in = f32[128,128]{1,0:T(8,128)S(1)} collective-permute-done((f32[128,128]{1,0:T(8,128)S(1)}, f32[128,128]{1,0:T(8,128)S(1)}, u32[]{:S(2)}, u32[]{:S(2)}) %collective-permute-start.3) | collective-permute-done | bytes 65568 | tf_op jit(solution)/shard_map/ppermute | solution.py:675
  14.7 0.8 %shard_map.133 = (f32[192,256]{1,0:T(8,128)S(1)}, f32[192,256]{1,0:T(8,128)S(1)}, f32[128,128]{1,0:T(8,128)S(1)}) custom-call(f32[2,192,128]{2,1,0:T(8,128)S(1)} %get-tuple-element.56.end_e.start_e, f32[2,192,128]{2,1,0:T(8,128)S(1)} %get-tuple-element.57.next_h.lone_h1, f32[2,192,128]{2,1,0:T(8,128)S(1)} %get-tuple-element.58.next_e.lone_e1, ...), custom_call_target="tpu_custom_call" | custom-call | flops 2629632 | bytes 2629632 | tf_op jit(solution)/shard_map/pallas_call | solution.py:647
  15.5 12.5 %all_to_all.11 = f32[8,16,128]{2,1,0:T(8,128)S(1)} all-to-all(f32[8,16,128]{2,1,0:T(8,128)S(1)} %bitcast.14), channel_id=1, replica_groups=mesh['exc'=8,'space'=4] {'exc'}, dimensions={0} | all-to-all | bytes 131072 | tf_op jit(solution)/shard_map/all_to_all | solution.py:743
  28.1 0.8 %shard_map.134 = (f32[192,256]{1,0:T(8,128)}, f32[192,256]{1,0:T(8,128)}, f32[16,64]{1,0:T(8,128)}, f32[16,64]{1,0:T(8,128)}) custom-call(f32[128,128]{1,0:T(8,128)S(1)} %bitcast.13, f32[192,256]{1,0:T(8,128)S(1)} %get-tuple-element.72.e, f32[192,256]{1,0:T(8,128)S(1)} %get-tuple-element.73.h), custom_call_target="tpu_custom_call" | custom-call | flops 860160 | bytes 860160 | tf_op jit(solution)/shard_map/pallas_call | solution.py:647
Async XLA Ops:
  2.3 5.8 %collective-permute-start = (f32[168,128]{1,0:T(8,128)S(1)}, f32[168,128]{1,0:T(8,128)S(1)}, u32[]{:S(2)}, u32[]{:S(2)}) collective-permute-start(f32[168,128]{1,0:T(8,128)S(1)} %get-tuple-element.54), channel_id=1, source_target_pairs={{1,2},{2,1},{5,6},{6,5},{9,10},{10,9},{13,14},{14,13},{17,18},{18,... | collective-permute-start | bytes 258056 | tf_op jit(solution)/shard_map/ppermute | solution.py:675
  4.2 3.9 %collective-permute-start.1 = (f32[168,128]{1,0:T(8,128)S(1)}, f32[168,128]{1,0:T(8,128)S(1)}, u32[]{:S(2)}, u32[]{:S(2)}) collective-permute-start(f32[168,128]{1,0:T(8,128)S(1)} %get-tuple-element.55), channel_id=1, source_target_pairs={{0,1},{2,3},{1,0},{3,2},{4,5},{6,7},{5,4},{7,6},{8,9},{10,11},{9,8... | collective-permute-start | bytes 258056 | tf_op jit(solution)/shard_map/ppermute | solution.py:677
  8.1 2.9 %copy-start = (bf16[1,5,192,256]{3,2,1,0:T(8,128)(2,1)S(1)}, bf16[1,5,192,256]{3,2,1,0:T(8,128)(2,1)}, u32[]{:S(2)}) copy-start(bf16[1,5,192,256]{3,2,1,0:T(8,128)(2,1)} %param.13) | copy-start | bytes 1474564
  9.1 2.5 %collective-permute-start.2 = (f32[128,128]{1,0:T(8,128)S(1)}, f32[128,128]{1,0:T(8,128)S(1)}, u32[]{:S(2)}, u32[]{:S(2)}) collective-permute-start(f32[128,128]{1,0:T(8,128)S(1)} %get-tuple-element.66), channel_id=1, source_target_pairs={{0,1},{2,3},{1,0},{3,2},{4,5},{6,7},{5,4},{7,6},{8,9},{10,11},{9,8... | collective-permute-start | bytes 196616 | tf_op jit(solution)/shard_map/ppermute | solution.py:674
  9.1 5.6 %collective-permute-start.3 = (f32[128,128]{1,0:T(8,128)S(1)}, f32[128,128]{1,0:T(8,128)S(1)}, u32[]{:S(2)}, u32[]{:S(2)}) collective-permute-start(f32[128,128]{1,0:T(8,128)S(1)} %get-tuple-element.67), channel_id=1, source_target_pairs={{1,2},{2,1},{5,6},{6,5},{9,10},{10,9},{13,14},{14,13},{17,18},{18,... | collective-permute-start | bytes 196616 | tf_op jit(solution)/shard_map/ppermute | solution.py:675

commit v13 on v12

--- a/solution.py
+++ b/solution.py
@@ -301,8 +301,8 @@
         traces = [sent[side][start + 16 * t : start + 16 * t + 16, :] for t in range(2)]
         if answers is not None:
             traces = [a + b for a, b in zip(traces, answers)]
-        mask = jnp.concatenate([valid[side]] * 2, axis=0)
-        return [picked(t, index(layer, face)) * mask for t in traces]
+        there = jnp.concatenate([valid[side]] * 2, axis=0) > 0.0
+        return [jnp.where(there, picked(t, index(layer, face)), 0.0) for t in traces]
 
     def inward(side, start, scale, answers=None):
         return lifted(sides[side][3], scale, *arrived(side, start, answers))
@@ -541,6 +541,7 @@
     for side, sent in enumerate((sent_a, sent_b)):
         near_v[side] = sent[V_NEAR : V_NEAR + 32, :]
         place = sent[N_NEAR : N_NEAR + 8, :].astype(jnp.int32)
+        place = jnp.bitwise_and(place, LAYER - 1)
         for face in range(6):
             near_places[6 * side + face] = jnp.broadcast_to(place[face : face + 1], (8, LAYER))
     index = index_of(places, near_places)

time: 29.1 us -> 29.1 us (level)
  no operation moved by 1% of the time
where the time goes in v13:
time: 29.1 us; the launch traced here: 28.8 us
  blocking collectives  12.5 us (43%)
  waiting for transfers between devices  6.54 us (22%)
  Pallas kernels  5.05 us (17%)
  starting transfers between devices  3.98 us (14%)
  between operations  0.72 us (2%)
    all_to_all x1, blocking collectives, local(): parts = lax.all_to_all(sums, 'exc', split_axis=0, concat_axis=0, tiled=True)  12.5 us
    ppermute x2, waiting for transfers between devices, exchange(): across = lax.ppermute(across, 'space', pairs(1))  6.54 us
    pallas_call x6, Pallas kernels, call(): pl.pallas_call(kernel, out_shape=outs, in_specs=[pl.BlockSpec(memory_spac...  5.05 us
    ppermute x2, starting transfers between devices, exchange(): across = lax.ppermute(across, 'space', pairs(1))  3.84 us
  transfers between devices with their start and end apart: 4, of which 2 were waited for; matrix products, arithmetic and copies ran while one was open for 0% of the time, Pallas kernels for 3%

profile of v13, /device:TPU:2, one launch (start us, length us, event | category | flops | bytes accessed | tf_op | source)
XLA Modules:
  0.0 28.8 jit_solution(12159736313754642548)
XLA Ops:
  0.6 1.7 %shard_map.129 = (s32[1,256]{1,0:T(1,128)S(1)}, f32[2,192,128]{2,1,0:T(8,128)S(1)}, f32[2,192,128]{2,1,0:T(8,128)S(1)}, f32[2,192,128]{2,1,0:T(8,128)S(1)}, f32[...) custom-call(f32[192,256]{1,0:T(8,128)} %bitcast.15, ...), custom_call_target="tpu_custom_call" | custom-call | flops 2171392 | bytes 2171392 | tf_op jit(solution)/shard_map/pallas_call | solution.py:648
  2.3 1.9 %collective-permute-start = (f32[168,128]{1,0:T(8,128)S(1)}, f32[168,128]{1,0:T(8,128)S(1)}, u32[]{:S(2)}, u32[]{:S(2)}) collective-permute-start(f32[168,128]{1,0:T(8,128)S(1)} %get-tuple-element.54), channel_id=1, source_target_pairs={{1,2},{2,1},{5,6},{6,5},{9,10},{10,9},{13,14},{14,13},{17,18},{18,... | collective-permute-start | bytes 258056 | tf_op jit(solution)/shard_map/ppermute | solution.py:676
  4.2 0.1 collective-permute-start.1
  4.3 0.4 %shard_map.130 = (f32[2,192,128]{2,1,0:T(8,128)S(1)}, f32[2,192,128]{2,1,0:T(8,128)S(1)}, f32[2,192,128]{2,1,0:T(8,128)S(1)}, bf16[128,256]{1,0:T(8,128)(2,1)S(1)}) custom-call(f32[2,192,128]{2,1,0:T(8,128)S(1)} %get-tuple-element.42.lone_h1, f32[2,192,128]{2,1,0:T(8,128)S(1)} %get-tuple-element.43.lone_e1, ...), custom_call_target="tpu_custom_call" | custom-call | flops 1688576 | bytes 1688576 | tf_op jit(solution)/shard_map/pallas_call | solution.py:648
  4.7 3.4 %collective-permute-done.across_in = f32[168,128]{1,0:T(8,128)S(1)} collective-permute-done((f32[168,128]{1,0:T(8,128)S(1)}, f32[168,128]{1,0:T(8,128)S(1)}, u32[]{:S(2)}, u32[]{:S(2)}) %collective-permute-start) | collective-permute-done | bytes 86048 | tf_op jit(solution)/shard_map/ppermute | solution.py:676
  8.1 0.0 collective-permute-done.1.inside_in
  8.1 0.0 copy-start
  8.1 0.9 %shard_map.131 = (f32[2,192,128]{2,1,0:T(8,128)S(1)}, f32[2,192,128]{2,1,0:T(8,128)S(1)}, f32[2,192,128]{2,1,0:T(8,128)S(1)}, f32[2,192,128]{2,1,0:T(8,128)S(1)}...) custom-call(f32[2,192,128]{2,1,0:T(8,128)S(1)} %get-tuple-element.41, ...), custom_call_target="tpu_custom_call" | custom-call | flops 3129344 | bytes 3129344 | tf_op jit(solution)/shard_map/pallas_call | solution.py:648
  9.0 0.1 collective-permute-start.2
  9.1 1.9 %collective-permute-start.3 = (f32[128,128]{1,0:T(8,128)S(1)}, f32[128,128]{1,0:T(8,128)S(1)}, u32[]{:S(2)}, u32[]{:S(2)}) collective-permute-start(f32[128,128]{1,0:T(8,128)S(1)} %get-tuple-element.67), channel_id=1, source_target_pairs={{1,2},{2,1},{5,6},{6,5},{9,10},{10,9},{13,14},{14,13},{17,18},{18,... | collective-permute-start | bytes 196616 | tf_op jit(solution)/shard_map/ppermute | solution.py:676
  11.0 0.0 copy-done
  11.1 0.5 %shard_map.132 = (f32[2,192,128]{2,1,0:T(8,128)S(1)}, f32[2,192,128]{2,1,0:T(8,128)S(1)}, f32[128,256]{1,0:T(8,128)S(1)}, f32[3,2,192,128]{3,2,1,0:T(8,128)S(1)}) custom-call(f32[2,192,128]{2,1,0:T(8,128)S(1)} %get-tuple-element.43.lone_e1, f32[2,192,128]{2,1,0:T(8,128)S(1)} %get-tuple-element.59.answer_e, ...), custom_call_target="tpu_custom_call" | custom-call | flops 3751936 | bytes 3751936 | tf_op jit(solution)/shard_map/pallas_call | solution.py:648
  11.6 0.0 collective-permute-done.2.inside_in
  11.6 3.1 %collective-permute-done.3.across_in = f32[128,128]{1,0:T(8,128)S(1)} collective-permute-done((f32[128,128]{1,0:T(8,128)S(1)}, f32[128,128]{1,0:T(8,128)S(1)}, u32[]{:S(2)}, u32[]{:S(2)}) %collective-permute-start.3) | collective-permute-done | bytes 65568 | tf_op jit(solution)/shard_map/ppermute | solution.py:676
  14.7 0.8 %shard_map.133 = (f32[192,256]{1,0:T(8,128)S(1)}, f32[192,256]{1,0:T(8,128)S(1)}, f32[128,128]{1,0:T(8,128)S(1)}) custom-call(f32[2,192,128]{2,1,0:T(8,128)S(1)} %get-tuple-element.56.end_e.start_e, f32[2,192,128]{2,1,0:T(8,128)S(1)} %get-tuple-element.57.next_h.lone_h1, f32[2,192,128]{2,1,0:T(8,128)S(1)} %get-tuple-element.58.next_e.lone_e1, ...), custom_call_target="tpu_custom_call" | custom-call | flops 2629632 | bytes 2629632 | tf_op jit(solution)/shard_map/pallas_call | solution.py:648
  15.5 12.5 %all_to_all.11 = f32[8,16,128]{2,1,0:T(8,128)S(1)} all-to-all(f32[8,16,128]{2,1,0:T(8,128)S(1)} %bitcast.14), channel_id=1, replica_groups=mesh['exc'=8,'space'=4] {'exc'}, dimensions={0} | all-to-all | bytes 131072 | tf_op jit(solution)/shard_map/all_to_all | solution.py:744
  28.1 0.8 %shard_map.134 = (f32[192,256]{1,0:T(8,128)}, f32[192,256]{1,0:T(8,128)}, f32[16,64]{1,0:T(8,128)}, f32[16,64]{1,0:T(8,128)}) custom-call(f32[128,128]{1,0:T(8,128)S(1)} %bitcast.13, f32[192,256]{1,0:T(8,128)S(1)} %get-tuple-element.72.e, f32[192,256]{1,0:T(8,128)S(1)} %get-tuple-element.73.h), custom_call_target="tpu_custom_call" | custom-call | flops 860160 | bytes 860160 | tf_op jit(solution)/shard_map/pallas_call | solution.py:648
Async XLA Ops:
  2.3 5.8 %collective-permute-start = (f32[168,128]{1,0:T(8,128)S(1)}, f32[168,128]{1,0:T(8,128)S(1)}, u32[]{:S(2)}, u32[]{:S(2)}) collective-permute-start(f32[168,128]{1,0:T(8,128)S(1)} %get-tuple-element.54), channel_id=1, source_target_pairs={{1,2},{2,1},{5,6},{6,5},{9,10},{10,9},{13,14},{14,13},{17,18},{18,... | collective-permute-start | bytes 258056 | tf_op jit(solution)/shard_map/ppermute | solution.py:676
  4.2 3.9 %collective-permute-start.1 = (f32[168,128]{1,0:T(8,128)S(1)}, f32[168,128]{1,0:T(8,128)S(1)}, u32[]{:S(2)}, u32[]{:S(2)}) collective-permute-start(f32[168,128]{1,0:T(8,128)S(1)} %get-tuple-element.55), channel_id=1, source_target_pairs={{0,1},{2,3},{1,0},{3,2},{4,5},{6,7},{5,4},{7,6},{8,9},{10,11},{9,8... | collective-permute-start | bytes 258056 | tf_op jit(solution)/shard_map/ppermute | solution.py:678
  8.1 2.9 %copy-start = (bf16[1,5,192,256]{3,2,1,0:T(8,128)(2,1)S(1)}, bf16[1,5,192,256]{3,2,1,0:T(8,128)(2,1)}, u32[]{:S(2)}) copy-start(bf16[1,5,192,256]{3,2,1,0:T(8,128)(2,1)} %param.13) | copy-start | bytes 1474564
  9.0 2.5 %collective-permute-start.2 = (f32[128,128]{1,0:T(8,128)S(1)}, f32[128,128]{1,0:T(8,128)S(1)}, u32[]{:S(2)}, u32[]{:S(2)}) collective-permute-start(f32[128,128]{1,0:T(8,128)S(1)} %get-tuple-element.66), channel_id=1, source_target_pairs={{0,1},{2,3},{1,0},{3,2},{4,5},{6,7},{5,4},{7,6},{8,9},{10,11},{9,8... | collective-permute-start | bytes 196616 | tf_op jit(solution)/shard_map/ppermute | solution.py:675
  9.1 5.6 %collective-permute-start.3 = (f32[128,128]{1,0:T(8,128)S(1)}, f32[128,128]{1,0:T(8,128)S(1)}, u32[]{:S(2)}, u32[]{:S(2)}) collective-permute-start(f32[128,128]{1,0:T(8,128)S(1)} %get-tuple-element.67), channel_id=1, source_target_pairs={{1,2},{2,1},{5,6},{6,5},{9,10},{10,9},{13,14},{14,13},{17,18},{18,... | collective-permute-start | bytes 196616 | tf_op jit(solution)/shard_map/ppermute | solution.py:676
